TPU v7x, 32 devices: a whole 2x2x4 slice. The times are simulated.
32 devices in a mesh: dp: 8 (over z, x), seq: 2 (over core), mp: 2 (over y).
Axes of the slice: x: 2, y: 2, z: 4, core: 2. Of those that a mesh axis runs over, the one named last changes fastest.
Arguments:
- mel_input: bfloat16 [8, 80, 4096], P('dp', None, 'seq'), may hold values from -6 to 6
- conv1_weight: bfloat16 [3, 80, 512], replicated, may hold values from -0.375 to 0.375
- conv1_bias: bfloat16 [512], replicated, may hold values from -2 to 2
- conv2_weight: bfloat16 [3, 512, 512], replicated, may hold values from -0.15625 to 0.15625
- conv2_bias: bfloat16 [512], replicated, may hold values from -2 to 2
- norm1_gain: bfloat16 [512], replicated, may hold values from 0.099609375 to 1.8984375
- norm1_bias: bfloat16 [512], replicated, may hold values from -2 to 2
- qkv_weight: bfloat16 [3, 512, 512], P(None, None, 'mp'), may hold values from -0.375 to 0.375
- qkv_bias: bfloat16 [2, 512], P(None, 'mp'), may hold values from -2 to 2
- out_weight: bfloat16 [512, 512], P('mp'), may hold values from -1 to 1
- out_bias: bfloat16 [512], replicated, may hold values from -2 to 2
- norm2_gain: bfloat16 [512], replicated, may hold values from 0.099609375 to 1.8984375
- norm2_bias: bfloat16 [512], replicated, may hold values from -2 to 2
- up_weight: bfloat16 [512, 2048], P(None, 'mp'), may hold values from -0.25 to 0.25
- up_bias: bfloat16 [2048], P('mp'), may hold values from -2.5 to 2.5
- down_weight: bfloat16 [2048, 512], P('mp'), may hold values from -0.25 to 0.25
- down_bias: bfloat16 [512], replicated, may hold values from -2 to 2
- cotangent: bfloat16 [8, 2048, 512], P('dp', 'seq'), may hold values from -6 to 6
- speech_mask: int32 [8, 2048], P('dp', 'seq'), may hold values 0 or 1
Outputs:
- encoded: bfloat16 [8, 2048, 512], P('dp', 'seq')
- mel_grad: float32 [8, 80, 4096], P('dp', None, 'seq')
- conv1_weight_grad: float32 [3, 80, 512], replicated
- conv1_bias_grad: float32 [512], replicated
- conv2_weight_grad: float32 [3, 512, 512], replicated
- conv2_bias_grad: float32 [512], replicated
- norm1_gain_grad: float32 [512], replicated
- norm1_bias_grad: float32 [512], replicated
- qkv_weight_grad: float32 [3, 512, 512], P(None, None, 'mp')
- qkv_bias_grad: float32 [2, 512], P(None, 'mp')
- out_weight_grad: float32 [512, 512], P('mp')
- out_bias_grad: float32 [512], replicated
- norm2_gain_grad: float32 [512], replicated
- norm2_bias_grad: float32 [512], replicated
- up_weight_grad: float32 [512, 2048], P(None, 'mp')
- up_bias_grad: float32 [2048], P('mp')
- down_weight_grad: float32 [2048, 512], P('mp')
- down_bias_grad: float32 [512], replicated
Inputs may be any that keep to these rules, and one draw needn't show every extreme that they name: `speech_mask`: 1 keeps the gradient of a frame, 0 marks a non-speech frame.
All inputs are finite; a program needn't handle non-finite values. No bound on the sum of `speech_mask` on one device may be relied on, other than what follows from the above.
Results may differ from a plain program's by a relative error of at most 0.02.
The roundings to bfloat16 on the way count: a program that leaves them out, or rounds other values in their place, can miss the bound.
Values may be sent and summed in bfloat16 or wider, within the bound.
A program may use at most 256 MiB of HBM per device.

v0:
```python
import math

import jax
import jax.numpy as jnp
from jax import lax
from jax.sharding import PartitionSpec as P

HEAD = 64


def padded_2(block, sides, width):
    for axis, dim in sides:
        count = lax.axis_size(axis)
        forward = [(i, i + 1) for i in range(count - 1)]
        backward = [(target, source) for source, target in forward]
        low = lax.ppermute(
            lax.slice_in_dim(block, block.shape[dim] - width, None, axis=dim), axis, forward
        )
        high = lax.ppermute(lax.slice_in_dim(block, 0, width, axis=dim), axis, backward)
        block = jnp.concatenate([low, block, high], axis=dim)
    return block


def passed_along(value, axis, by):
    count = lax.axis_size(axis)
    pairs = [(i, i + by) for i in range(count) if 0 <= i + by < count]
    return lax.ppermute(value, axis, pairs)


def gelu_exact(values):
    return jax.nn.gelu(values, approximate=False)


def layer_norm(values, scale_row, shift_row):
    center = values - jnp.mean(values, axis=-1, keepdims=True)
    spread = jnp.mean(center * center, axis=-1, keepdims=True)
    return center * lax.rsqrt(spread + 1e-05) * scale_row + shift_row


def sinusoids(positions, channels):
    half_width = channels // 2
    increment = math.log(10000.0) / (half_width - 1)
    inverse = jnp.exp(-increment * jnp.arange(half_width, dtype=jnp.float32))
    angles = positions.astype(jnp.float32)[:, None] * inverse[None, :]
    return jnp.concatenate([jnp.sin(angles), jnp.cos(angles)], axis=1)


def product(left_side, right_side):
    return jnp.dot(left_side, right_side, preferred_element_type=jnp.float32)


def cross(left_side, right_side):
    return lax.dot_general(
        left_side, right_side, (((0,), (0,)), ((), ())), preferred_element_type=jnp.float32
    )


def against(left_side, right_side):
    return lax.dot_general(
        left_side, right_side, (((1,), (1,)), ((), ())), preferred_element_type=jnp.float32
    )


def column_sum(values):
    return jnp.sum(values.astype(jnp.float32), axis=0)


def gelu_pull(pre_values, grad_values):
    return jax.vjp(gelu_exact, pre_values)[1](grad_values)[0]


def on_device(
    mel_input,
    conv1_weight,
    conv1_bias,
    conv2_weight,
    conv2_bias,
    norm1_gain,
    norm1_bias,
    qkv_weight,
    qkv_bias,
    out_weight,
    out_bias,
    norm2_gain,
    norm2_bias,
    up_weight,
    up_bias,
    down_weight,
    down_bias,
    cotangent,
    speech_mask,
):
    spectrum = mel_input[0]
    frames = cotangent.shape[1]
    local_width = qkv_weight.shape[2]
    local_heads = local_width // HEAD
    scaling = HEAD ** (-0.5)
    gain_first = norm1_gain.astype(jnp.float32)
    shift_first = norm1_bias.astype(jnp.float32)
    gain_second = norm2_gain.astype(jnp.float32)
    shift_second = norm2_bias.astype(jnp.float32)
    padded = padded_2(spectrum, (("seq", 1),), 1)
    first_pre = conv1_bias.astype(jnp.float32)
    for offset in range(3):
        first_pre = first_pre + jnp.einsum(
            "ct,cd->td",
            padded[:, offset : offset + 2 * frames],
            conv1_weight[offset],
            preferred_element_type=jnp.float32,
        )
    hidden = gelu_exact(first_pre).astype(jnp.bfloat16)
    edge_row = passed_along(hidden[-1:], "seq", 1)
    shifted = jnp.concatenate([edge_row, hidden], axis=0)
    stride_taps = [shifted[offset : offset + 2 * frames : 2] for offset in range(3)]
    second_pre = conv2_bias.astype(jnp.float32)
    for offset in range(3):
        second_pre = second_pre + product(stride_taps[offset], conv2_weight[offset])
    positions = lax.axis_index("seq") * frames + jnp.arange(frames, dtype=jnp.int32)
    stream = gelu_exact(second_pre) + sinusoids(positions, second_pre.shape[1])
    normed = layer_norm(stream, gain_first, shift_first).astype(jnp.bfloat16)
    queries = (product(normed, qkv_weight[0]) + qkv_bias[0].astype(jnp.float32)).astype(
        jnp.bfloat16
    )
    key_rows = product(normed, qkv_weight[1]).astype(jnp.bfloat16)
    value_rows = (product(normed, qkv_weight[2]) + qkv_bias[1].astype(jnp.float32)).astype(
        jnp.bfloat16
    )
    key_all, value_all = (
        lax.all_gather(key_rows, "seq", axis=0, tiled=True),
        lax.all_gather(value_rows, "seq", axis=0, tiled=True),
    )
    query_heads = queries.reshape(frames, local_heads, HEAD)
    key_heads = key_all.reshape(-1, local_heads, HEAD)
    value_heads = value_all.reshape(-1, local_heads, HEAD)
    scores = (
        jnp.einsum("qhe,khe->hqk", query_heads, key_heads, preferred_element_type=jnp.float32)
        * scaling
    )
    row_max = jnp.max(scores, axis=-1, keepdims=True)
    expanded = jnp.exp(scores - row_max)
    row_total = jnp.sum(expanded, axis=-1, keepdims=True)
    probs = expanded / row_total
    log_total = row_max + jnp.log(row_total)
    mixture = (
        jnp.einsum(
            "hqk,khe->qhe",
            probs.astype(jnp.bfloat16),
            value_heads,
            preferred_element_type=jnp.float32,
        )
        .reshape(frames, local_width)
        .astype(jnp.bfloat16)
    )
    attended = lax.psum(product(mixture, out_weight).astype(jnp.bfloat16), "mp").astype(
        jnp.float32
    ) + out_bias.astype(jnp.float32)
    stream_mid = stream + attended
    normed_two = layer_norm(stream_mid, gain_second, shift_second).astype(jnp.bfloat16)
    inner_pre = product(normed_two, up_weight) + up_bias.astype(jnp.float32)
    active = gelu_exact(inner_pre).astype(jnp.bfloat16)
    branch_out = lax.psum(product(active, down_weight).astype(jnp.bfloat16), "mp").astype(
        jnp.float32
    ) + down_bias.astype(jnp.float32)
    encoded = (stream_mid + branch_out).astype(jnp.bfloat16)[None]
    upstream = cotangent[0].astype(jnp.float32) * speech_mask[0].astype(jnp.float32)[:, None]
    branch_grad = upstream.astype(jnp.bfloat16)
    grad_down_bias = column_sum(branch_grad)
    grad_down = cross(active, branch_grad)
    inner_grad = gelu_pull(inner_pre, against(branch_grad, down_weight)).astype(jnp.bfloat16)
    grad_up = cross(normed_two, inner_grad)
    grad_up_bias = column_sum(inner_grad)
    normed_two_grad = lax.psum(against(inner_grad, up_weight).astype(jnp.bfloat16), "mp").astype(
        jnp.float32
    )
    second_pull = jax.vjp(layer_norm, stream_mid, gain_second, shift_second)[1]
    mid_part, grad_norm2_gain, grad_norm2_bias = second_pull(normed_two_grad)
    stream_mid_grad = upstream + mid_part
    attended_grad = stream_mid_grad.astype(jnp.bfloat16)
    grad_out_bias = column_sum(attended_grad)
    grad_out = cross(mixture, attended_grad)
    mixture_grad = (
        against(attended_grad, out_weight).astype(jnp.bfloat16).reshape(frames, local_heads, HEAD)
    )
    scores_again = (
        jnp.einsum("qhe,khe->hqk", query_heads, key_heads, preferred_element_type=jnp.float32)
        * scaling
    )
    probs_again = jnp.exp(scores_again - log_total)
    prob_grad = jnp.einsum(
        "qhe,khe->hqk", mixture_grad, value_heads, preferred_element_type=jnp.float32
    )
    diagonal_term = jnp.sum(probs_again * prob_grad, axis=-1, keepdims=True)
    score_grad = (probs_again * (prob_grad - diagonal_term)).astype(jnp.bfloat16)
    query_grad = (
        (
            jnp.einsum("hqk,khe->qhe", score_grad, key_heads, preferred_element_type=jnp.float32)
            * scaling
        )
        .reshape(frames, local_width)
        .astype(jnp.bfloat16)
    )
    key_part = (
        jnp.einsum("hqk,qhe->khe", score_grad, query_heads, preferred_element_type=jnp.float32)
        * scaling
    ).reshape(-1, local_width)
    value_part = jnp.einsum(
        "hqk,qhe->khe",
        probs_again.astype(jnp.bfloat16),
        mixture_grad,
        preferred_element_type=jnp.float32,
    ).reshape(-1, local_width)
    key_sum, value_sum = (
        lax.psum_scatter(
            key_part.astype(jnp.bfloat16), "seq", scatter_dimension=0, tiled=True
        ).astype(jnp.float32),
        lax.psum_scatter(
            value_part.astype(jnp.bfloat16), "seq", scatter_dimension=0, tiled=True
        ).astype(jnp.float32),
    )
    key_grad = key_sum.astype(jnp.bfloat16)
    value_grad = value_sum.astype(jnp.bfloat16)
    grad_qkv = jnp.stack(
        [cross(normed, query_grad), cross(normed, key_grad), cross(normed, value_grad)]
    )
    grad_qkv_bias = jnp.stack([column_sum(query_grad), column_sum(value_grad)])
    normed_part = (
        against(query_grad, qkv_weight[0])
        + against(key_grad, qkv_weight[1])
        + against(value_grad, qkv_weight[2])
    )
    normed_grad = lax.psum(normed_part.astype(jnp.bfloat16), "mp").astype(jnp.float32)
    first_pull = jax.vjp(layer_norm, stream, gain_first, shift_first)[1]
    stream_part, grad_norm1_gain, grad_norm1_bias = first_pull(normed_grad)
    stream_grad = stream_mid_grad + stream_part
    second_grad = gelu_pull(second_pre, stream_grad).astype(jnp.bfloat16)
    grad_conv2_bias = column_sum(second_grad)
    grad_conv2 = jnp.stack([cross(stride_taps[offset], second_grad) for offset in range(3)])
    tap_grads = [against(second_grad, conv2_weight[offset]) for offset in range(3)]
    even_rows = jnp.pad(tap_grads[0], ((0, 1), (0, 0))) + jnp.pad(tap_grads[2], ((1, 0), (0, 0)))
    woven = jnp.stack([even_rows[:frames], tap_grads[1]], axis=1).reshape(2 * frames, -1)
    edge_piece = woven[:1]
    hidden_grad = jnp.concatenate([woven[1:], even_rows[frames:]], axis=0)
    returned = passed_along(edge_piece, "seq", -1)
    hidden_grad = jnp.concatenate([hidden_grad[:-1], hidden_grad[-1:] + returned], axis=0)
    first_grad = gelu_pull(first_pre, hidden_grad).astype(jnp.bfloat16)
    grad_conv1_bias = column_sum(first_grad)
    grad_conv1 = jnp.stack(
        [
            jnp.einsum(
                "ct,td->cd",
                padded[:, offset : offset + 2 * frames],
                first_grad,
                preferred_element_type=jnp.float32,
            )
            for offset in range(3)
        ]
    )
    padded_grad = jnp.zeros((spectrum.shape[0], 2 * frames + 2), jnp.float32)
    for offset in range(3):
        padded_grad = padded_grad + jnp.pad(
            jnp.einsum(
                "td,cd->ct", first_grad, conv1_weight[offset], preferred_element_type=jnp.float32
            ),
            ((0, 0), (offset, 2 - offset)),
        )
    rim_pair = jnp.concatenate([padded_grad[:, :1], padded_grad[:, -1:]], axis=1)
    rim_back = padded_2(rim_pair, (("seq", 1),), 1)
    inner_cols = padded_grad[:, 1:-1]
    mel_grad = jnp.concatenate(
        [
            inner_cols[:, :1] + rim_back[:, :1],
            inner_cols[:, 1:-1],
            inner_cols[:, -1:] + rim_back[:, 3:],
        ],
        axis=1,
    )[None]
    (
        grad_conv1,
        grad_conv1_bias,
        grad_conv2,
        grad_conv2_bias,
        grad_norm1_gain,
        grad_norm1_bias,
        grad_qkv,
        grad_qkv_bias,
        grad_out,
        grad_out_bias,
        grad_norm2_gain,
        grad_norm2_bias,
        grad_up,
        grad_up_bias,
        grad_down,
        grad_down_bias,
    ) = lax.psum(
        (
            grad_conv1,
            grad_conv1_bias,
            grad_conv2,
            grad_conv2_bias,
            grad_norm1_gain,
            grad_norm1_bias,
            grad_qkv,
            grad_qkv_bias,
            grad_out,
            grad_out_bias,
            grad_norm2_gain,
            grad_norm2_bias,
            grad_up,
            grad_up_bias,
            grad_down,
            grad_down_bias,
        ),
        ("dp", "seq"),
    )
    return (
        encoded,
        mel_grad,
        grad_conv1,
        grad_conv1_bias,
        grad_conv2,
        grad_conv2_bias,
        grad_norm1_gain,
        grad_norm1_bias,
        grad_qkv,
        grad_qkv_bias,
        grad_out,
        grad_out_bias,
        grad_norm2_gain,
        grad_norm2_bias,
        grad_up,
        grad_up_bias,
        grad_down,
        grad_down_bias,
    )


def solution(mesh):
    placed = (
        P("dp", None, "seq"),
        P(),
        P(),
        P(),
        P(),
        P(),
        P(),
        P(None, None, "mp"),
        P(None, "mp"),
        P("mp", None),
        P(),
        P(),
        P(),
        P(None, "mp"),
        P("mp"),
        P("mp", None),
        P(),
        P("dp", "seq", None),
        P("dp", "seq"),
    )
    return jax.shard_map(
        on_device,
        mesh=mesh,
        in_specs=placed,
        out_specs=(
            P("dp", "seq", None),
            P("dp", None, "seq"),
            P(),
            P(),
            P(),
            P(),
            P(),
            P(),
            P(None, None, "mp"),
            P(None, "mp"),
            P("mp", None),
            P(),
            P(),
            P(),
            P(None, "mp"),
            P("mp"),
            P("mp", None),
            P(),
        ),
        check_vma=False,
    )
```

profile of v0, /device:TPU:0, one launch (start us, length us, event | category | flops | bytes accessed | tf_op | source)
XLA Modules:
  0.0 693.9 jit_solution(2775971534682668972)
XLA Ops:
  11.9 3.7 fusion.83
  15.6 4.8 multiply_sine_fusion
  22.7 11.8 %multiply_convert_fusion.2 = (bf16[2048,512]{1,0:T(8,128)(2,1)S(1)}, f32[2048,512]{1,0:T(8,128)}, f32[2048,512]{1,0:T(8,128)}) fusion(bf16[3,80,512]{2,1,0:T(8,128)(2,1)S(1)} %copy-done.46, bf16[80,1]{1,0:T(8,128)(2,1)S(1)} %collective-permute-done.1, bf16[80,2048]{1,0:T(8,128)(2,1)S(1)} %bitcast.182, f32[2048,512]{1,0:T(8,128)S(1)} %copy-done.34, ...), kind=kOutput, calls=%fused_computation.33 | convolution fusion | flops 239730688 | bytes 19306496 | tf_op jit(solution)/shard_map/ct,cd->td/dot_general | solution.py:105
  35.8 11.0 %slice.113 = bf16[1024,512]{1,0:T(8,128)(2,1)} slice(bf16[2048,512]{1,0:T(8,128)(2,1)} %copy-done.23), slice={[1:2048:2], [0:512:1]} | slice | bytes 2097152 | tf_op jit(solution)/shard_map/slice | solution.py:114
  46.8 6.8 slice.111
  56.7 3.4 fusion.50
  65.1 10.9 %slice.109 = bf16[1024,512]{1,0:T(8,128)(2,1)} slice(bf16[2049,512]{1,0:T(8,128)(2,1)} %pad_maximum_fusion.3), slice={[0:2048:2], [0:512:1]} | slice | bytes 2097152 | tf_op jit(solution)/shard_map/slice | solution.py:114
  76.1 8.7 %fusion.110 = (f32[1024]{0:T(1024)S(1)}, f32[1024,512]{0,1:T(8,128)S(1)}, f32[1024,512]{0,1:T(8,128)}) fusion(f32[1024,256]{0,1:T(8,128)} %get-tuple-element.101, f32[1024,256]{0,1:T(8,128)} %get-tuple-element.100, f32[1024,512]{0,1:T(8,128)} %fusion.50, f32[1024,512]{0,1:T(8,128)} %fusion.53, bf16[1024,512]{1,0:T(8,128)(2,1)} %slice.109, ...), kind=kOutput, calls=%fused_computation.221 | convolution fusion | flops 573570048 | bytes 12064768 | tf_op jit(solution)/shard_map/dot_general | solution.py:49
  95.1 6.0 all-gather.5.cloned.1.call-done
  103.4 17.5 %multiply_reduce_fusion.1 = (f32[4,1024]{1,0:T(4,128)S(1)}, f32[4,1024,2048]{2,1,0:T(8,128)}) fusion(bf16[1024,4,64]{0,2,1:T(8,128)(2,1)} %bitcast.176, bf16[2048,4,64]{0,2,1:T(8,128)(2,1)} %bitcast.178), kind=kOutput, calls=%fused_computation.6 | convolution fusion | flops 1090514944 | bytes 35143680 | tf_op jit(solution)/shard_map/qhe,khe->hqk/dot_general | solution.py:136
  121.0 14.0 %fusion = f32[4,1024]{1,0:T(4,128)S(1)} fusion(f32[4,1024,2048]{2,1,0:T(8,128)} %get-tuple-element.107, f32[4,1024]{1,0:T(4,128)S(1)} %get-tuple-element.106), kind=kLoop, calls=%fused_computation.5 | loop fusion | flops 25161728 | bytes 33587200 | tf_op jit(solution)/shard_map/reduce_sum | solution.py:141
  137.3 15.3 %fusion.42 = bf16[4,64,1024]{2,1,0:T(8,128)(2,1)} fusion(bf16[2048,4,64]{0,2,1:T(8,128)(2,1)} %bitcast.189, f32[4,1024,2048]{2,1,0:T(8,128)} %get-tuple-element.107, f32[4,1024]{1,0:T(4,128)S(1)} %fusion, f32[4,1024]{1,0:T(4,128)S(1)} %get-tuple-element.106), kind=kOutput, calls=%fused_computation.126 | convolution fusion | flops 1107558400 | bytes 35160064 | tf_op jit(solution)/shard_map/hqk,khe->qhe/dot_general | solution.py:145
  158.0 38.5 %all-reduce.13.cloned.1.call-done = bf16[1024,512]{0,1:T(8,128)(2,1)} async-done(((bf16[1024,512]{0,1:T(8,128)(2,1)}), bf16[1024,512]{0,1:T(8,128)(2,1)}) %all-reduce.13.cloned.1.call-update) | async-done | bytes 1048592 | tf_op jit(solution)/shard_map/psum | solution.py:154
  198.5 11.5 %multiply_convert_fusion.1 = (bf16[1024,1024]{1,0:T(8,128)(2,1)}, f32[1024,1024]{1,0:T(8,128)S(1)}, f32[1024,1024]{1,0:T(8,128)S(1)}) fusion(f32[1024]{0:T(1024)S(1)} %convert_element_type.224, bf16[512,1024]{1,0:T(8,128)(2,1)S(1)} %copy-done, f32[1024,512]{0,1:T(8,128)S(1)} %get-tuple-element.89, f32[512]{0:T(512)S(1)} %convert_element_type.222, ...), kind=kOutput, calls=%fused_computation.20 | convolution fusion | flops 1145569280 | bytes 13647872 | tf_op jit(solution)/shard_map/dot_general | solution.py:49
  210.0 3.2 convert_reduce_fusion
  216.8 40.1 %all-reduce.15.cloned.1.call-done = bf16[1024,512]{0,1:T(8,128)(2,1)} async-done(((bf16[1024,512]{0,1:T(8,128)(2,1)}), bf16[1024,512]{0,1:T(8,128)(2,1)}) %all-reduce.15.cloned.1.call-update) | async-done | bytes 1048592 | tf_op jit(solution)/shard_map/psum | solution.py:172
  263.8 22.5 %multiply_reduce_fusion = (f32[4,1024]{1,0:T(4,128)S(1)}, f32[4,1024,2048]{2,1,0:T(8,128)}) fusion(f32[4,1024,2048]{2,1,0:T(8,128)} %get-tuple-element.107, f32[4,1024]{1,0:T(4,128)S(1)} %log_add_fusion, bf16[1024,4,64]{0,2,1:T(8,128)(2,1)S(1)} %bitcast.187, bf16[2048,4,64]{0,2,1:T(8,128)(2,1)S(1)} %bitcast.190), kind=kOutput, calls=%fused_computation.1 | convolution fusion | flops 1107292160 | bytes 68714496 | tf_op jit(solution)/shard_map/qhe,khe->hqk/dot_general | solution.py:189
  286.2 27.9 %multiply_convert_fusion = bf16[4,1024,2048]{2,1,0:T(8,128)(2,1)} fusion(f32[4,1024,2048]{2,1,0:T(8,128)} %get-tuple-element.110, f32[4,1024,2048]{2,1,0:T(8,128)} %get-tuple-element.107, f32[4,1024]{1,0:T(4,128)S(1)} %get-tuple-element.109, f32[4,1024]{1,0:T(4,128)S(1)} %log_add_fusion), kind=kLoop, calls=%fused_computation | loop fusion | flops 41943040 | bytes 83918848 | tf_op jit(solution)/shard_map/convert_element_type | solution.py:193
  314.1 9.9 %fusion.17 = bf16[4,64,2048]{2,1,0:T(8,128)(2,1)} fusion(bf16[1024,4,64]{0,2,1:T(8,128)(2,1)} %bitcast.177, bf16[4,1024,2048]{2,1,0:T(8,128)(2,1)} %multiply_convert_fusion), kind=kOutput, calls=%fused_computation.60 | convolution fusion | flops 1074790400 | bytes 18350080 | tf_op jit(solution)/shard_map/hqk,qhe->khe/dot_general | solution.py:203
  324.1 15.8 %fusion.18 = bf16[4,64,2048]{2,1,0:T(8,128)(2,1)} fusion(bf16[1024,4,64]{0,2,1:T(8,128)(2,1)} %bitcast.188, f32[4,1024,2048]{2,1,0:T(8,128)} %get-tuple-element.107, f32[4,1024]{1,0:T(4,128)S(1)} %log_add_fusion), kind=kOutput, calls=%fused_computation.61 | convolution fusion | flops 1099431936 | bytes 35143680 | tf_op jit(solution)/shard_map/hqk,qhe->khe/dot_general | solution.py:206
  340.1 4.2 convolution_convert_fusion.1
  344.2 12.6 %convert_reduce_fusion.8 = (f32[4,64]{1,0:T(4,128)S(1)}, bf16[4,64,1024]{2,1,0:T(8,128)(2,1)}) fusion(bf16[2048,4,64]{0,2,1:T(8,128)(2,1)} %bitcast.179, bf16[4,1024,2048]{2,1,0:T(8,128)(2,1)} %multiply_convert_fusion), kind=kOutput, calls=%fused_computation.136 | convolution fusion | flops 1074790144 | bytes 18351104 | tf_op jit(solution)/shard_map/hqk,khe->qhe/dot_general | solution.py:196
  362.7 3.9 add_convert_fusion.3
  367.3 4.7 fusion.45
  379.5 50.3 %all-reduce.19.cloned.1.call-done = (bf16[1024,512]{0,1:T(8,128)(2,1)}, bf16[1024,512]{0,1:T(8,128)(2,1)}) async-done(((bf16[1024,512]{0,1:T(8,128)(2,1)}, bf16[1024,512]{0,1:T(8,128)(2,1)}), (bf16[1024,512]{0,1:T(8,128)(2,1)}, bf16[1024,512]{0,1:T(8,128)(2,1)})) %all-reduce.19.cloned.1.call-update) | async-done | bytes 2097168 | tf_op jit(solution)/shard_map/psum | solution.py:161
  433.8 9.1 %convert_reduce_fusion.6 = (f32[512]{0:T(512)S(1)}, bf16[1024,512]{0,1:T(8,128)(2,1)S(1)}, bf16[1,1024,512]{1,2,0:T(8,128)(2,1)}) fusion(f32[1024,512]{0,1:T(8,128)S(1)} %copy-done.37, f32[1024]{0:T(1024)S(1)} %negate_multiply_fusion.3, f32[1024]{0:T(1024)S(1)} %multiply_multiply_fusion.15, f32[1024,512]{0,1:T(8,128)S(1)} %get-tuple-element.91, ...), kind=kLoop, calls=%fused_computation.85 | loop fusion | flops 51379712 | bytes 12627968 | tf_op jit(solution)/shard_map/reduce_sum | solution.py:65
  452.7 5.3 copy.59
  457.9 6.2 reshape.164
  466.6 3.5 pad_maximum_fusion.2
  490.0 64.3 %all-reduce.5 = (f32[512]{0:T(512)}, f32[512]{0:T(512)}, f32[512]{0:T(512)}, f32[512]{0:T(512)}, f32[2,256]{1,0:T(2,128)}, /*index=5*/f32[512]{0:T(512)}, f32[51...) all-reduce(f32[512]{0:T(512)S(1)} %get-tuple-element.84, ...), channel_id=1, replica_groups=mesh['dp'=8,'seq'=2,'mp'=2] {'dp','seq'}, use_global_device_ids=true, to_apply=%region_19.0 | all-reduce | flops 5632 | bytes 45056 | tf_op jit(solution)/shard_map/psum | solution.py:294
  556.5 118.5 %all-reduce.17.cloned.1.call-done = (f32[3,80,512]{2,1,0:T(8,128)}, f32[3,512,512]{2,1,0:T(8,128)}, f32[3,512,256]{2,1,0:T(8,128)}, f32[256,512]{1,0:T(8,128)}, f32[512,1024]{1,0:T(8,128)}, /*index=5*/f32[1024,512]{1,0:T(8,128)}) async-done(((f32[3,80,512]{2,1,0:T(8,128)}, f32[3,512,512]{2,1,0:T(8,128)}, f32[3,512,256]{2,1,0:T(8,128)}, f32[256,512]{1,0:T(8,128)}, f32[512,1024]{1,0:T(8,128)}, ...) | async-done | bytes 9928720 | tf_op jit(solution)/shard_map/psum | solution.py:294
  676.8 4.0 copy.78
  (268 shorter events, 108.6 us)
Async XLA Ops:
  7.2 191.2 %copy-start = (bf16[512,1024]{1,0:T(8,128)(2,1)S(1)}, bf16[512,1024]{1,0:T(8,128)(2,1)}, u32[]{:S(2)}) copy-start(bf16[512,1024]{1,0:T(8,128)(2,1)} %param.32) | copy-start | bytes 3145732
  7.2 94.0 %all-gather.5.cloned.1.call-start = ((), (), s32[]{:S(2)}) async-start(), calls=%async_computation.3 | async-start | bytes 1572864 | tf_op jit(solution)/shard_map/all_gather | solution.py:129
  8.2 12.3 %collective-permute-start = (bf16[80,1]{1,0:T(8,128)(2,1)S(1)}, bf16[80,1]{1,0:T(8,128)(2,1)S(1)}, u32[]{:S(2)}, u32[]{:S(2)}) collective-permute-start(bf16[80,1]{1,0:T(8,128)(2,1)S(1)} %get-tuple-element.99), channel_id=1, source_target_pairs={{0,2},{1,3},{4,6},{5,7},{8,10},{9,11},{12,14},{13,15},{16,18},{17,... | collective-permute-start | bytes 488 | tf_op jit(solution)/shard_map/ppermute | solution.py:16
  10.5 10.8 %collective-permute-start.1 = (bf16[80,1]{1,0:T(8,128)(2,1)S(1)}, bf16[80,1]{1,0:T(8,128)(2,1)S(1)}, u32[]{:S(2)}, u32[]{:S(2)}) collective-permute-start(bf16[80,1]{1,0:T(8,128)(2,1)S(1)} %get-tuple-element.98), channel_id=1, source_target_pairs={{2,0},{3,1},{6,4},{7,5},{10,8},{11,9},{14,12},{15,13},{18,16},{19,... | collective-permute-start | bytes 488 | tf_op jit(solution)/shard_map/ppermute | solution.py:19
  20.5 65.2 %copy-start.55 = (f32[512]{0:T(512)}, f32[512]{0:T(512)S(1)}, u32[]{:S(2)}) copy-start(f32[512]{0:T(512)S(1)} %convert_element_type.208) | copy-start | bytes 6148
  22.7 11.8 %copy-start.59 = (bf16[80,1]{1,0:T(8,128)(2,1)}, bf16[80,1]{1,0:T(8,128)(2,1)S(1)}, u32[]{:S(2)}) copy-start(bf16[80,1]{1,0:T(8,128)(2,1)S(1)} %collective-permute-done.1) | copy-start | bytes 484
  35.8 11.0 %copy-start.24 = (bf16[2048,512]{1,0:T(8,128)(2,1)S(1)}, bf16[2048,512]{1,0:T(8,128)(2,1)}, u32[]{:S(2)}) copy-start(bf16[2048,512]{1,0:T(8,128)(2,1)} %copy-done.23) | copy-start | bytes 6291460
  53.6 6.6 copy-start.31
  53.6 9.7 %collective-permute-start.2 = (bf16[1,512]{1,0:T(2,128)(2,1)S(1)}, bf16[1,512]{1,0:T(2,128)(2,1)S(1)}, u32[]{:S(2)}, u32[]{:S(2)}) collective-permute-start(bf16[1,512]{1,0:T(2,128)(2,1)S(1)} %slice.131), channel_id=1, source_target_pairs={{0,2},{1,3},{4,6},{5,7},{8,10},{9,11},{12,14},{13,15},{16,18},{17,... | collective-permute-start | bytes 3080 | tf_op jit(solution)/shard_map/ppermute | solution.py:27
  89.9 45.1 %all-gather.3.cloned.1.call-start = ((), (), s32[]{:S(2)}) async-start(), calls=%async_computation.2 | async-start | bytes 1572864 | tf_op jit(solution)/shard_map/all_gather | solution.py:130
  95.1 101.4 %all-reduce.13.cloned.1.call-start = ((), (), s32[]{:S(2)}) async-start(), calls=%async_computation.4 | async-start | bytes 2097152 | tf_op jit(solution)/shard_map/psum | solution.py:154
  137.3 15.3 %copy-start.43 = (bf16[256,512]{1,0:T(8,128)(2,1)S(1)}, bf16[256,512]{1,0:T(8,128)(2,1)}, u32[]{:S(2)}) copy-start(bf16[256,512]{1,0:T(8,128)(2,1)} %param.28) | copy-start | bytes 786436
  152.6 5.4 copy-start.61
  155.1 101.8 %all-reduce.15.cloned.1.call-start = ((), (), s32[]{:S(2)}) async-start(), calls=%async_computation.5 | async-start | bytes 2097152 | tf_op jit(solution)/shard_map/psum | solution.py:172
  198.1 11.9 %copy-start.2 = (f32[1024,512]{0,1:T(8,128)}, f32[1024,512]{0,1:T(8,128)S(1)}, u32[]{:S(2)}) copy-start(f32[1024,512]{0,1:T(8,128)S(1)} %get-tuple-element.89) | copy-start | bytes 6291460
  198.4 11.5 %copy-start.15 = (bf16[1,1024,512]{1,2,0:T(8,128)(2,1)S(1)}, bf16[1,1024,512]{1,2,0:T(8,128)(2,1)}, u32[]{:S(2)}) copy-start(bf16[1,1024,512]{1,2,0:T(8,128)(2,1)} %copy.54) | copy-start | bytes 3145732
  198.4 11.5 %copy-start.72 = (bf16[1024,512]{1,0:T(8,128)(2,1)S(1)}, bf16[1024,512]{1,0:T(8,128)(2,1)}, u32[]{:S(2)}) copy-start(bf16[1024,512]{1,0:T(8,128)(2,1)} %param.34) | copy-start | bytes 3145732
  216.8 143.0 %reduce-scatter.3.cloned.1.call-start = ((), (), s32[]{:S(2)}) async-start(), calls=%async_computation.6 | async-start | bytes 1572864 | tf_op jit(solution)/shard_map/reduce_scatter | solution.py:213
  263.6 22.6 %copy-start.26 = (bf16[1024,256]{0,1:T(8,128)(2,1)}, bf16[1024,256]{0,1:T(8,128)(2,1)S(1)}, u32[]{:S(2)}) copy-start(bf16[1024,256]{0,1:T(8,128)(2,1)S(1)} %convolution_convert_fusion.3) | copy-start | bytes 1572868
  324.1 38.6 %reduce-scatter.5.cloned.1.call-start = ((), (), s32[]{:S(2)}) async-start(), calls=%async_computation.7 | async-start | bytes 1572864 | tf_op jit(solution)/shard_map/reduce_scatter | solution.py:216
  340.0 89.8 %all-reduce.19.cloned.1.call-start = ((), (), s32[]{:S(2)}) async-start(), calls=%async_computation.9 | async-start | bytes 4194304 | tf_op jit(solution)/shard_map/psum | solution.py:161
  366.6 308.4 %all-reduce.17.cloned.1.call-start = ((), (), s32[]{:S(2)}) async-start(), calls=%async_computation.8 | async-start | bytes 19857408 | tf_op jit(solution)/shard_map/psum | solution.py:294
  378.3 51.6 %copy-start.50 = (f32[1024]{0:T(1024)S(1)}, f32[1024]{0:T(1024)}, u32[]{:S(2)}) copy-start(f32[1024]{0:T(1024)} %copy-done.49) | copy-start | bytes 12292
  378.3 51.6 %copy-start.56 = (f32[512]{0:T(512)S(1)}, f32[512]{0:T(512)}, u32[]{:S(2)}) copy-start(f32[512]{0:T(512)} %copy-done.55) | copy-start | bytes 6148
  379.5 52.4 %copy-start.58 = (f32[1024]{0:T(1024)S(1)}, f32[1024]{0:T(1024)}, u32[]{:S(2)}) copy-start(f32[1024]{0:T(1024)} %copy-done.57) | copy-start | bytes 12292
  379.5 52.5 %copy-start.54 = (f32[1024]{0:T(1024)S(1)}, f32[1024]{0:T(1024)}, u32[]{:S(2)}) copy-start(f32[1024]{0:T(1024)} %copy-done.53) | copy-start | bytes 12292
  433.8 9.1 %copy-start.29 = (bf16[3,512,512]{2,1,0:T(8,128)(2,1)S(1)}, bf16[3,512,512]{2,1,0:T(8,128)(2,1)}, u32[]{:S(2)}) copy-start(bf16[3,512,512]{2,1,0:T(8,128)(2,1)} %param.22) | copy-start | bytes 4718596
  444.5 7.2 %copy-start.6 = (f32[1024,512]{1,0:T(8,128)}, f32[1024,512]{1,0:T(8,128)S(1)}, u32[]{:S(2)}) copy-start(f32[1024,512]{1,0:T(8,128)S(1)} %fusion.55) | copy-start | bytes 6291460
  457.9 8.6 %copy-start.45 = (f32[1,512,512]{2,1,0:T(8,128)S(1)}, f32[1,512,512]{2,1,0:T(8,128)}, u32[]{:S(2)}) copy-start(f32[1,512,512]{2,1,0:T(8,128)} %convolution_bitcast_fusion.6) | copy-start | bytes 3145732
  464.8 5.8 collective-permute-start.3
  484.7 3.1 collective-permute-start.5
  487.9 66.6 %collective-permute-start.4 = (f32[80,1]{1,0:T(8,128)S(1)}, f32[80,1]{1,0:T(8,128)S(1)}, u32[]{:S(2)}, u32[]{:S(2)}) collective-permute-start(f32[80,1]{1,0:T(8,128)S(1)} %get-tuple-element.96), channel_id=1, source_target_pairs={{0,2},{1,3},{4,6},{5,7},{8,10},{9,11},{12,14},{13,15},{16,18},{17,... | collective-permute-start | bytes 968 | tf_op jit(solution)/shard_map/ppermute | solution.py:16
  (57 other events, 143.0 us)
Sparse Core Ops, SparseCore 0:
  90.0 11.1 all-gather.4
  103.3 10.2 all-gather.2
  155.3 41.2 all-reduce.12
  216.9 40.0 all-reduce.14
  324.2 8.5 reduce-scatter.2
  340.1 8.5 reduce-scatter.4
  366.7 63.0 all-reduce.18
  479.1 195.8 all-reduce.16
where the time goes:
time: 704 us; the launch traced here: 694 us
  waiting for transfers between devices  255 us (36%)
  matrix products  187 us (27%)
  local copies, waits for them, and re-layouts  80.3 us (11%)
  other arithmetic  78.6 us (11%)
  blocking collectives  64.3 us (9%)
  between operations  15.2 us (2%)
  starting transfers between devices  12.8 us (2%)
    psum x1, waiting for transfers between devices, on_device(): lax.psum((grad_conv1, grad_conv1_bias, grad_conv2, grad_conv2_bias, grad_...  119 us
    psum x1, blocking collectives, on_device(): lax.psum((grad_conv1, grad_conv1_bias, grad_conv2, grad_conv2_bias, grad_...  64.3 us
    psum x1, waiting for transfers between devices, on_device(): lax.psum(product(active, down_weight).astype(jnp.bfloat16), 'mp')  50.3 us
    dot_general x9, matrix products, product(): return jnp.dot(left_side, right_side, preferred_element_type=jnp.float32)  40.6 us
    psum x1, waiting for transfers between devices, on_device(): lax.psum(against(inner_grad, up_weight).astype(jnp.bfloat16), 'mp')  40.1 us
    psum x1, waiting for transfers between devices, on_device(): lax.psum(product(mixture, out_weight).astype(jnp.bfloat16), 'mp')  38.5 us
    unnamed x158, local copies, waits for them, and re-layouts  32.1 us
    slice x3, local copies, waits for them, and re-layouts, on_device(): stride_taps = [shifted[offset:offset + 2 * frames:2] for offset in range(3)]  28.7 us
  transfers between devices with their start and end apart: 14, of which 6 were waited for; matrix products, arithmetic and copies ran while one was open for 17% of the time, Pallas kernels for 0%

commit v1 on v0

v1 whole, which is shorter than its diff:
```python
import functools
import math

import jax
import jax.numpy as jnp
from jax import lax
from jax.experimental import pallas as pl
from jax.experimental.pallas import tpu as pltpu
from jax.sharding import PartitionSpec as P

HEAD = 64
BF = jnp.bfloat16
F32 = jnp.float32
MESH = pl.DeviceIdType.MESH
VMEM_LIMIT = 60 * 1024 * 1024
C1B, C2B, N1G, N1B, OUB, N2G, N2B, DNB, QB, VB, UPB = range(11)


class Box:
    pass


def dot(a, b, ca, cb):
    return lax.dot_general(a, b, (((ca,), (cb,)), ((), ())), preferred_element_type=F32)


def nn(a, b):
    return dot(a, b, 1, 0)


def nt(a, b):
    return dot(a, b, 1, 1)


def tn(a, b):
    return dot(a, b, 0, 0)


def rows_loop(total, step, body, unroll=1):
    step = min(step, total)

    def one(i, carry):
        body(pl.ds(pl.multiple_of(i * step, step), step))
        return carry

    lax.fori_loop(0, total // step, one, 0, unroll=unroll)


def gelu_parts(v):
    t = 1.0 / (1.0 + (0.3275911 / math.sqrt(2.0)) * jnp.abs(v))
    e = jnp.exp(-0.5 * v * v)
    poly = 1.061405429 * t - 1.453152027
    poly = poly * t + 1.421413741
    poly = poly * t - 0.284496736
    poly = poly * t + 0.254829592
    tail = (0.5 * t) * poly * e
    return jnp.where(v >= 0, 1.0 - tail, tail), e * (1.0 / math.sqrt(2.0 * math.pi))


def gelu_both(v):
    cdf, pdf = gelu_parts(v)
    return v * cdf, cdf + v * pdf


def normal(x):
    center = x - jnp.mean(x, axis=-1, keepdims=True)
    spread = jnp.mean(center * center, axis=-1, keepdims=True)
    inv = lax.rsqrt(spread + 1e-05)
    return center * inv, inv


def normal_pull(gy, hat, inv):
    return inv * (
        gy
        - jnp.mean(gy, axis=-1, keepdims=True)
        - hat * jnp.mean(gy * hat, axis=-1, keepdims=True)
    )


def vec(r, i):
    return r.vecs[i : i + 1, :]


def add_small(r, i, value):
    r.small[i : i + 1, :] += value


def col(value):
    return jnp.sum(value, axis=0, keepdims=True)


def stage_stem(r):
    T, D = r.stream.shape
    c = lax.axis_index("seq")
    m = lax.axis_index("mp")
    w1 = r.w1[...]
    first = jnp.logical_and(c == 0, m == 0)
    edge = nn(r.xh[...], w1) + vec(r, C1B)
    edge = gelu_both(edge)[0] * jnp.where(first, 0.0, 1.0)
    r.odd[0:8, :] = edge[0:8, :]
    r.tmp[...] = nn(r.xe[...], w1)

    def even(rows):
        value, slope = gelu_both(r.tmp[rows, :] + vec(r, C1B))
        r.he[rows, :] = value.astype(BF)
        r.dge[rows, :] = slope

    rows_loop(T, 32, even)
    r.tmp[...] = nn(r.xo[...], w1)

    def odd(rows):
        value, slope = gelu_both(r.tmp[rows, :] + vec(r, C1B))
        r.ho[rows, :] = value.astype(BF)
        r.odd[pl.ds(pl.multiple_of(rows.start + 8, 8), rows.size), :] = value
        r.dgo[rows, :] = slope

    rows_loop(T, 32, odd)
    r.hp[...] = r.odd[7 : 7 + T, :].astype(BF)
    r.tmp[...] = nn(r.hp[...], r.w2[0]) + nn(r.he[...], r.w2[1]) + nn(r.ho[...], r.w2[2])

    def second(rows):
        value, slope = gelu_both(r.tmp[rows, :] + vec(r, C2B))
        stream = value + r.pos[rows, :]
        r.dg2[rows, :] = slope
        r.stream[rows, :] = stream
        r.normed[rows, :] = (normal(stream)[0] * vec(r, N1G) + vec(r, N1B)).astype(BF)

    rows_loop(T, 32, second)


def stage_qkv(r):
    T, D = r.stream.shape
    half = D // 2
    normed = r.normed[...]
    for part, bias, scale in ((1, None, 1.0), (2, VB, 1.0), (0, QB, HEAD**-0.5)):
        for m in range(2):
            value = nn(normed, r.wqkv[m, part])
            if bias is not None:
                value = value + r.vecs[bias : bias + 1, m * half : (m + 1) * half]
            value = (value.astype(BF).astype(F32) * scale).T.astype(BF)
            if part == 0:
                r.qt[m * half : (m + 1) * half, :] = value
            else:
                r.kv[part - 1, m * half : (m + 1) * half, :] = value


def head_rows(h):
    return pl.ds(pl.multiple_of(h * HEAD, HEAD), HEAD)


def attend_block(r, kv, first):
    D, T = r.qt.shape

    def one(h, carry):
        rows = head_rows(h)
        s = tn(kv[0, rows, :], r.qt[rows, :])
        top = jnp.max(s, axis=0, keepdims=True)
        if not first:
            top = jnp.maximum(top, r.top[h])
        p = jnp.exp(s - top)
        total = jnp.sum(p, axis=0, keepdims=True)
        mixed = nn(kv[1, rows, :], p.astype(BF))
        if not first:
            keep = jnp.exp(r.top[h] - top)
            total = total + keep * r.total[h]
            mixed = mixed + keep * r.mixt[rows, :]
        r.top[h] = top
        r.total[h] = total
        r.mixt[rows, :] = mixed
        return carry

    lax.fori_loop(0, D // HEAD, one, 0)


def attend_end(r):
    D, T = r.qt.shape

    def one(h, carry):
        rows = head_rows(h)
        total = r.total[h]
        value = r.mixt[rows, :] * (1.0 / total)
        r.mixt[rows, :] = value
        r.mixb[rows, :] = value.astype(BF)
        r.top[h] = r.top[h] + jnp.log(total)
        return carry

    lax.fori_loop(0, D // HEAD, one, 0)


def stage_mid(r):
    T, D = r.stream.shape
    r.tmp[...] = tn(r.mixb[...], r.wo[...])

    def one(rows):
        mid = r.stream[rows, :] + r.tmp[rows, :] + vec(r, OUB)
        r.mid[rows, :] = mid
        r.ntwo[rows, :] = (normal(mid)[0] * vec(r, N2G) + vec(r, N2B)).astype(BF)

    rows_loop(T, 32, one)


def stage_ff(r):
    T, D = r.stream.shape
    parts = r.up.shape[0]
    width = r.up.shape[2]
    add_small(r, DNB, col(r.bg[...].astype(F32)))

    def chunk(j, carry):
        r.tmp[...] = nn(r.ntwo[...], r.up[j])
        r.tmp2[...] = nt(r.bg[...], r.down[j])
        bias = r.vecs[pl.ds(UPB + j, 1), :]

        def one(i, acc):
            rows = pl.ds(pl.multiple_of(i * 32, 32), 32)
            value, slope = gelu_both(r.tmp[rows, :] + bias)
            r.act[rows, :] = value.astype(BF)
            grad = (r.tmp2[rows, :] * slope).astype(BF)
            r.ing[rows, :] = grad
            return acc + col(grad.astype(F32))

        r.small[pl.ds(UPB + j, 1), :] = lax.fori_loop(0, T // 32, one, jnp.zeros((1, width), F32))
        act = r.act[...]
        ing = r.ing[...]
        out = nn(act, r.down[j])
        back = nt(ing, r.up[j])

        @pl.when(j == 0)
        def _():
            r.ffo[...] = out
            r.ntg[...] = back

        @pl.when(j > 0)
        def _():
            r.ffo[...] += out
            r.ntg[...] += back

        r.gdown[j] = tn(act, r.bg[...]).astype(BF)
        r.gup[j] = tn(r.ntwo[...], ing).astype(BF)
        return carry

    lax.fori_loop(0, parts, chunk, 0)


def stage_mid_pull(r):
    T, D = r.stream.shape

    def one(i, accs):
        rows = pl.ds(pl.multiple_of(i * 32, 32), 32)
        mid = r.mid[rows, :]
        r.enc[rows, :] = (mid + r.ffo[rows, :] + vec(r, DNB)).astype(BF)
        hat, inv = normal(mid)
        grad = r.ntg[rows, :]
        smg = r.bg[rows, :].astype(F32) + normal_pull(grad * vec(r, N2G), hat, inv)
        r.smg[rows, :] = smg
        attg = smg.astype(BF)
        r.attg[rows, :] = attg
        return accs[0] + col(grad * hat), accs[1] + col(grad), accs[2] + col(attg.astype(F32))

    zero = jnp.zeros((1, D), F32)
    gain, bias, out_bias = lax.fori_loop(0, T // 32, one, (zero, zero, zero))
    add_small(r, N2G, gain)
    add_small(r, N2B, bias)
    add_small(r, OUB, out_bias)
    attg = r.attg[...]
    r.dot[...] = nt(r.wo[...], attg).astype(BF)
    r.gout[...] = nn(r.mixb[...], attg).astype(BF)

    def head(h, carry):
        rows = head_rows(h)
        r.diag[h] = jnp.sum(r.dot[rows, :].astype(F32) * r.mixt[rows, :], axis=0, keepdims=True)
        return carry

    lax.fori_loop(0, D // HEAD, head, 0)


def pull_block(r, kv, dkv, first):
    D, T = r.qt.shape

    def one(h, carry):
        rows = head_rows(h)
        k, v, q, do = kv[0, rows, :], kv[1, rows, :], r.qt[rows, :], r.dot[rows, :]
        p = jnp.exp(tn(k, q) - r.top[h])
        ds = (p * (tn(v, do) - r.diag[h])).astype(BF)
        dkv[1, rows, :] = nt(do, p.astype(BF)).astype(dkv.dtype)
        dkv[0, rows, :] = nt(q, ds).astype(dkv.dtype)
        dq = nn(k, ds)
        if first:
            r.dqt[rows, :] = dq
        else:
            r.dqt[rows, :] += dq
        return carry

    lax.fori_loop(0, D // HEAD, one, 0)


def stage_qkv_pull(r):
    T, D = r.stream.shape
    half = D // 2
    normedt = r.normed[...].astype(F32).T.astype(BF)
    ones = jnp.ones((8, T), BF)
    total = None
    for part, ref in enumerate((r.dqb, r.dkb, r.dvb)):
        if part != 1:
            add_small(r, QB if part == 0 else VB, nt(ones, ref[...])[0:1, :])
        for m in range(2):
            piece = ref[m * half : (m + 1) * half, :]
            grad = nt(normedt, piece).astype(BF)
            r.gqkv[m, part, :, 0:half] = grad[0:half, :]
            r.gqkv[m, part, :, half : 2 * half] = grad[half : 2 * half, :]
            back = nn(r.wqkv[m, part], piece)
            total = back if total is None else total + back
    r.tmp[...] = total.T

    def one(i, accs):
        rows = pl.ds(pl.multiple_of(i * 32, 32), 32)
        hat, inv = normal(r.stream[rows, :])
        grad = r.tmp[rows, :]
        back = r.smg[rows, :] + normal_pull(grad * vec(r, N1G), hat, inv)
        sg = (back * r.dg2[rows, :]).astype(BF)
        r.sg[rows, :] = sg
        return accs[0] + col(grad * hat), accs[1] + col(grad), accs[2] + col(sg.astype(F32))

    zero = jnp.zeros((1, D), F32)
    gain, bias, c2b = lax.fori_loop(0, T // 32, one, (zero, zero, zero))
    add_small(r, N1G, gain)
    add_small(r, N1B, bias)
    add_small(r, C2B, c2b)


def stage_conv2_pull(r, next_row):
    T, D = r.stream.shape
    sg = r.sg[...]
    r.shift[0:T, :] = nt(sg, r.w2[0])
    r.shift[T : T + 16, :] = nt(next_row, r.w2[0])
    r.tmp[...] = nt(sg, r.w2[1])
    r.tmp2[...] = nt(sg, r.w2[2]) + r.shift[1 : T + 1, :]

    def one(i, acc):
        rows = pl.ds(pl.multiple_of(i * 32, 32), 32)
        even = (r.tmp[rows, :] * r.dge[rows, :]).astype(BF)
        odd = (r.tmp2[rows, :] * r.dgo[rows, :]).astype(BF)
        r.fe[rows, :] = even
        r.fo[rows, :] = odd
        return acc + col(even.astype(F32)) + col(odd.astype(F32))

    add_small(r, C1B, lax.fori_loop(0, T // 32, one, jnp.zeros((1, D), F32)))


def stage_conv_weights(r):
    sg = r.sg[...]
    r.gc2[0] = tn(r.hp[...], sg).astype(BF)
    r.gc2[1] = tn(r.he[...], sg).astype(BF)
    r.gc2[2] = tn(r.ho[...], sg).astype(BF)
    r.gc1[...] = (tn(r.xe[...], r.fe[...]) + tn(r.xo[...], r.fo[...])).astype(BF)


def stage_mel(r, next_row, prev_row):
    T, D = r.stream.shape
    fe, fo = r.fe[...], r.fo[...]
    r.wide[16 : 16 + T, :] = nt(fo, r.w1p[2])
    r.wide[0:16, :] = nt(prev_row, r.w1p[2])
    r.melg[:, 0:128] = nt(fe, r.w1p[1]) + nt(fo, r.w1p[0]) + r.wide[15 : 15 + T, :]
    r.wide[0:T, :] = nt(fe, r.w1p[0])
    r.wide[T : T + 16, :] = nt(next_row, r.w1p[0])
    r.melg[:, 128:256] = nt(fe, r.w1p[2]) + nt(fo, r.w1p[1]) + r.wide[1 : 1 + T, :]


def call(name, body, ins, outs, scratch, sems=(), **params):
    names_in, names_out, names_scr = list(ins), list(outs), list(scratch)

    def kernel(*refs):
        r = Box()
        names = names_in + names_out + names_scr + [n for n, _ in sems]
        for n, ref in zip(names, refs):
            setattr(r, n, ref)
        body(r)

    got = pl.pallas_call(
        kernel,
        name=name,
        out_shape=[jax.ShapeDtypeStruct(*outs[n]) for n in names_out],
        in_specs=[pl.BlockSpec(memory_space=pltpu.VMEM)] * len(ins),
        out_specs=[pl.BlockSpec(memory_space=pltpu.VMEM)] * len(outs),
        scratch_shapes=[pltpu.VMEM(*scratch[n]) for n in names_scr] + [s for _, s in sems],
        compiler_params=pltpu.CompilerParams(vmem_limit_bytes=VMEM_LIMIT, **params),
    )(*[ins[n] for n in names_in])
    return dict(zip(names_out, got))


def kernel_stem(r):
    stage_stem(r)
    stage_qkv(r)


def kernel_mid(r):
    r.small[...] = jnp.zeros_like(r.small)
    for b in range(4):
        attend_block(r, r.kvs.at[b], b == 0)
    attend_end(r)
    stage_mid(r)
    stage_ff(r)
    stage_mid_pull(r)
    for b in range(4):
        pull_block(r, r.kvs.at[b], r.dkvs.at[b], b == 0)
    r.dqb[...] = (r.dqt[...] * HEAD**-0.5).astype(BF)


def partners():
    c, m, d = lax.axis_index("seq"), lax.axis_index("mp"), lax.axis_index("dp")
    return (d, 1 - c, m), (d, c, 1 - m)


def rim_copies(r, source, slots, start):
    copies = []
    for i, target in enumerate(partners()):
        copies.append(
            pltpu.make_async_remote_copy(
                src_ref=source,
                dst_ref=slots.at[i],
                send_sem=r.send.at[start + i],
                recv_sem=r.recv.at[start + i],
                device_id=target,
                device_id_type=MESH,
            )
        )
    return copies


def quarter():
    c, m = lax.axis_index("seq"), lax.axis_index("mp")
    return 2 * c + jnp.bitwise_xor(c, m)


def pick_next(slots):
    q = quarter()
    by_y = jnp.where(q % 2 == 0, 1.0, 0.0)
    by_core = jnp.where(q == 1, 1.0, 0.0)
    return (slots[0].astype(F32) * by_core + slots[1].astype(F32) * by_y).astype(BF)


def pick_prev(slots):
    q = quarter()
    by_y = jnp.where(q % 2 == 1, 1.0, 0.0)
    by_core = jnp.where(q == 2, 1.0, 0.0)
    return (slots[0].astype(F32) * by_core + slots[1].astype(F32) * by_y).astype(BF)


def kernel_back(r):
    T, D = r.stream.shape
    barrier = pltpu.get_barrier_semaphore()
    for target in partners():
        pl.semaphore_signal(barrier, inc=1, device_id=target, device_id_type=MESH)
    pl.semaphore_wait(barrier, 2)
    r.small[...] = jnp.zeros_like(r.small)
    stage_qkv_pull(r)
    first = rim_copies(r, r.sg.at[0:16], r.slots.at[0], 0)
    for copy in first:
        copy.start()
    for copy in first:
        copy.wait()
    stage_conv2_pull(r, pick_next(r.slots.at[0]))
    second = rim_copies(r, r.fe.at[0:16], r.slots.at[1], 2)
    second += rim_copies(r, r.fo.at[T - 16 : T], r.slots.at[2], 4)
    for copy in second:
        copy.start()
    stage_conv_weights(r)
    for copy in second:
        copy.wait()
    stage_mel(r, pick_next(r.slots.at[1]), pick_prev(r.slots.at[2]))


def sinusoids(positions, channels):
    half_width = channels // 2
    increment = math.log(10000.0) / (half_width - 1)
    inverse = jnp.exp(-increment * jnp.arange(half_width, dtype=F32))
    angles = positions.astype(F32)[:, None] * inverse[None, :]
    return jnp.concatenate([jnp.sin(angles), jnp.cos(angles)], axis=1)


def on_device(
    mel_input,
    conv1_weight,
    conv1_bias,
    conv2_weight,
    conv2_bias,
    norm1_gain,
    norm1_bias,
    qkv_weight,
    qkv_bias,
    out_weight,
    out_bias,
    norm2_gain,
    norm2_bias,
    up_weight,
    up_bias,
    down_weight,
    down_bias,
    cotangent,
    speech_mask,
):
    mel = mel_input[0]
    mels, span = mel.shape
    T, D = cotangent.shape[1] // 2, cotangent.shape[2]
    F = 2 * up_weight.shape[1]
    NF = F // D
    H = D // HEAD
    half = D // 2
    c, m = lax.axis_index("seq"), lax.axis_index("mp")
    sub = jnp.bitwise_xor(c, m)

    low = lax.ppermute(mel[:, -2:], "seq", [(0, 1)])
    high = lax.ppermute(mel[:, :2], "seq", [(1, 0)])
    window = lax.dynamic_slice_in_dim(
        jnp.concatenate([low, mel, high], axis=1), sub * 2 * T, 2 * T + 4, axis=1
    )
    pairs = window.T.reshape(T + 2, 2 * mels)
    xe = jnp.concatenate([pairs[0:T, mels:], pairs[1 : T + 1]], axis=1)
    xo = jnp.concatenate([pairs[1 : T + 1], pairs[2 : T + 2, :mels]], axis=1)
    xh = jnp.concatenate([pairs[0:1], pairs[1:2, :mels]], axis=1)
    lanes = -(-3 * mels // 128) * 128
    xe = jnp.pad(xe, ((0, 0), (0, lanes - 3 * mels)))
    xo = jnp.pad(xo, ((0, 0), (0, lanes - 3 * mels)))
    xh = jnp.pad(xh, ((15, 0), (0, lanes - 3 * mels)))
    xh = jnp.roll(xh, 8, axis=0)
    w1 = jnp.pad(conv1_weight.reshape(3 * mels, D), ((0, lanes - 3 * mels), (0, 0)))
    w1p = jnp.pad(conv1_weight, ((0, 0), (0, 128 - mels), (0, 0)))
    pos = sinusoids((c * 2 + sub) * T + jnp.arange(T, dtype=jnp.int32), D)

    wqkv = lax.all_gather(qkv_weight, "mp", axis=0)
    wo = lax.all_gather(out_weight, "mp", axis=0, tiled=True)
    up = lax.all_gather(
        up_weight.reshape(D, NF // 2, D).transpose(1, 0, 2), "mp", axis=0, tiled=True
    )
    down = lax.all_gather(down_weight.reshape(NF // 2, D, D), "mp", axis=0, tiled=True)
    qb = lax.all_gather(qkv_bias, "mp", axis=1, tiled=True)
    ub = lax.all_gather(up_bias, "mp", axis=0, tiled=True).reshape(NF, D)
    table = [conv1_bias, conv2_bias, norm1_gain, norm1_bias, out_bias, norm2_gain, norm2_bias]
    table = jnp.stack(table + [down_bias, qb[0], qb[1]])
    vecs = jnp.concatenate([table, ub], axis=0).astype(F32)
    vecs = jnp.pad(vecs, ((0, 16 - vecs.shape[0]), (0, 0)))

    cot = lax.dynamic_slice_in_dim(cotangent[0], sub * T, T, axis=0)
    mask = lax.dynamic_slice_in_dim(speech_mask[0], sub * T, T, axis=0)
    bg = cot * mask.astype(BF)[:, None]

    td, dt = (T, D), (D, T)
    a = call(
        "stem",
        kernel_stem,
        dict(xe=xe, xo=xo, xh=xh, w1=w1, w2=conv2_weight, vecs=vecs, pos=pos, wqkv=wqkv),
        dict(
            he=(td, BF), ho=(td, BF), hp=(td, BF), dge=(td, F32), dgo=(td, F32), dg2=(td, F32),
            stream=(td, F32), normed=(td, BF), qt=(dt, BF), kv=((2, D, T), BF),
        ),
        dict(tmp=(td, F32), odd=((T + 8, D), F32)),
    )
    kvs = lax.all_gather(a["kv"], ("seq", "mp"), axis=0)
    b = call(
        "middle",
        kernel_mid,
        dict(kvs=kvs, qt=a["qt"], stream=a["stream"], wo=wo, up=up, down=down, bg=bg, vecs=vecs),
        dict(
            enc=(td, BF), gdown=((NF, D, D), BF), gup=((NF, D, D), BF), gout=((D, D), BF),
            small=((16, D), F32), smg=(td, F32), dqb=(dt, BF), dkvs=((4, 2, D, T), BF),
        ),
        dict(
            tmp=(td, F32), tmp2=(td, F32), top=((H, 1, T), F32), total=((H, 1, T), F32),
            mixt=(dt, F32), mixb=(dt, BF), mid=(td, F32), ntwo=(td, BF), act=(td, BF),
            ing=(td, BF), ffo=(td, F32), ntg=(td, F32), attg=(td, BF), dot=(dt, BF),
            diag=((H, 1, T), F32), dqt=(dt, F32),
        ),
    )
    dkv = lax.psum_scatter(b["dkvs"], ("seq", "mp"), scatter_dimension=0, tiled=True)[0]
    e = call(
        "back",
        kernel_back,
        dict(
            dqb=b["dqb"], dkb=dkv[0], dvb=dkv[1], smg=b["smg"], vecs=vecs, wqkv=wqkv, w2=conv2_weight,
            w1p=w1p, xe=xe, xo=xo, he=a["he"], ho=a["ho"], hp=a["hp"], dge=a["dge"], dgo=a["dgo"],
            dg2=a["dg2"], stream=a["stream"], normed=a["normed"],
        ),
        dict(
            gqkv=((2, 3, half, D), BF), gc2=((3, D, D), BF), gc1=((lanes, D), BF),
            small=((16, D), F32), melg=((T, 256), F32),
        ),
        dict(
            tmp=(td, F32), tmp2=(td, F32), sg=(td, BF), fe=(td, BF), fo=(td, BF),
            shift=((T + 16, D), F32), wide=((T + 16, 128), F32), slots=((3, 2, 16, D), BF),
        ),
        (("send", pltpu.SemaphoreType.DMA((6,))), ("recv", pltpu.SemaphoreType.DMA((6,)))),
        collective_id=1,
        has_side_effects=True,
    )

    packed = jnp.concatenate(
        [
            b["gdown"].reshape(2, -1, D),
            b["gup"].reshape(2, -1, D),
            b["gout"].reshape(2, -1, D),
            e["gqkv"].reshape(2, -1, D),
        ],
        axis=1,
    )
    mine = lax.psum_scatter(packed, "mp", scatter_dimension=0, tiled=True)[0]
    mine = lax.psum(mine, ("dp", "seq")).astype(F32)
    conv = jnp.concatenate([e["gc2"].reshape(-1, D), e["gc1"]], axis=0)
    conv = lax.psum(conv, ("dp", "seq", "mp")).astype(F32)
    small = lax.psum(b["small"] + e["small"], ("dp", "seq", "mp"))
    cut = [F // 2, F, F + half, F + half + 3 * half]
    grad_down = mine[: cut[0]]
    grad_up = mine[cut[0] : cut[1]].reshape(NF // 2, D, D).transpose(1, 0, 2).reshape(D, F // 2)
    grad_out = mine[cut[1] : cut[2]]
    grad_qkv = mine[cut[2] : cut[3]].reshape(3, half, 2, half).transpose(0, 2, 1, 3).reshape(3, D, half)
    grad_conv2 = conv[: 3 * D].reshape(3, D, D)
    grad_conv1 = conv[3 * D : 3 * D + 3 * mels].reshape(3, mels, D)
    own_half = lax.dynamic_slice_in_dim(small[QB : QB + 2], m * half, half, axis=1)
    own_up = lax.dynamic_slice_in_dim(
        small[UPB : UPB + NF], m * (NF // 2), NF // 2, axis=0
    ).reshape(-1)

    def ordered(value):
        both = lax.all_gather(value, "mp", axis=0)
        both = jnp.where(c == 0, both, both[::-1])
        return both.reshape((-1,) + value.shape[1:])

    encoded = ordered(b["enc"])[None]
    melg = ordered(e["melg"]).reshape(4 * T, 128)[:, :mels].T[None]
    return (
        encoded,
        melg,
        grad_conv1,
        small[C1B],
        grad_conv2,
        small[C2B],
        small[N1G],
        small[N1B],
        grad_qkv,
        own_half,
        grad_out,
        small[OUB],
        small[N2G],
        small[N2B],
        grad_up,
        own_up,
        grad_down,
        small[DNB],
    )


def solution(mesh):
    placed = (
        P("dp", None, "seq"),
        P(),
        P(),
        P(),
        P(),
        P(),
        P(),
        P(None, None, "mp"),
        P(None, "mp"),
        P("mp", None),
        P(),
        P(),
        P(),
        P(None, "mp"),
        P("mp"),
        P("mp", None),
        P(),
        P("dp", "seq", None),
        P("dp", "seq"),
    )
    return jax.shard_map(
        on_device,
        mesh=mesh,
        in_specs=placed,
        out_specs=(
            P("dp", "seq", None),
            P("dp", None, "seq"),
            P(),
            P(),
            P(),
            P(),
            P(),
            P(),
            P(None, None, "mp"),
            P(None, "mp"),
            P("mp", None),
            P(),
            P(),
            P(),
            P(None, "mp"),
            P("mp"),
            P("mp", None),
            P(),
        ),
        check_vma=False,
    )
```

time: 704 us -> 698 us (level); the launches traced: 694 us -> 698 us
  waiting for transfers between devices: 255 us -> 449 us
  matrix products: 187 us -> 0 us
  Pallas kernels: 0 us -> 114 us
  other arithmetic: 78.6 us -> 20.3 us
  local copies, waits for them, and re-layouts: 80.3 us -> 31.8 us
  starting transfers between devices: 12.8 us -> 4.26 us
    dot_general x42 -> x0, matrix products: 187 us -> none  [the longest x9 40.6 us: product(): return jnp.dot(left_side, right_side, preferred_element_type=jnp.float32)]
    all_gather x2 -> x6, waiting for transfers between devices: 6.07 us -> 129 us  [the longest x2 39.3 us: ordered(): both = lax.all_gather(value, 'mp', axis=0)]
    reduce_scatter x2, waiting for transfers between devices: 0.01 us -> 118 us  [the longest x1 74.8 us: on_device(): mine = lax.psum_scatter(packed, 'mp', scatter_dimension=0, tiled=True)[0]]
    pallas_call x0 -> x3, Pallas kernels: none -> 114 us  [call(): pl.pallas_call(kernel, name=name, out_shape=[jax.ShapeDtypeStruct(*outs[n...]
    psum x4 -> x2, waiting for transfers between devices: 248 us -> 199 us  [the longest x1 104 us: on_device(): mine = lax.psum(mine, ('dp', 'seq')).astype(F32)]
    reduce_sum x12 -> x0, other arithmetic: 35.7 us -> none  [the longest x1 14 us: on_device(): row_total = jnp.sum(expanded, axis=-1, keepdims=True)]
    convert_element_type x13 -> x2, other arithmetic: 28.3 us -> 0.03 us  [the longest x1 0.03 us: on_device(): bg = cot * mask.astype(BF)[:, None]]
    unnamed x158 -> x48, local copies, waits for them, and re-layouts: 32.1 us -> 5.12 us
  transfers between devices with their start and end apart: 14 -> 12, of which waited for: 6 -> 10; matrix products, arithmetic and copies ran while one was open for 17% -> 4% of each run, Pallas kernels for 0% -> 2%
where the time goes in v1:
time: 698 us
  waiting for transfers between devices  449 us (64%)
  Pallas kernels  114 us (16%)
  blocking collectives  64.2 us (9%)
  local copies, waits for them, and re-layouts  31.8 us (5%)
  other arithmetic  20.3 us (3%)
  between operations  14.7 us (2%)
    pallas_call x3, Pallas kernels, call(): pl.pallas_call(kernel, name=name, out_shape=[jax.ShapeDtypeStruct(*outs[n...  114 us
    psum x1, waiting for transfers between devices, on_device(): mine = lax.psum(mine, ('dp', 'seq')).astype(F32)  104 us
    psum x1, waiting for transfers between devices, on_device(): conv = lax.psum(conv, ('dp', 'seq', 'mp')).astype(F32)  94.6 us
    reduce_scatter x1, waiting for transfers between devices, on_device(): mine = lax.psum_scatter(packed, 'mp', scatter_dimension=0, tiled=True)[0]  74.8 us
    reduce_scatter x1, waiting for transfers between devices, on_device(): lax.psum_scatter(b['dkvs'], ('seq', 'mp'), scatter_dimension=0, tiled=True)  43.6 us
    psum x1, blocking collectives, on_device(): small = lax.psum(b['small'] + e['small'], ('dp', 'seq', 'mp'))  39.8 us
    all_gather x2, waiting for transfers between devices, ordered(): both = lax.all_gather(value, 'mp', axis=0)  39.3 us
    all_gather x1, waiting for transfers between devices, on_device(): kvs = lax.all_gather(a['kv'], ('seq', 'mp'), axis=0)  36.5 us
  transfers between devices with their start and end apart: 12, of which 10 were waited for; matrix products, arithmetic and copies ran while one was open for 4% of the time, Pallas kernels for 2%

profile of v1, /device:TPU:0, one launch (start us, length us, event | category | flops | bytes accessed | tf_op | source)
XLA Modules:
  0.0 697.9 jit_solution(5298819483831985595)
XLA Ops:
  8.0 1.5 copy.53
  11.8 2.3 collective-permute-start
  15.5 4.6 all_gather.40
  20.3 4.2 all_gather.39
  25.3 1.9 multiply_sine_fusion
  32.4 7.2 %all-gather.15.cloned.1.call-done = bf16[6,512,256]{2,1,0:T(8,128)(2,1)} async-done(((bf16[3,512,256]{2,1,0:T(8,128)(2,1)}), bf16[6,512,256]{2,1,0:T(8,128)(2,1)}) %all-gather.15.cloned.1.call-update) | async-done | bytes 1572880 | tf_op jit(solution)/shard_map/all_gather | solution.py:529
  39.5 12.9 %stem.1 = (bf16[512,512]{1,0:T(8,128)(2,1)}, bf16[512,512]{1,0:T(8,128)(2,1)}, bf16[512,512]{1,0:T(8,128)(2,1)}, f32[512,512]{1,0:T(8,128)}, f32[512,512]{1,0:T(...) custom-call(bf16[512,256]{1,0:T(8,128)(2,1)} %get-tuple-element.109., ...), custom_call_target="tpu_custom_call" | custom-call | tf_op jit(solution)/shard_map/stem/pallas_call | solution.py:378
  52.5 15.5 %all_gather.45.refs_3_ = bf16[512,512]{1,0:T(8,128)(2,1)} all-gather(bf16[256,512]{1,0:T(8,128)(2,1)S(1)} %copy-done.7), channel_id=1, replica_groups=mesh['dp'=8,'seq'=2,'mp'=2] {'mp'}, dimensions={0}, use_global_device_ids=true | all-gather | bytes 786432 | tf_op jit(solution)/shard_map/all_gather | solution.py:530
  69.0 11.4 %all-gather.11.cloned.1.call-done.refs_4_ = bf16[4,512,512]{2,1,0:T(8,128)(2,1)} async-done(((bf16[2,512,512]{2,1,0:T(8,128)(2,1)}), bf16[4,512,512]{2,1,0:T(8,128)(2,1)}) %all-gather.11.cloned.1.call-update) | async-done | bytes 2097168 | tf_op jit(solution)/shard_map/all_gather | solution.py:531
  80.4 34.7 %all-gather.13.cloned.1.call-done.refs_5_ = bf16[4,512,512]{2,1,0:T(8,128)(2,1)} async-done(((bf16[2,512,512]{2,1,0:T(8,128)(2,1)}), bf16[4,512,512]{2,1,0:T(8,128)(2,1)}) %all-gather.13.cloned.1.call-update) | async-done | bytes 2097168 | tf_op jit(solution)/shard_map/all_gather | solution.py:534
  115.2 36.5 %all-gather.17.cloned.1.call-done = bf16[8,512,512]{2,1,0:T(8,128)(2,1)} async-done(((bf16[2,512,512]{2,1,0:T(8,128)(2,1)}), bf16[8,512,512]{2,1,0:T(8,128)(2,1)}) %all-gather.17.cloned.1.call-update) | async-done | bytes 4194320 | tf_op jit(solution)/shard_map/all_gather | solution.py:557
  151.7 79.3 %middle.1 = (bf16[512,512]{1,0:T(8,128)(2,1)}, bf16[4,512,512]{2,1,0:T(8,128)(2,1)}, bf16[4,512,512]{2,1,0:T(8,128)(2,1)}, bf16[512,512]{1,0:T(8,128)(2,1)}, f32...) custom-call(bf16[4,2,512,512]{3,2,1,0:T(8,128)(2,1)} %bitcast.53, ...), custom_call_target="tpu_custom_call" | custom-call | tf_op jit(solution)/shard_map/middle/pallas_call | solution.py:378
  232.0 43.6 %reduce-scatter.3.cloned.1.call-done = bf16[1,2,512,512]{3,2,1,0:T(8,128)(2,1)} async-done(((bf16[4,2,512,512]{3,2,1,0:T(8,128)(2,1)}), bf16[1,2,512,512]{3,2,1,0:T(8,128)(2,1)}) %reduce-scatter.3.cloned.1.call-update) | async-done | bytes 1048592 | tf_op jit(solution)/shard_map/reduce_scatter | solution.py:573
  275.7 2.3 slice_bitcast_fusion.1
  278.0 21.4 %back.1 = (bf16[2,3,256,512]{3,2,1,0:T(8,128)(2,1)}, bf16[3,512,512]{2,1,0:T(8,128)(2,1)}, bf16[256,512]{1,0:T(8,128)(2,1)}, f32[16,512]{1,0:T(8,128)}, f32[512,256]{1,0:T(8,128)}) custom-call(bf16[512,512]{1,0:T(8,128)(2,1)} %get-tuple-element.45.refs_0_, bf16[512,512]{1,0:T(8,128)(2,1)} %get-tuple-element.103.refs_1_, ...), custom_call_target="tpu_custom_call" | custom-call | tf_op jit(solution)/shard_map/back/pallas_call | solution.py:378
  299.4 8.7 %pad_maximum_fusion = bf16[2,3072,512]{2,1,0:T(8,128)(2,1)} fusion(bf16[2,768,512]{2,1,0:T(8,128)(2,1)} %bitcast.61, bf16[2,256,512]{2,1,0:T(8,128)(2,1)S(1)} %bitcast.68, bf16[2,1024,512]{2,1,0:T(8,128)(2,1)} %bitcast.59, bf16[2,1024,512]{2,1,0:T(8,128)(2,1)S(1)} %bitcast.58), kind=kLoop, calls=%fused_computation | loop fusion | flops 25165824 | bytes 12582912 | tf_op jit(solution)/shard_map/concatenate | solution.py:595
  309.5 1.3 pad_maximum_fusion.1
  311.7 74.8 %reduce-scatter.5.cloned.1.call-done = bf16[1,3072,512]{2,1,0:T(8,128)(2,1)} async-done(((bf16[2,3072,512]{2,1,0:T(8,128)(2,1)}), bf16[1,3072,512]{2,1,0:T(8,128)(2,1)}) %reduce-scatter.5.cloned.1.call-update) | async-done | bytes 3145744 | tf_op jit(solution)/shard_map/reduce_scatter | solution.py:604
  386.5 22.9 %all-gather.19.cloned.1.call-done = bf16[1024,512]{1,0:T(8,128)(2,1)} async-done(((bf16[512,512]{1,0:T(8,128)(2,1)}), bf16[1024,512]{1,0:T(8,128)(2,1)}) %all-gather.19.cloned.1.call-update) | async-done | bytes 1048592 | tf_op jit(solution)/shard_map/all_gather | solution.py:622
  409.4 2.9 reverse_select_fusion.1
  412.2 39.8 %psum.22 = f32[16,512]{1,0:T(8,128)S(1)} all-reduce(f32[16,512]{1,0:T(8,128)S(1)} %add.58), channel_id=1, replica_groups=mesh['dp'=8,'seq'=2,'mp'=2] {'dp','seq','mp'}, use_global_device_ids=true, to_apply=%region_2.3 | all-reduce | flops 8192 | bytes 65536 | tf_op jit(solution)/shard_map/psum | solution.py:608
  453.9 94.6 %all-reduce.10.cloned.1.call-done = bf16[1792,512]{1,0:T(8,128)(2,1)} async-done(((bf16[1792,512]{1,0:T(8,128)(2,1)}), bf16[1792,512]{1,0:T(8,128)(2,1)}) %all-reduce.10.cloned.1.call-update) | async-done | bytes 1835024 | tf_op jit(solution)/shard_map/psum | solution.py:607
  548.5 3.5 slice.137
  552.0 1.8 slice.135
  553.8 16.4 %all-gather.21.cloned.1.call-done = f32[1024,256]{1,0:T(8,128)} async-done(((f32[512,256]{1,0:T(8,128)}), f32[1024,256]{1,0:T(8,128)}) %all-gather.21.cloned.1.call-update) | async-done | bytes 1048592 | tf_op jit(solution)/shard_map/all_gather | solution.py:622
  570.2 1.7 reverse_select_fusion
  573.2 104.0 %all-reduce.12.cloned.1.call-done = bf16[3072,512]{1,0:T(8,128)(2,1)} async-done(((bf16[3072,512]{1,0:T(8,128)(2,1)}), bf16[3072,512]{1,0:T(8,128)(2,1)}) %all-reduce.12.cloned.1.call-update) | async-done | bytes 3145744 | tf_op jit(solution)/shard_map/psum | solution.py:605
  677.2 3.2 fusion.12
  680.4 1.5 copy.58
  683.1 1.4 slice.141
  684.4 3.1 reshape.123
  687.5 2.7 copy.55
  (113 shorter events, 19.6 us)
Async XLA Ops:
  7.2 32.3 %all-gather.15.cloned.1.call-start = ((), (), s32[]{:S(2)}) async-start(), calls=%async_computation.8 | async-start | bytes 2359296 | tf_op jit(solution)/shard_map/all_gather | solution.py:529
  7.9 72.5 %all-gather.11.cloned.1.call-start = ((), (), s32[]{:S(2)}) async-start(), calls=%async_computation.2 | async-start | bytes 3145728 | tf_op jit(solution)/shard_map/all_gather | solution.py:531
  9.5 2.3 copy-start.5
  9.5 6.0 copy-start.11
  9.5 10.7 %copy-start.12 = (bf16[512]{0:T(512)(128)(2,1)S(1)}, bf16[512]{0:T(512)(128)(2,1)}, u32[]{:S(2)}) copy-start(bf16[512]{0:T(512)(128)(2,1)} %param.21) | copy-start | bytes 3076
  9.5 10.7 %copy-start.13 = (bf16[512]{0:T(512)(128)(2,1)S(1)}, bf16[512]{0:T(512)(128)(2,1)}, u32[]{:S(2)}) copy-start(bf16[512]{0:T(512)(128)(2,1)} %param.23) | copy-start | bytes 3076
  9.5 10.7 %copy-start.14 = (bf16[512]{0:T(512)(128)(2,1)S(1)}, bf16[512]{0:T(512)(128)(2,1)}, u32[]{:S(2)}) copy-start(bf16[512]{0:T(512)(128)(2,1)} %param.24) | copy-start | bytes 3076
  9.5 10.7 %copy-start.15 = (bf16[512]{0:T(512)(128)(2,1)S(1)}, bf16[512]{0:T(512)(128)(2,1)}, u32[]{:S(2)}) copy-start(bf16[512]{0:T(512)(128)(2,1)} %param.25) | copy-start | bytes 3076
  9.5 10.7 %copy-start.16 = (bf16[512]{0:T(512)(128)(2,1)S(1)}, bf16[512]{0:T(512)(128)(2,1)}, u32[]{:S(2)}) copy-start(bf16[512]{0:T(512)(128)(2,1)} %param.29) | copy-start | bytes 3076
  9.6 10.7 %copy-start.17 = (bf16[512]{0:T(512)(128)(2,1)S(1)}, bf16[512]{0:T(512)(128)(2,1)}, u32[]{:S(2)}) copy-start(bf16[512]{0:T(512)(128)(2,1)} %param.30) | copy-start | bytes 3076
  9.6 10.7 %copy-start.18 = (bf16[512]{0:T(512)(128)(2,1)S(1)}, bf16[512]{0:T(512)(128)(2,1)}, u32[]{:S(2)}) copy-start(bf16[512]{0:T(512)(128)(2,1)} %param.31) | copy-start | bytes 3076
  9.6 10.7 %copy-start.19 = (bf16[512]{0:T(512)(128)(2,1)S(1)}, bf16[512]{0:T(512)(128)(2,1)}, u32[]{:S(2)}) copy-start(bf16[512]{0:T(512)(128)(2,1)} %param.35) | copy-start | bytes 3076
  9.6 10.7 %copy-start.20 = (bf16[2,256]{1,0:T(2,128)(2,1)S(1)}, bf16[2,256]{1,0:T(2,128)(2,1)}, u32[]{:S(2)}) copy-start(bf16[2,256]{1,0:T(2,128)(2,1)} %param.27) | copy-start | bytes 3076
  11.0 104.2 %all-gather.13.cloned.1.call-start = ((), (), s32[]{:S(2)}) async-start(), calls=%async_computation.3 | async-start | bytes 3145728 | tf_op jit(solution)/shard_map/all_gather | solution.py:534
  11.0 17.3 %copy-start.3 = (bf16[3,80,512]{2,1,0:T(8,128)(2,1)S(1)}, bf16[3,80,512]{2,1,0:T(8,128)(2,1)}, u32[]{:S(2)}) copy-start(bf16[3,80,512]{2,1,0:T(8,128)(2,1)} %param.20) | copy-start | bytes 737284
  11.7 140.0 %all-gather.17.cloned.1.call-start = ((), (), s32[]{:S(2)}) async-start(), calls=%async_computation.9 | async-start | bytes 5242880 | tf_op jit(solution)/shard_map/all_gather | solution.py:557
  11.8 17.2 %collective-permute-start = (bf16[80,2]{1,0:T(8,128)(2,1)S(1)}, bf16[80,2]{1,0:T(8,128)(2,1)S(1)}, u32[]{:S(2)}, u32[]{:S(2)}) collective-permute-start(bf16[80,2]{1,0:T(8,128)(2,1)S(1)} %get-tuple-element.105), channel_id=1, source_target_pairs={{0,2},{1,3},{4,6},{5,7},{8,10},{9,11},{12,14},{13,15},{16,18},{17,... | collective-permute-start | bytes 968 | tf_op jit(solution)/shard_map/ppermute | solution.py:511
  14.2 14.8 %collective-permute-start.1 = (bf16[80,2]{1,0:T(8,128)(2,1)S(1)}, bf16[80,2]{1,0:T(8,128)(2,1)S(1)}, u32[]{:S(2)}, u32[]{:S(2)}) collective-permute-start(bf16[80,2]{1,0:T(8,128)(2,1)S(1)} %get-tuple-element.104), channel_id=1, source_target_pairs={{2,0},{3,1},{6,4},{7,5},{10,8},{11,9},{14,12},{15,13},{18,16},{19,... | collective-permute-start | bytes 968 | tf_op jit(solution)/shard_map/ppermute | solution.py:512
  39.5 13.0 %copy-start.21 = (s32[1,1024]{1,0:T(1,128)S(1)}, s32[1,1024]{1,0:T(1,128)}, u32[]{:S(2)}) copy-start(s32[1,1024]{1,0:T(1,128)} %param.37) | copy-start | bytes 12292
  39.5 13.0 %copy-start.7 = (bf16[256,512]{1,0:T(8,128)(2,1)S(1)}, bf16[256,512]{1,0:T(8,128)(2,1)}, u32[]{:S(2)}) copy-start(bf16[256,512]{1,0:T(8,128)(2,1)} %param.28) | copy-start | bytes 786436
  52.4 15.6 %copy-start.8 = (bf16[1,1024,512]{2,1,0:T(8,128)(2,1)S(1)}, bf16[1,1024,512]{2,1,0:T(8,128)(2,1)}, u32[]{:S(2)}) copy-start(bf16[1,1024,512]{2,1,0:T(8,128)(2,1)} %param.36) | copy-start | bytes 3145732
  52.4 223.2 %reduce-scatter.3.cloned.1.call-start = ((), (), s32[]{:S(2)}) async-start(), calls=%async_computation.4 | async-start | bytes 5242880 | tf_op jit(solution)/shard_map/reduce_scatter | solution.py:573
  231.0 155.5 %reduce-scatter.5.cloned.1.call-start = ((), (), s32[]{:S(2)}) async-start(), calls=%async_computation.6 | async-start | bytes 9437184 | tf_op jit(solution)/shard_map/reduce_scatter | solution.py:604
  277.9 21.5 %copy-start.1 = (bf16[4,512,512]{2,1,0:T(8,128)(2,1)S(1)}, bf16[4,512,512]{2,1,0:T(8,128)(2,1)}, u32[]{:S(2)}) copy-start(bf16[4,512,512]{2,1,0:T(8,128)(2,1)} %get-tuple-element.60) | copy-start | bytes 6291460
  278.0 21.5 %copy-start.4 = (bf16[512,512]{1,0:T(8,128)(2,1)S(1)}, bf16[512,512]{1,0:T(8,128)(2,1)}, u32[]{:S(2)}) copy-start(bf16[512,512]{1,0:T(8,128)(2,1)} %get-tuple-element.62) | copy-start | bytes 1572868
  308.1 101.3 %all-gather.19.cloned.1.call-start = ((), (), s32[]{:S(2)}) async-start(), calls=%async_computation.10 | async-start | bytes 1572864 | tf_op jit(solution)/shard_map/all_gather | solution.py:622
  308.9 239.6 %all-reduce.10.cloned.1.call-start = ((), (), s32[]{:S(2)}) async-start(), calls=%async_computation.5 | async-start | bytes 3670016 | tf_op jit(solution)/shard_map/psum | solution.py:607
  310.9 259.3 %all-gather.21.cloned.1.call-start = ((), (), s32[]{:S(2)}) async-start(), calls=%async_computation.11 | async-start | bytes 1572864 | tf_op jit(solution)/shard_map/all_gather | solution.py:622
  311.6 365.6 %all-reduce.12.cloned.1.call-start = ((), (), s32[]{:S(2)}) async-start(), calls=%async_computation.7 | async-start | bytes 6291456 | tf_op jit(solution)/shard_map/psum | solution.py:605
  386.5 25.8 %copy-start.9 = (f32[16,512]{1,0:T(8,128)S(1)}, f32[16,512]{1,0:T(8,128)}, u32[]{:S(2)}) copy-start(f32[16,512]{1,0:T(8,128)} %get-tuple-element.58) | copy-start | bytes 98308
  386.5 25.8 %copy-start.10 = (f32[16,512]{1,0:T(8,128)S(1)}, f32[16,512]{1,0:T(8,128)}, u32[]{:S(2)}) copy-start(f32[16,512]{1,0:T(8,128)} %get-tuple-element.59) | copy-start | bytes 98308
  680.4 2.6 copy-start
  (2 other events, 2.8 us)
Sparse Core Ops, SparseCore 0:
  9.6 29.9 all-gather.14
  41.6 38.7 all-gather.10
  82.0 33.1 all-gather.12
  117.2 34.4 all-gather.16
  231.1 44.5 reduce-scatter.2
  308.2 78.1 reduce-scatter.4
  388.0 21.3 all-gather.18
  415.3 133.1 all-reduce.9
  550.0 20.1 all-gather.20
  573.6 103.5 all-reduce.11

commit v2 on v1

v2 whole, which is shorter than its diff:
```python
import functools
import math

import jax
import jax.numpy as jnp
from jax import lax
from jax.experimental import pallas as pl
from jax.experimental.pallas import tpu as pltpu
from jax.sharding import PartitionSpec as P

HEAD = 64
BF = jnp.bfloat16
F32 = jnp.float32
MESH = pl.DeviceIdType.MESH
VMEM_LIMIT = 60 * 1024 * 1024
C1B, C2B, N1G, N1B, OUB, N2G, N2B, DNB, QB, VB, UPB = range(11)


class Box:
    pass


def dot(a, b, ca, cb):
    return lax.dot_general(a, b, (((ca,), (cb,)), ((), ())), preferred_element_type=F32)


def nn(a, b):
    return dot(a, b, 1, 0)


def nt(a, b):
    return dot(a, b, 1, 1)


def tn(a, b):
    return dot(a, b, 0, 0)


def rows_loop(total, step, body, unroll=1):
    step = min(step, total)

    def one(i, carry):
        body(pl.ds(pl.multiple_of(i * step, step), step))
        return carry

    lax.fori_loop(0, total // step, one, 0, unroll=unroll)


def gelu_parts(v):
    t = 1.0 / (1.0 + (0.3275911 / math.sqrt(2.0)) * jnp.abs(v))
    e = jnp.exp(-0.5 * v * v)
    poly = 1.061405429 * t - 1.453152027
    poly = poly * t + 1.421413741
    poly = poly * t - 0.284496736
    poly = poly * t + 0.254829592
    tail = (0.5 * t) * poly * e
    return jnp.where(v >= 0, 1.0 - tail, tail), e * (1.0 / math.sqrt(2.0 * math.pi))


def gelu_both(v):
    cdf, pdf = gelu_parts(v)
    return v * cdf, cdf + v * pdf


def normal(x):
    center = x - jnp.mean(x, axis=-1, keepdims=True)
    spread = jnp.mean(center * center, axis=-1, keepdims=True)
    inv = lax.rsqrt(spread + 1e-05)
    return center * inv, inv


def normal_pull(gy, hat, inv):
    return inv * (
        gy
        - jnp.mean(gy, axis=-1, keepdims=True)
        - hat * jnp.mean(gy * hat, axis=-1, keepdims=True)
    )


def vec(r, i):
    return r.vecs[i : i + 1, :]


def add_small(r, i, value):
    r.small[i : i + 1, :] += value


def col(value):
    return jnp.sum(value, axis=0, keepdims=True)


def stage_stem(r):
    T, D = r.stream.shape
    c = lax.axis_index("seq")
    m = lax.axis_index("mp")
    w1 = r.w1[...]
    first = jnp.logical_and(c == 0, m == 0)
    edge = nn(r.xh[...], w1) + vec(r, C1B)
    edge = gelu_both(edge)[0] * jnp.where(first, 0.0, 1.0)
    r.odd[0:8, :] = edge[0:8, :]
    r.tmp[...] = nn(r.xe[...], w1)

    def even(rows):
        value, slope = gelu_both(r.tmp[rows, :] + vec(r, C1B))
        r.he[rows, :] = value.astype(BF)
        r.dge[rows, :] = slope

    rows_loop(T, 32, even)
    r.tmp[...] = nn(r.xo[...], w1)

    def odd(rows):
        value, slope = gelu_both(r.tmp[rows, :] + vec(r, C1B))
        r.ho[rows, :] = value.astype(BF)
        r.odd[pl.ds(pl.multiple_of(rows.start + 8, 8), rows.size), :] = value
        r.dgo[rows, :] = slope

    rows_loop(T, 32, odd)
    r.hp[...] = r.odd[7 : 7 + T, :].astype(BF)
    r.tmp[...] = nn(r.hp[...], r.w2[0]) + nn(r.he[...], r.w2[1]) + nn(r.ho[...], r.w2[2])

    def second(rows):
        value, slope = gelu_both(r.tmp[rows, :] + vec(r, C2B))
        stream = value + r.stream[rows, :]
        r.dg2[rows, :] = slope
        r.stream[rows, :] = stream
        r.normed[rows, :] = (normal(stream)[0] * vec(r, N1G) + vec(r, N1B)).astype(BF)

    rows_loop(T, 32, second)


def stage_qkv(r, parts):
    T, D = r.stream.shape
    half = D // 2
    normed = r.normed[...]
    for part in parts:
        bias, scale = ((QB, HEAD**-0.5), (None, 1.0), (VB, 1.0))[part]
        for m in range(2):
            value = nn(normed, r.wqkv[m, part])
            if bias is not None:
                value = value + r.vecs[bias : bias + 1, m * half : (m + 1) * half]
            value = (value.astype(BF).astype(F32) * scale).T.astype(BF)
            if part == 0:
                r.qt[m * half : (m + 1) * half, :] = value
            else:
                at = (part - 1) * D + m * half
                r.kv[at : at + half, :] = value


def head_rows(h):
    return pl.ds(pl.multiple_of(h * HEAD, HEAD), HEAD)


def block_rows(r, slot, part, h):
    D = r.qt.shape[0]
    return pl.ds(pl.multiple_of((2 * slot + part) * D + h * HEAD, HEAD), HEAD)


def attend_block(r, slot):
    D, T = r.qt.shape
    first = slot == 0

    def one(h, carry):
        rows = head_rows(h)
        s = tn(r.kv[block_rows(r, slot, 0, h), :], r.qt[rows, :])
        top = jnp.max(s, axis=0, keepdims=True)
        if not first:
            top = jnp.maximum(top, r.top[h])
        p = jnp.exp(s - top)
        total = jnp.sum(p, axis=0, keepdims=True)
        mixed = nn(r.kv[block_rows(r, slot, 1, h), :], p.astype(BF))
        if not first:
            keep = jnp.exp(r.top[h] - top)
            total = total + keep * r.total[h]
            mixed = mixed + keep * r.mixt[rows, :]
        r.top[h] = top
        r.total[h] = total
        r.mixt[rows, :] = mixed
        return carry

    lax.fori_loop(0, D // HEAD, one, 0)


def attend_end(r):
    D, T = r.qt.shape

    def one(h, carry):
        rows = head_rows(h)
        total = r.total[h]
        value = r.mixt[rows, :] * (1.0 / total)
        r.mixt[rows, :] = value
        r.mixb[rows, :] = value.astype(BF)
        r.top[h] = r.top[h] + jnp.log(total)
        return carry

    lax.fori_loop(0, D // HEAD, one, 0)


def stage_mid(r):
    T, D = r.stream.shape
    r.tmp[...] = tn(r.mixb[...], r.wo[...])

    def one(rows):
        mid = r.stream[rows, :] + r.tmp[rows, :] + vec(r, OUB)
        r.mid[rows, :] = mid
        r.ntwo[rows, :] = (normal(mid)[0] * vec(r, N2G) + vec(r, N2B)).astype(BF)

    rows_loop(T, 32, one)


def stage_ff(r):
    T, D = r.stream.shape
    side = r.up.shape[2] // D
    parts, width = 2 * side, D
    add_small(r, DNB, col(r.bg[...].astype(F32)))

    def chunk(j, carry):
        into, at = j // side, j % side
        up = r.up[into, :, pl.ds(pl.multiple_of(at * D, D), D)]
        down = r.down[pl.ds(pl.multiple_of(j * D, D), D), :]
        r.tmp[...] = nn(r.ntwo[...], up)
        r.tmp2[...] = nt(r.bg[...], down)
        bias = r.vecs[pl.ds(UPB + j, 1), :]

        def one(i, acc):
            rows = pl.ds(pl.multiple_of(i * 32, 32), 32)
            value, slope = gelu_both(r.tmp[rows, :] + bias)
            r.act[rows, :] = value.astype(BF)
            grad = (r.tmp2[rows, :] * slope).astype(BF)
            r.ing[rows, :] = grad
            return acc + col(grad.astype(F32))

        r.small[pl.ds(UPB + j, 1), :] = lax.fori_loop(0, T // 32, one, jnp.zeros((1, width), F32))
        act = r.act[...]
        ing = r.ing[...]
        out = nn(act, down)
        back = nt(ing, up)

        @pl.when(j == 0)
        def _():
            r.ffo[...] = out
            r.ntg[...] = back

        @pl.when(j > 0)
        def _():
            r.ffo[...] += out
            r.ntg[...] += back

        r.g_down[pl.ds(pl.multiple_of(j * D, D), D), :] = tn(act, r.bg[...]).astype(BF)
        base = into * (r.g_up.shape[0] // 2) + at * D
        r.g_up[pl.ds(pl.multiple_of(base, 16), D), :] = tn(r.ntwo[...], ing).astype(BF)
        return carry

    lax.fori_loop(0, parts, chunk, 0)


def stage_mid_pull(r):
    T, D = r.stream.shape

    def one(i, accs):
        rows = pl.ds(pl.multiple_of(i * 32, 32), 32)
        mid = r.mid[rows, :]
        r.enc[rows, :] = (mid + r.ffo[rows, :] + vec(r, DNB)).astype(BF)
        hat, inv = normal(mid)
        grad = r.ntg[rows, :]
        smg = r.bg[rows, :].astype(F32) + normal_pull(grad * vec(r, N2G), hat, inv)
        r.smg[rows, :] = smg
        attg = smg.astype(BF)
        r.attg[rows, :] = attg
        return accs[0] + col(grad * hat), accs[1] + col(grad), accs[2] + col(attg.astype(F32))

    zero = jnp.zeros((1, D), F32)
    gain, bias, out_bias = lax.fori_loop(0, T // 32, one, (zero, zero, zero))
    add_small(r, N2G, gain)
    add_small(r, N2B, bias)
    add_small(r, OUB, out_bias)
    attg = r.attg[...]
    r.dot[...] = nt(r.wo[...], attg).astype(BF)
    gout = nn(r.mixb[...], attg).astype(BF)
    rows, half = r.g_up.shape[0] // 2, D // 2
    r.g_up[rows - half : rows, :] = gout[0:half, :]
    r.g_up[2 * rows - half : 2 * rows, :] = gout[half:D, :]

    def head(h, carry):
        rows = head_rows(h)
        r.diag[h] = jnp.sum(r.dot[rows, :].astype(F32) * r.mixt[rows, :], axis=0, keepdims=True)
        return carry

    lax.fori_loop(0, D // HEAD, head, 0)


def pull_block(r, slot, dkv, hook):
    D, T = r.qt.shape
    first = slot == 3
    H = D // HEAD

    def one(h, carry):
        rows = head_rows(h)
        k, v = r.kv[block_rows(r, slot, 0, h), :], r.kv[block_rows(r, slot, 1, h), :]
        q, do = r.qt[rows, :], r.dot[rows, :]
        p = jnp.exp(tn(k, q) - r.top[h])
        ds = (p * (tn(v, do) - r.diag[h])).astype(BF)
        dkv[1, rows, :] = nt(do, p.astype(BF)).astype(dkv.dtype)
        dkv[0, rows, :] = nt(q, ds).astype(dkv.dtype)
        dq = nn(k, ds)
        if first:
            r.dqt[rows, :] = dq
        else:
            r.dqt[rows, :] += dq
        return carry

    for part in range(2):
        lax.fori_loop(part * H // 2, (part + 1) * H // 2, one, 0)
        hook()


def stage_qkv_weights(r):
    T, D = r.stream.shape
    half = D // 2
    normedt = r.normed[...].astype(F32).T.astype(BF)
    ones = jnp.ones((8, T), BF)
    for part, ref in enumerate((r.dqb, r.dkb, r.dvb)):
        if part != 1:
            add_small(r, QB if part == 0 else VB, nt(ones, ref[...])[0:1, :])
        for m in range(2):
            grad = nt(normedt, ref[m * half : (m + 1) * half, :]).astype(BF)
            at = (3 * m + part) * half
            r.g_qkv[at : at + half, 0:half] = grad[0:half, :]
            r.g_qkv[at : at + half, half:D] = grad[half:D, :]


def stage_qkv_pull(r):
    T, D = r.stream.shape
    half = D // 2
    total = None
    for part, ref in enumerate((r.dqb, r.dkb, r.dvb)):
        for m in range(2):
            back = nn(r.wqkv[m, part], ref[m * half : (m + 1) * half, :])
            total = back if total is None else total + back
    r.tmp[...] = total.T

    def one(i, accs):
        rows = pl.ds(pl.multiple_of(i * 32, 32), 32)
        hat, inv = normal(r.stream[rows, :])
        grad = r.tmp[rows, :]
        back = r.smg[rows, :] + normal_pull(grad * vec(r, N1G), hat, inv)
        sg = (back * r.dg2[rows, :]).astype(BF)
        r.sg[rows, :] = sg
        return accs[0] + col(grad * hat), accs[1] + col(grad), accs[2] + col(sg.astype(F32))

    zero = jnp.zeros((1, D), F32)
    gain, bias, c2b = lax.fori_loop(0, T // 32, one, (zero, zero, zero))
    add_small(r, N1G, gain)
    add_small(r, N1B, bias)
    add_small(r, C2B, c2b)


def stage_conv2_pull(r, next_row):
    T, D = r.stream.shape
    sg = r.sg[...]
    r.shift[0:T, :] = nt(sg, r.w2[0])
    r.shift[T : T + 16, :] = nt(next_row, r.w2[0])
    r.tmp[...] = nt(sg, r.w2[1])
    r.tmp2[...] = nt(sg, r.w2[2]) + r.shift[1 : T + 1, :]

    def one(i, acc):
        rows = pl.ds(pl.multiple_of(i * 32, 32), 32)
        even = (r.tmp[rows, :] * r.dge[rows, :]).astype(BF)
        odd = (r.tmp2[rows, :] * r.dgo[rows, :]).astype(BF)
        r.fe[rows, :] = even
        r.fo[rows, :] = odd
        return acc + col(even.astype(F32)) + col(odd.astype(F32))

    add_small(r, C1B, lax.fori_loop(0, T // 32, one, jnp.zeros((1, D), F32)))


def stage_conv2_weights(r):
    D = r.stream.shape[1]
    sg = r.sg[...]
    for i, tap in enumerate((r.hp, r.he, r.ho)):
        r.g_c2[i * D : (i + 1) * D, :] = tn(tap[...], sg).astype(BF)


def stage_conv1_weights(r):
    r.g_c1[...] = (tn(r.xe[...], r.fe[...]) + tn(r.xo[...], r.fo[...])).astype(BF)


def stage_mel(r, next_row, prev_row):
    T, D = r.stream.shape
    fe, fo = r.fe[...], r.fo[...]
    r.wide[16 : 16 + T, :] = nt(fo, r.w1p[2])
    r.wide[0:16, :] = nt(prev_row, r.w1p[2])
    r.melg[:, 0:128] = nt(fe, r.w1p[1]) + nt(fo, r.w1p[0]) + r.wide[15 : 15 + T, :]
    r.wide[0:T, :] = nt(fe, r.w1p[0])
    r.wide[T : T + 16, :] = nt(next_row, r.w1p[0])
    r.melg[:, 128:256] = nt(fe, r.w1p[2]) + nt(fo, r.w1p[1]) + r.wide[1 : 1 + T, :]


class Net:
    def __init__(self, r, bits):
        self.r, self.bits, self.used, self.used_here = r, bits, 0, 0
        self.d, self.c, self.m = (lax.axis_index(n) for n in ("dp", "seq", "mp"))

    def bit(self, dim):
        if dim == "c":
            return self.c
        if dim == "y":
            return self.m
        return (self.d // (1 << dim)) % 2

    def peer(self, dim):
        if dim == "c":
            return (self.d, 1 - self.c, self.m)
        if dim == "y":
            return (self.d, self.c, 1 - self.m)
        step = 1 << dim
        return (self.d + step - 2 * step * self.bit(dim), self.c, self.m)

    def greet(self):
        barrier = pltpu.get_barrier_semaphore()
        dims = ["c", "y"] + list(range(self.bits))
        for dim in dims:
            pl.semaphore_signal(barrier, inc=1, device_id=self.peer(dim), device_id_type=MESH)
        pl.semaphore_wait(barrier, len(dims))

    def send(self, src, dst, dim):
        i = self.used
        self.used += 1
        copy = pltpu.make_async_remote_copy(
            src_ref=src,
            dst_ref=dst,
            send_sem=self.r.send.at[i],
            recv_sem=self.r.recv.at[i],
            device_id=self.peer(dim),
            device_id_type=MESH,
        )
        copy.start()
        return copy

    def here(self, src, dst):
        i = self.used_here
        self.used_here += 1
        copy = pltpu.make_async_copy(src, dst, self.r.own.at[i])
        copy.start()
        return copy


def wait_all(copies):
    for copy in copies:
        copy.wait()


def rows16(start, size):
    return pl.ds(pl.multiple_of(start, 16), size)


def sum_plan(rows, halves, order):
    steps, need = [], 0
    for dim in order:
        if dim == "y" and halves == 2:
            steps.append((dim, "other", rows))
            halves = 1
        elif rows % 32 == 0:
            rows //= 2
            steps.append((dim, "halve", rows))
        else:
            steps.append((dim, "swap", rows))
        need += rows * halves
    return steps, need


def bucket_sum(net, g, got, done, halves, order):
    R = g.shape[0] // halves
    lo, rows, at, bases = 0, R, 0, [h * R for h in range(halves)]
    back = []
    for dim, kind, n in sum_plan(R, halves, order)[0]:
        b = net.bit(dim)
        keep = give = lo
        givers = bases
        if kind == "halve":
            keep, give = lo + b * n, lo + (1 - b) * n
            back.append((dim, n, lo))
        if kind == "other":
            givers, bases = [(1 - b) * R], [b * R]
        copies = [
            net.send(g.at[rows16(base + give, n)], got.at[rows16(at + i * n, n)], dim)
            for i, base in enumerate(givers)
        ]
        yield
        wait_all(copies)
        step = 32 if n % 32 == 0 else 16
        for i, base in enumerate(bases):

            def add(k, carry, base=base, keep=keep, at=at, i=i, n=n):
                mine = rows16(base + keep + k * step, step)
                value = g[mine, :].astype(F32) + got[rows16(at + i * n + k * step, step), :].astype(F32)
                g[mine, :] = value.astype(BF)
                return carry

            lax.fori_loop(0, n // step, add, 0)
        at += n * len(bases)
        lo, rows = keep, n
    for k in range(rows // 16):
        done[rows16(lo + 16 * k, 16), :] = g[rows16(bases[0] + lo + 16 * k, 16), :]
    for dim, n, before in reversed(back):
        part = rows16(lo, n)
        copy = net.send(done.at[part], done.at[part], dim)
        yield
        copy.wait()
        lo = before


def small_sum(net, value, slots, order):
    for i, dim in enumerate(order):
        copy = net.send(value, slots.at[i], dim)
        yield
        copy.wait()
        value[...] += slots[i]


def advance(*sums):
    for one in sums:
        next(one, None)


def drain(*sums):
    left = list(sums)
    while left:
        left = [one for one in left if next(one, left) is not left]


def quarter(net):
    return 2 * net.c + net.c + net.m - 2 * net.c * net.m


def choose(slots, by_core, by_y):
    core = jnp.where(by_core, 1.0, 0.0)
    y = jnp.where(by_y, 1.0, 0.0)
    return (slots[0].astype(F32) * core + slots[1].astype(F32) * y).astype(BF)


def pick_next(net, slots):
    q = quarter(net)
    return choose(slots, q == 1, q % 2 == 0)


def pick_prev(net, slots):
    q = quarter(net)
    return choose(slots, q == 2, q % 2 == 1)


def layer(r, bits):
    T, D = r.stream.shape
    half, F2 = D // 2, r.down_l.shape[0]
    net = Net(r, bits)
    c, m = net.c, net.m
    sub = c + m - 2 * c * m
    dims = list(range(bits))
    net.greet()

    own = [
        net.here(r.pos, r.stream),
        net.here(r.wqkv_l, r.wqkv.at[m]),
        net.here(r.wo_l, r.wo.at[rows16(m * half, half)]),
        net.here(r.up_l, r.up.at[m]),
        net.here(r.down_l, r.down.at[rows16(m * F2, F2)]),
    ]
    vec_copy = net.send(r.vecs_in.at[8:16], r.vec_got, "y")
    piece = rows16(c * half, half)
    qkv_y = net.send(r.wqkv_l.at[:, piece], r.wqkv.at[m, :, piece], "y")
    p = 2 * c + net.bit(0)
    ff_y = [
        net.send(r.wo_l.at[rows16(p * (half // 4), half // 4)], r.wo.at[rows16(m * half + p * (half // 4), half // 4)], "y"),
        net.send(r.up_l.at[rows16(p * (D // 4), D // 4)], r.up.at[m, rows16(p * (D // 4), D // 4)], "y"),
        net.send(r.down_l.at[rows16(p * (F2 // 4), F2 // 4)], r.down.at[rows16(m * F2 + p * (F2 // 4), F2 // 4)], "y"),
    ]

    def pass_on(at, parts, dim):
        wo = r.wo.at[rows16((1 - m) * half + at * (half // 4), parts * (half // 4))]
        up = r.up.at[1 - m, rows16(at * (D // 4), parts * (D // 4))]
        down = r.down.at[rows16((1 - m) * F2 + at * (F2 // 4), parts * (F2 // 4))]
        return [net.send(x, x, dim) for x in (wo, up, down)]

    r.small[...] = jnp.zeros_like(r.small)
    r.vecs[...] = r.vecs_in[...]
    own[0].wait()
    stage_stem(r)
    qkv_y.wait()
    arrived = r.wqkv.at[1 - m, :, piece]
    qkv_c = net.send(arrived, arrived, "c")
    vec_copy.wait()
    r.vecs[8:16, :] += r.vec_got[...]
    own[1].wait()
    qkv_c.wait()

    def block(slot, part):
        return r.kv.at[(2 * slot + part) * D : (2 * slot + part + 1) * D]

    kv_y, kv_c = [], []
    for part in range(2):
        stage_qkv(r, (1 + part,))
        kv_y.append(net.send(block(0, part), block(2, part), "y"))
        kv_c.append(net.send(block(0, part), block(1, part), "c"))
    stage_qkv(r, (0,))
    attend_block(r, 0)
    wait_all(ff_y)
    ff_x = pass_on(p, 1, 0)
    wait_all(kv_c)
    attend_block(r, 1)
    wait_all(ff_x)
    ff_c = pass_on(2 * c, 2, "c")
    wait_all(kv_y)
    kv_d = [net.send(block(2, part), block(3, part), "c") for part in range(2)]
    attend_block(r, 2)
    wait_all(kv_d)
    attend_block(r, 3)
    attend_end(r)
    wait_all(own[2:])
    wait_all(ff_c)
    stage_mid(r)
    stage_ff(r)
    down_sum = bucket_sum(net, r.g_down, r.got_down, r.done_down, 2, ["c"] + dims + ["y"])
    advance(down_sum)
    stage_mid_pull(r)
    rows_of_mine = rows16(sub * T, T)
    enc = [
        net.here(r.enc, r.enc_o.at[rows_of_mine]),
        net.send(r.enc, r.enc_o.at[rows_of_mine], "y"),
    ]
    up_sum = bucket_sum(net, r.g_up, r.got_up, r.done_up, 2, ["c"] + dims[1:] + dims[:1] + ["y"])
    advance(up_sum)

    turn = [0]

    def hook():
        turn[0] += 1
        advance(down_sum if turn[0] % 2 else up_sum)

    def halves(ref):
        return [ref.at[0], ref.at[1]]

    pull_block(r, 3, r.part_a, hook)
    to_c = [net.send(r.part_a, r.from_d, "c")]
    pull_block(r, 2, r.part_y, hook)
    wait_all(to_c)

    def join(i, carry):
        for part in range(2):
            rows = rows16(i * 32, 32)
            value = r.part_y[part, rows, :].astype(F32) + r.from_d[part, rows, :].astype(F32)
            r.part_y[part, rows, :] = value.astype(BF)
        return carry

    lax.fori_loop(0, D // 32, join, 0)
    to_y = net.send(r.part_y, r.from_y, "y")
    pull_block(r, 1, r.part_a, hook)
    to_s = net.send(r.part_a, r.from_s, "c")
    pull_block(r, 0, r.part_o, hook)
    r.dqb[...] = (r.dqt[...] * HEAD**-0.5).astype(BF)
    to_s.wait()
    to_y.wait()

    def total(i, carry):
        for part in range(2):
            rows = rows16(i * 32, 32)
            value = r.part_o[part, rows, :].astype(F32) + r.from_s[part, rows, :].astype(F32)
            r.part_o[part, rows, :] = (value + r.from_y[part, rows, :].astype(F32)).astype(BF)
        return carry

    lax.fori_loop(0, D // 32, total, 0)
    r.dkb, r.dvb = r.part_o.at[0], r.part_o.at[1]

    stage_qkv_weights(r)
    qkv_sum = bucket_sum(net, r.g_qkv, r.got_qkv, r.done_qkv, 2, ["c"] + dims[1:] + dims[:1] + ["y"])
    advance(qkv_sum, down_sum)
    stage_qkv_pull(r)
    rim = [net.send(r.sg.at[0:16], r.slots.at[0, i], dim) for i, dim in enumerate(("c", "y"))]
    stage_conv2_weights(r)
    c2_sum = bucket_sum(net, r.g_c2, r.got_c2, r.done_c2, 1, ["c"] + dims + ["y"])
    advance(c2_sum, qkv_sum, up_sum)
    wait_all(rim)
    stage_conv2_pull(r, pick_next(net, r.slots.at[0]))
    rim = [net.send(r.fe.at[0:16], r.slots.at[1, i], dim) for i, dim in enumerate(("c", "y"))]
    rim += [net.send(r.fo.at[T - 16 : T], r.slots.at[2, i], dim) for i, dim in enumerate(("c", "y"))]
    stage_conv1_weights(r)
    c1_sum = bucket_sum(net, r.g_c1, r.got_c1, r.done_c1, 1, ["c"] + dims + ["y"])
    vec_sum = small_sum(net, r.small, r.got_small, ["c"] + dims + ["y"])
    advance(c1_sum, vec_sum, c2_sum, qkv_sum, down_sum)
    wait_all(rim)
    stage_mel(r, pick_next(net, r.slots.at[1]), pick_prev(net, r.slots.at[2]))
    ends = [
        net.here(r.melg, r.mel_o.at[rows_of_mine]),
        net.send(r.melg, r.mel_o.at[rows_of_mine], "y"),
    ]
    drain(c2_sum, qkv_sum, c1_sum, vec_sum, up_sum, down_sum)

    side = F2 // D
    ends.append(net.here(r.done_down, r.down_o))
    for j in range(side):
        ends.append(net.here(r.done_up.at[j * D : (j + 1) * D], r.up_o.at[:, j * D : (j + 1) * D]))
    ends.append(net.here(r.done_up.at[side * D : side * D + half], r.out_o))
    for part in range(3):
        for j in range(2):
            ends.append(
                net.here(
                    r.done_qkv.at[part * half : (part + 1) * half, j * half : (j + 1) * half],
                    r.qkv_o.at[part, j * half : (j + 1) * half],
                )
            )
    ends.append(net.here(r.done_c2, r.c2_o))
    ends.append(net.here(r.done_c1, r.c1_o))
    ends.append(net.here(r.small, r.small_o))
    wait_all(enc)
    wait_all(ends)


def run_layer(bits, near, far, outs, T, D, F2, lanes):
    half, H = D // 2, D // HEAD
    td, dt = (T, D), (D, T)
    dims = list(range(bits))
    first, second = ["c"] + dims + ["y"], ["c"] + dims[1:] + dims[:1] + ["y"]
    buckets = dict(
        down=(F2, 2, first),
        up=(F2 + half, 2, second),
        qkv=(3 * half, 2, second),
        c2=(3 * D, 1, first),
        c1=(lanes, 1, first),
    )
    scratch = dict(
        wqkv=((2, 3, D, half), BF),
        wo=((D, D), BF),
        up=((2, D, F2), BF),
        down=((2 * F2, D), BF),
        vecs=((16, D), F32),
        vec_got=((8, D), F32),
        stream=(td, F32),
        he=(td, BF),
        ho=(td, BF),
        hp=(td, BF),
        dge=(td, F32),
        dgo=(td, F32),
        dg2=(td, F32),
        normed=(td, BF),
        qt=(dt, BF),
        kv=((8 * D, T), BF),
        mixt=(dt, F32),
        mixb=(dt, BF),
        dot=(dt, BF),
        top=((H, 1, T), F32),
        total=((H, 1, T), F32),
        diag=((H, 1, T), F32),
        tmp=(td, F32),
        tmp2=(td, F32),
        shift=((T + 16, D), F32),
        wide=((T + 16, 128), F32),
        mid=(td, F32),
        ntwo=(td, BF),
        act=(td, BF),
        ing=(td, BF),
        ffo=(td, F32),
        ntg=(td, F32),
        attg=(td, BF),
        dqb=(dt, BF),
        part_a=((2, D, T), BF),
        part_y=((2, D, T), BF),
        part_o=((2, D, T), BF),
        from_d=((2, D, T), BF),
        from_y=((2, D, T), BF),
        from_s=((2, D, T), BF),
        enc=(td, BF),
        melg=((T, 256), F32),
        small=((16, D), F32),
        got_small=((bits + 2, 16, D), F32),
        slots=((3, 2, 16, D), BF),
    )
    for n, (rows, halves, order) in buckets.items():
        if n not in ("qkv", "c2") or T != D:
            scratch["g_" + n] = ((rows * halves, D), BF)
        scratch["got_" + n] = ((sum_plan(rows, halves, order)[1], D), BF)
        scratch["done_" + n] = ((rows, D), BF)
    names = list(near) + list(far) + list(outs) + list(scratch) + ["send", "recv", "own"]

    def kernel(*refs):
        r = Box()
        for n, ref in zip(names, refs):
            setattr(r, n, ref)
        r.odd, r.smg, r.sg, r.fe, r.fo, r.dqt = r.shift, r.mid, r.ntwo, r.act, r.ing, r.ffo
        if T == D:
            r.g_qkv, r.g_c2 = r.kv.at[0 : 6 * half], r.kv.at[3 * D : 6 * D]
        layer(r, bits)

    vmem, anywhere = pl.BlockSpec(memory_space=pltpu.VMEM), pl.BlockSpec(memory_space=pl.ANY)
    got = pl.pallas_call(
        kernel,
        name="layer",
        out_shape=[jax.ShapeDtypeStruct(*o) for o in outs.values()],
        in_specs=[vmem] * len(near) + [anywhere] * len(far),
        out_specs=[anywhere] * len(outs),
        scratch_shapes=[pltpu.VMEM(*s) for s in scratch.values()]
        + [pltpu.SemaphoreType.DMA((160,)), pltpu.SemaphoreType.DMA((160,)), pltpu.SemaphoreType.DMA((32,))],
        compiler_params=pltpu.CompilerParams(
            vmem_limit_bytes=VMEM_LIMIT, collective_id=1, has_side_effects=True
        ),
    )(*near.values(), *far.values())
    return dict(zip(outs, got))


def sinusoids(positions, channels):
    half_width = channels // 2
    increment = math.log(10000.0) / (half_width - 1)
    inverse = jnp.exp(-increment * jnp.arange(half_width, dtype=F32))
    angles = positions.astype(F32)[:, None] * inverse[None, :]
    return jnp.concatenate([jnp.sin(angles), jnp.cos(angles)], axis=1)


def on_device(
    mel_input,
    conv1_weight,
    conv1_bias,
    conv2_weight,
    conv2_bias,
    norm1_gain,
    norm1_bias,
    qkv_weight,
    qkv_bias,
    out_weight,
    out_bias,
    norm2_gain,
    norm2_bias,
    up_weight,
    up_bias,
    down_weight,
    down_bias,
    cotangent,
    speech_mask,
):
    mel = mel_input[0]
    mels = mel.shape[0]
    T, D = cotangent.shape[1] // 2, cotangent.shape[2]
    F2 = up_weight.shape[1]
    side, half = F2 // D, D // 2
    bits = (lax.axis_size("dp") - 1).bit_length()
    c, m = lax.axis_index("seq"), lax.axis_index("mp")
    sub = jnp.bitwise_xor(c, m)

    low = lax.ppermute(mel[:, -2:], "seq", [(0, 1)])
    high = lax.ppermute(mel[:, :2], "seq", [(1, 0)])
    window = lax.dynamic_slice_in_dim(
        jnp.concatenate([low, mel, high], axis=1), sub * 2 * T, 2 * T + 4, axis=1
    )
    pairs = window.T.reshape(T + 2, 2 * mels)
    xe = jnp.concatenate([pairs[0:T, mels:], pairs[1 : T + 1]], axis=1)
    xo = jnp.concatenate([pairs[1 : T + 1], pairs[2 : T + 2, :mels]], axis=1)
    xh = jnp.concatenate([pairs[0:1], pairs[1:2, :mels]], axis=1)
    lanes = -(-3 * mels // 128) * 128
    xe = jnp.pad(xe, ((0, 0), (0, lanes - 3 * mels)))
    xo = jnp.pad(xo, ((0, 0), (0, lanes - 3 * mels)))
    xh = jnp.pad(xh, ((7, 8), (0, lanes - 3 * mels)))
    w1 = jnp.pad(conv1_weight.reshape(3 * mels, D), ((0, lanes - 3 * mels), (0, 0)))
    w1p = jnp.pad(conv1_weight, ((0, 0), (0, 128 - mels), (0, 0)))
    pos = sinusoids((c * 2 + sub) * T + jnp.arange(T, dtype=jnp.int32), D)

    table = [conv1_bias, conv2_bias, norm1_gain, norm1_bias, out_bias, norm2_gain, norm2_bias]
    table = jnp.stack(table + [down_bias]).astype(F32)
    mine = jnp.zeros((8, D), F32)
    mine = lax.dynamic_update_slice(mine, qkv_bias.astype(F32), (0, m * half))
    mine = lax.dynamic_update_slice(mine, up_bias.astype(F32).reshape(side, D), (2 + m * side, 0))
    vecs = jnp.concatenate([table, mine], axis=0)

    cot = lax.dynamic_slice_in_dim(cotangent[0], sub * T, T, axis=0)
    mask = lax.dynamic_slice_in_dim(speech_mask[0], sub * T, T, axis=0)
    bg = cot * mask.astype(BF)[:, None]

    got = run_layer(
        bits,
        dict(xe=xe, xo=xo, xh=xh, w1=w1, w1p=w1p, w2=conv2_weight, vecs_in=vecs, bg=bg),
        dict(pos=pos, wqkv_l=qkv_weight, wo_l=out_weight, up_l=up_weight, down_l=down_weight),
        dict(
            enc_o=((2 * T, D), BF),
            mel_o=((2 * T, 256), F32),
            down_o=((F2, D), BF),
            up_o=((D, F2), BF),
            out_o=((half, D), BF),
            qkv_o=((3, D, half), BF),
            c2_o=((3 * D, D), BF),
            c1_o=((lanes, D), BF),
            small_o=((16, D), F32),
        ),
        T,
        D,
        F2,
        lanes,
    )
    small = got["small_o"]
    own_half = lax.dynamic_slice_in_dim(small[QB : QB + 2], m * half, half, axis=1)
    own_up = lax.dynamic_slice_in_dim(small[UPB : UPB + 2 * side], m * side, side, axis=0).reshape(-1)
    melg = got["mel_o"].reshape(4 * T, 128)[:, :mels].T[None]
    return (
        got["enc_o"][None],
        melg,
        got["c1_o"][: 3 * mels].astype(F32).reshape(3, mels, D),
        small[C1B],
        got["c2_o"].astype(F32).reshape(3, D, D),
        small[C2B],
        small[N1G],
        small[N1B],
        got["qkv_o"].astype(F32),
        own_half,
        got["out_o"].astype(F32),
        small[OUB],
        small[N2G],
        small[N2B],
        got["up_o"].astype(F32),
        own_up,
        got["down_o"].astype(F32),
        small[DNB],
    )


def solution(mesh):
    placed = (
        P("dp", None, "seq"),
        P(),
        P(),
        P(),
        P(),
        P(),
        P(),
        P(None, None, "mp"),
        P(None, "mp"),
        P("mp", None),
        P(),
        P(),
        P(),
        P(None, "mp"),
        P("mp"),
        P("mp", None),
        P(),
        P("dp", "seq", None),
        P("dp", "seq"),
    )
    return jax.shard_map(
        on_device,
        mesh=mesh,
        in_specs=placed,
        out_specs=(
            P("dp", "seq", None),
            P("dp", None, "seq"),
            P(),
            P(),
            P(),
            P(),
            P(),
            P(),
            P(None, None, "mp"),
            P(None, "mp"),
            P("mp", None),
            P(),
            P(),
            P(),
            P(None, "mp"),
            P("mp"),
            P("mp", None),
            P(),
        ),
        check_vma=False,
    )
```

time: 698 us -> 254 us (0.36)
  waiting for transfers between devices: 449 us -> 0.01 us
  Pallas kernels: 114 us -> 214 us
  blocking collectives: 64.2 us -> 0 us
  local copies, waits for them, and re-layouts: 31.8 us -> 16.5 us
  between operations: 14.7 us -> 0.85 us
    psum x2 -> x0, waiting for transfers between devices: 199 us -> none  [the longest x1 104 us: on_device(): mine = lax.psum(mine, ('dp', 'seq')).astype(F32)]
    all_gather x6 -> x0, waiting for transfers between devices: 129 us -> none  [the longest x2 39.3 us: ordered(): both = lax.all_gather(value, 'mp', axis=0)]
    reduce_scatter x2 -> x0, waiting for transfers between devices: 118 us -> none  [the longest x1 74.8 us: on_device(): mine = lax.psum_scatter(packed, 'mp', scatter_dimension=0, tiled=True)[0]]
    pallas_call x3 -> x1, Pallas kernels: 114 us -> 214 us  [run_layer(): pl.pallas_call(kernel, name='layer', out_shape=[jax.ShapeDtypeStruct(*o)...]
    psum x1 -> x0, blocking collectives: 39.8 us -> none  [on_device(): small = lax.psum(b['small'] + e['small'], ('dp', 'seq', 'mp'))]
    all_gather x3 -> x0, blocking collectives: 24.4 us -> none  [the longest x1 15.5 us: on_device(): wo = lax.all_gather(out_weight, 'mp', axis=0, tiled=True)]
    slice x6 -> x2, local copies, waits for them, and re-layouts: 10.7 us -> 0.74 us  [the longest x1 0.72 us: on_device(): small[UPB:UPB + 2 * side]]
    concatenate x2 -> x1, other arithmetic: 10 us -> 0.62 us  [on_device(): vecs = jnp.concatenate([table, mine], axis=0)]
  transfers between devices with their start and end apart: 12 -> 2, of which waited for: 10 -> 0; matrix products, arithmetic and copies ran while one was open for 4% -> 6% of each run, Pallas kernels for 2% -> 0%
where the time goes in v2:
time: 254 us
  Pallas kernels  214 us (84%)
  other arithmetic  18.6 us (7%)
  local copies, waits for them, and re-layouts  16.5 us (6%)
  starting transfers between devices  3.64 us (1%)
    pallas_call x1, Pallas kernels, run_layer(): pl.pallas_call(kernel, name='layer', out_shape=[jax.ShapeDtypeStruct(*o)...  214 us
    another operation x9, local copies, waits for them, and re-layouts, on_device(): table = jnp.stack(table + [down_bias]).astype(F32)  5.49 us
  transfers between devices with their start and end apart: 2, of which 0 were waited for; matrix products, arithmetic and copies ran while one was open for 6% of the time, Pallas kernels for 0%

profile of v2, /device:TPU:0, one launch (start us, length us, event | category | flops | bytes accessed | tf_op | source)
XLA Modules:
  0.0 253.6 jit_solution(2630479163576029505)
XLA Ops:
  0.7 0.8 fusion.13
  1.5 2.3 collective-permute-start
  3.8 1.3 collective-permute-start.1
  5.2 0.7 reshape.97
  5.9 0.7 stack.27
  6.5 0.7 stack.28
  7.2 0.7 stack.29
  7.9 0.7 stack.30
  8.6 0.7 stack.31
  9.3 0.7 stack.32
  10.0 0.7 stack.33
  11.4 0.7 convert_reduce_fusion
  12.1 2.0 bitcast_multiply_fusion.refs_7_
  14.2 0.7 convert_dynamic-update-slice_fusion
  15.5 1.9 multiply_sine_fusion
  17.4 1.1 pad_maximum_fusion.refs_8_
  18.5 0.8 pad.23.refs_4_
  19.3 0.7 pad.22.refs_3_
  21.6 0.7 fusion.11.refs_2_
  22.3 1.0 fusion.5
  23.3 214.0 %layer.1 = (bf16[1024,512]{1,0:T(8,128)(2,1)}, f32[1024,256]{1,0:T(8,128)}, bf16[1024,512]{1,0:T(8,128)(2,1)}, bf16[512,1024]{1,0:T(8,128)(2,1)}, bf16[256,512]{...) custom-call(bf16[512,256]{1,0:T(8,128)(2,1)} %get-tuple-element.41.r, ...), custom_call_target="tpu_custom_call" | custom-call | tf_op jit(solution)/shard_map/layer/pallas_call | solution.py:792
  237.3 0.7 slice.83
  238.1 1.6 fusion.15
  239.7 0.7 slice.79
  240.4 3.6 %convert.4 = f32[3,512,512]{2,1,0:T(8,128)} convert(bf16[3,512,512]{2,1,0:T(8,128)(2,1)} %bitcast.27) | non-fusion elementwise | flops 786432 | bytes 4718592 | tf_op jit(solution)/shard_map/reshape | solution.py:902
  244.0 1.6 convert_element_type.54
  245.6 1.6 convert_element_type.55
  247.3 1.2 copy.45
  248.4 1.3 convert_element_type.52
  249.7 0.8 convert.3
  250.6 0.9 convert_element_type.53
  252.6 1.0 copy.50
  (45 shorter events, 4.2 us)
Async XLA Ops:
  1.5 18.5 %collective-permute-start = (bf16[80,2]{1,0:T(8,128)(2,1)S(1)}, bf16[80,2]{1,0:T(8,128)(2,1)S(1)}, u32[]{:S(2)}, u32[]{:S(2)}) collective-permute-start(bf16[80,2]{1,0:T(8,128)(2,1)S(1)} %get-tuple-element.37), channel_id=1, source_target_pairs={{0,2},{1,3},{4,6},{5,7},{8,10},{9,11},{12,14},{13,15},{16,18},{17,... | collective-permute-start | bytes 968 | tf_op jit(solution)/shard_map/ppermute | solution.py:845
  3.8 16.2 %collective-permute-start.1 = (bf16[80,2]{1,0:T(8,128)(2,1)S(1)}, bf16[80,2]{1,0:T(8,128)(2,1)S(1)}, u32[]{:S(2)}, u32[]{:S(2)}) collective-permute-start(bf16[80,2]{1,0:T(8,128)(2,1)S(1)} %get-tuple-element.36), channel_id=1, source_target_pairs={{2,0},{3,1},{6,4},{7,5},{10,8},{11,9},{14,12},{15,13},{18,16},{19,... | collective-permute-start | bytes 968 | tf_op jit(solution)/shard_map/ppermute | solution.py:846
  12.1 6.4 %copy-start.4 = (bf16[3,80,512]{2,1,0:T(8,128)(2,1)S(1)}, bf16[3,80,512]{2,1,0:T(8,128)(2,1)}, u32[]{:S(2)}) copy-start(bf16[3,80,512]{2,1,0:T(8,128)(2,1)} %param.20) | copy-start | bytes 737284
  15.5 4.5 %copy-start.6 = (bf16[1,80,2048]{2,1,0:T(8,128)(2,1)S(1)}, bf16[1,80,2048]{2,1,0:T(8,128)(2,1)}, u32[]{:S(2)}) copy-start(bf16[1,80,2048]{2,1,0:T(8,128)(2,1)} %param.19) | copy-start | bytes 983044
  240.4 3.6 %copy-start.1 = (bf16[512,1024]{1,0:T(8,128)(2,1)S(1)}, bf16[512,1024]{1,0:T(8,128)(2,1)}, u32[]{:S(2)}) copy-start(bf16[512,1024]{1,0:T(8,128)(2,1)} %get-tuple-element.34) | copy-start | bytes 3145732
  244.0 1.6 copy-start
  245.6 1.6 copy-start.3
  247.2 1.3 copy-start.5
  247.3 2.5 copy-start.8
  248.4 2.1 copy-start.7
  248.4 4.2 %copy-start.2 = (bf16[1024,512]{1,0:T(8,128)(2,1)S(1)}, bf16[1024,512]{1,0:T(8,128)(2,1)}, u32[]{:S(2)}) copy-start(bf16[1024,512]{1,0:T(8,128)(2,1)} %get-tuple-element.27) | copy-start | bytes 3145732

commit v3 on v2

--- a/solution.py
+++ b/solution.py
@@ -3,6 +3,7 @@
 
 import jax
 import jax.numpy as jnp
+import numpy as np
 from jax import lax
 from jax.experimental import pallas as pl
 from jax.experimental.pallas import tpu as pltpu
@@ -89,15 +90,47 @@
     return jnp.sum(value, axis=0, keepdims=True)
 
 
-def stage_stem(r):
-    T, D = r.stream.shape
-    c = lax.axis_index("seq")
-    m = lax.axis_index("mp")
-    w1 = r.w1[...]
-    first = jnp.logical_and(c == 0, m == 0)
-    edge = nn(r.xh[...], w1) + vec(r, C1B)
+def stage_mel_rows(r, sub):
+    T, D = r.stream.shape
+    row = lax.broadcasted_iota(jnp.int32, (256, 256), 0)
+    lane = lax.broadcasted_iota(jnp.int32, (256, 256), 1)
+    pick = jnp.where(lane == 2 * (row % 128) + row // 128, 1.0, 0.0).astype(BF)
+    base = sub * 2 * T
+
+    def lanes(start, size):
+        return r.melbuf[:, pl.ds(pl.multiple_of(base + start, 128), size)]
+
+    row = lax.broadcasted_iota(jnp.int32, (16, 128), 0)
+    lane = lax.broadcasted_iota(jnp.int32, (16, 128), 1)
+
+    def select(at, to):
+        return jnp.where(jnp.logical_and(row == to, lane == at), 1.0, 0.0).astype(BF)
+
+    before, after = lanes(0, 128), lanes(128 + 2 * T, 128)
+    r.mele[0:8, :] = nt(select(126, 7), before)[0:8, :]
+    r.melo[0:8, :] = nt(select(127, 7), before)[0:8, :]
+    r.mele[T + 8 : T + 16, :] = nt(select(0, 0), after)[0:8, :]
+    for k in range(T // 128):
+        both = nt(pick, lanes(128 + 256 * k, 256))
+        r.mele[8 + 128 * k : 136 + 128 * k, :] = both[0:128, :]
+        r.melo[8 + 128 * k : 136 + 128 * k, :] = both[128:256, :]
+
+
+def three(a, b, c):
+    return jnp.concatenate([a, b, c], axis=1).astype(BF)
+
+
+def stage_first(r, first):
+    T, D = r.stream.shape
+    for o in range(3):
+        r.w1p[128 * o : 128 * o + r.w1.shape[1], :] = r.w1[o]
+        r.w1p[128 * o + r.w1.shape[1] : 128 * (o + 1), :] = jnp.zeros((128 - r.w1.shape[1], D), BF)
+    w1 = r.w1p[...]
+    edge = nn(three(r.mele[0:16, :], r.melo[0:16, :], r.mele[1:17, :]), w1) + vec(r, C1B)
     edge = gelu_both(edge)[0] * jnp.where(first, 0.0, 1.0)
     r.odd[0:8, :] = edge[0:8, :]
+    r.xe[...] = three(r.melo[7 : 7 + T, :], r.mele[8 : 8 + T, :], r.melo[8 : 8 + T, :])
+    r.xo[...] = three(r.mele[8 : 8 + T, :], r.melo[8 : 8 + T, :], r.mele[9 : 9 + T, :])
     r.tmp[...] = nn(r.xe[...], w1)
 
     def even(rows):
@@ -115,17 +148,38 @@
         r.dgo[rows, :] = slope
 
     rows_loop(T, 32, odd)
+
+
+def stage_second(r, place):
+    T, D = r.stream.shape
     r.hp[...] = r.odd[7 : 7 + T, :].astype(BF)
     r.tmp[...] = nn(r.hp[...], r.w2[0]) + nn(r.he[...], r.w2[1]) + nn(r.ho[...], r.w2[2])
+    fine = r.fine_s.shape[0]
 
     def second(rows):
         value, slope = gelu_both(r.tmp[rows, :] + vec(r, C2B))
-        stream = value + r.stream[rows, :]
+        at = place * (T // fine) + rows.start // fine
+        s0, c0 = r.coarse_s[pl.ds(at, 1), :], r.coarse_c[pl.ds(at, 1), :]
+        s1, c1 = r.fine_s[...], r.fine_c[...]
+        stream = value + jnp.concatenate([s0 * c1 + c0 * s1, c0 * c1 - s0 * s1], axis=1)
         r.dg2[rows, :] = slope
         r.stream[rows, :] = stream
         r.normed[rows, :] = (normal(stream)[0] * vec(r, N1G) + vec(r, N1B)).astype(BF)
 
-    rows_loop(T, 32, second)
+    rows_loop(T, fine, second)
+
+
+def stage_mask(r, sub):
+    T, D = r.stream.shape
+    row = r.mask[0:1, pl.ds(pl.multiple_of(sub * T, 128), T)].astype(F32)
+    r.wide[0:T, :] = jnp.broadcast_to(row, (128, T)).T
+
+    def one(rows):
+        keep = r.wide[rows, :]
+        keep = jnp.concatenate([keep] * (D // 128), axis=1)
+        r.bg[rows, :] = (r.bg[rows, :].astype(F32) * keep).astype(BF)
+
+    rows_loop(T, 32, one)
 
 
 def stage_qkv(r, parts):
@@ -308,8 +362,8 @@
             r.dqt[rows, :] += dq
         return carry
 
-    for part in range(2):
-        lax.fori_loop(part * H // 2, (part + 1) * H // 2, one, 0)
+    for part in range(4):
+        lax.fori_loop(part * H // 4, (part + 1) * H // 4, one, 0)
         hook()
 
 
@@ -377,22 +431,28 @@
     D = r.stream.shape[1]
     sg = r.sg[...]
     for i, tap in enumerate((r.hp, r.he, r.ho)):
-        r.g_c2[i * D : (i + 1) * D, :] = tn(tap[...], sg).astype(BF)
+        value = tn(tap[...], sg).astype(BF)
+        r.g_c2[i * D : (i + 1) * D, :] = value
 
 
 def stage_conv1_weights(r):
-    r.g_c1[...] = (tn(r.xe[...], r.fe[...]) + tn(r.xo[...], r.fo[...])).astype(BF)
+    value = (tn(r.xe[...], r.fe[...]) + tn(r.xo[...], r.fo[...])).astype(BF)
+    mels = r.w1.shape[1]
+    for o in range(3):
+        r.g_c1[mels * o : mels * (o + 1), :] = value[128 * o : 128 * o + mels, :]
+    r.g_c1[3 * mels :, :] = jnp.zeros((r.g_c1.shape[0] - 3 * mels, r.g_c1.shape[1]), BF)
 
 
 def stage_mel(r, next_row, prev_row):
     T, D = r.stream.shape
     fe, fo = r.fe[...], r.fo[...]
-    r.wide[16 : 16 + T, :] = nt(fo, r.w1p[2])
-    r.wide[0:16, :] = nt(prev_row, r.w1p[2])
-    r.melg[:, 0:128] = nt(fe, r.w1p[1]) + nt(fo, r.w1p[0]) + r.wide[15 : 15 + T, :]
-    r.wide[0:T, :] = nt(fe, r.w1p[0])
-    r.wide[T : T + 16, :] = nt(next_row, r.w1p[0])
-    r.melg[:, 128:256] = nt(fe, r.w1p[2]) + nt(fo, r.w1p[1]) + r.wide[1 : 1 + T, :]
+    w = [r.w1p[128 * o : 128 * (o + 1), :] for o in range(3)]
+    r.wide[16 : 16 + T, :] = nt(fo, w[2])
+    r.wide[0:16, :] = nt(prev_row, w[2])
+    r.melg[:, 0:128] = (nt(fe, w[1]) + nt(fo, w[0]) + r.wide[15 : 15 + T, :]).astype(BF)
+    r.wide[0:T, :] = nt(fe, w[0])
+    r.wide[T : T + 16, :] = nt(next_row, w[0])
+    r.melg[:, 128:256] = (nt(fe, w[2]) + nt(fo, w[1]) + r.wide[1 : 1 + T, :]).astype(BF)
 
 
 class Net:
@@ -548,48 +608,90 @@
     return choose(slots, q == 2, q % 2 == 1)
 
 
+ROW_BIASES = ("c1b", "c2b", "n1g", "n1b", "oub", "n2g", "n2b", "dnb")
+
+
+def orders(bits):
+    dims = list(range(bits))
+    z_first = dims[1:2] + dims[:1] + dims[2:]
+    return dict(
+        down=["c", "y"] + dims,
+        up=["c"] + dims + ["y"],
+        qkv=["c"] + z_first + ["y"],
+        c2a=["c", "y"] + dims,
+        c2b=["c"] + dims[:1] + ["y"] + dims[1:],
+        c1=["c"] + dims + ["y"],
+        vec=["c"] + dims + ["y"],
+    )
+
+
 def layer(r, bits):
     T, D = r.stream.shape
     half, F2 = D // 2, r.down_l.shape[0]
+    side = F2 // D
+    mels, span = r.w1.shape[1], 4 * T
     net = Net(r, bits)
     c, m = net.c, net.m
     sub = c + m - 2 * c * m
-    dims = list(range(bits))
+    order = orders(bits)
+    rows_of_mine = rows16(sub * T, T)
+
+    r.melbuf[...] = jnp.zeros_like(r.melbuf)
+    r.vec_mine[...] = jnp.zeros_like(r.vec_mine)
+    own_lanes = pl.ds(pl.multiple_of(m * half, 128), half)
+    r.vec_mine[0:2, own_lanes] = r.qkvb[...].astype(F32)
+    for k in range(side):
+        r.vec_mine[pl.ds(2 + m * side + k, 1), :] = r.upb[k * D : (k + 1) * D].astype(F32).reshape(1, D)
+    for k, n in enumerate(ROW_BIASES):
+        r.vecs[k : k + 1, :] = getattr(r, n)[...].astype(F32).reshape(1, D)
     net.greet()
-
+    mel_own = net.here(r.mel.at[0], r.melbuf.at[0:mels, 128 : 128 + span])
+    src = pl.ds(pl.multiple_of((1 - c) * (span - 128), 128), 128)
+    dst = pl.ds(pl.multiple_of(c * (span + 128), 128), 128)
+    mel_rim = net.send(r.mel.at[0, :, src], r.melbuf.at[0:mels, dst], "c")
+    piece = rows16(c * half, half)
+    qkv_y = net.send(r.wqkv_l.at[:, piece], r.wqkv.at[m, :, piece], "y")
+    vec_copy = net.send(r.vec_mine, r.vec_got, "y")
+    w2_own = net.here(r.w2_l, r.w2)
     own = [
-        net.here(r.pos, r.stream),
         net.here(r.wqkv_l, r.wqkv.at[m]),
+        net.here(r.cot.at[0, rows_of_mine], r.bg),
         net.here(r.wo_l, r.wo.at[rows16(m * half, half)]),
         net.here(r.up_l, r.up.at[m]),
         net.here(r.down_l, r.down.at[rows16(m * F2, F2)]),
     ]
-    vec_copy = net.send(r.vecs_in.at[8:16], r.vec_got, "y")
-    piece = rows16(c * half, half)
-    qkv_y = net.send(r.wqkv_l.at[:, piece], r.wqkv.at[m, :, piece], "y")
-    p = 2 * c + net.bit(0)
-    ff_y = [
-        net.send(r.wo_l.at[rows16(p * (half // 4), half // 4)], r.wo.at[rows16(m * half + p * (half // 4), half // 4)], "y"),
-        net.send(r.up_l.at[rows16(p * (D // 4), D // 4)], r.up.at[m, rows16(p * (D // 4), D // 4)], "y"),
-        net.send(r.down_l.at[rows16(p * (F2 // 4), F2 // 4)], r.down.at[rows16(m * F2 + p * (F2 // 4), F2 // 4)], "y"),
-    ]
-
-    def pass_on(at, parts, dim):
-        wo = r.wo.at[rows16((1 - m) * half + at * (half // 4), parts * (half // 4))]
-        up = r.up.at[1 - m, rows16(at * (D // 4), parts * (D // 4))]
-        down = r.down.at[rows16((1 - m) * F2 + at * (F2 // 4), parts * (F2 // 4))]
-        return [net.send(x, x, dim) for x in (wo, up, down)]
+
+    p = 4 * c + 2 * net.bit(0) + net.bit(1) if bits > 1 else 2 * c + net.bit(0)
+    cuts = 8 if bits > 1 else 4
+
+    def ff_parts(of, at, count, local):
+        def cut(n, base):
+            return rows16(base + at * (n // cuts), count * (n // cuts))
+
+        if local:
+            return [r.wo_l.at[cut(half, 0)], r.up_l.at[cut(D, 0)], r.down_l.at[cut(F2, 0)]]
+        return [r.wo.at[cut(half, of * half)], r.up.at[of, cut(D, 0)], r.down.at[cut(F2, of * F2)]]
+
+    def pass_on(at, count, dim):
+        return [net.send(x, x, dim) for x in ff_parts(1 - m, at, count, False)]
 
     r.small[...] = jnp.zeros_like(r.small)
-    r.vecs[...] = r.vecs_in[...]
-    own[0].wait()
-    stage_stem(r)
+    mel_own.wait()
+    mel_rim.wait()
+    stage_mel_rows(r, sub)
+    stage_first(r, jnp.logical_and(c == 0, m == 0))
     qkv_y.wait()
     arrived = r.wqkv.at[1 - m, :, piece]
     qkv_c = net.send(arrived, arrived, "c")
+    ff = [
+        net.send(a, b, "y")
+        for a, b in zip(ff_parts(m, p, 1, True), ff_parts(m, p, 1, False))
+    ]
+    w2_own.wait()
+    stage_second(r, quarter(net))
     vec_copy.wait()
-    r.vecs[8:16, :] += r.vec_got[...]
-    own[1].wait()
+    r.vecs[8:16, :] = r.vec_mine[...] + r.vec_got[...]
+    wait_all(own[0:1])
     qkv_c.wait()
 
     def block(slot, part):
@@ -601,13 +703,17 @@
         kv_y.append(net.send(block(0, part), block(2, part), "y"))
         kv_c.append(net.send(block(0, part), block(1, part), "c"))
     stage_qkv(r, (0,))
+    wait_all(ff)
+    ff = pass_on(p, 1, 1) if bits > 1 else []
+    wait_all(own[1:2])
+    stage_mask(r, sub)
     attend_block(r, 0)
-    wait_all(ff_y)
-    ff_x = pass_on(p, 1, 0)
+    wait_all(ff)
+    ff = pass_on((p // 2) * 2 if bits > 1 else p, 2 if bits > 1 else 1, 0)
     wait_all(kv_c)
     attend_block(r, 1)
-    wait_all(ff_x)
-    ff_c = pass_on(2 * c, 2, "c")
+    wait_all(ff)
+    ff = pass_on(c * (cuts // 2), cuts // 2, "c")
     wait_all(kv_y)
     kv_d = [net.send(block(2, part), block(3, part), "c") for part in range(2)]
     attend_block(r, 2)
@@ -615,33 +721,49 @@
     attend_block(r, 3)
     attend_end(r)
     wait_all(own[2:])
-    wait_all(ff_c)
+    wait_all(ff)
     stage_mid(r)
     stage_ff(r)
-    down_sum = bucket_sum(net, r.g_down, r.got_down, r.done_down, 2, ["c"] + dims + ["y"])
+
+    def summed(n, halves):
+        return bucket_sum(
+            net, getattr(r, "g_" + n), getattr(r, "got_" + n), getattr(r, "done_" + n), halves, order[n]
+        )
+
+    down_sum = summed("down", 2)
     advance(down_sum)
     stage_mid_pull(r)
-    rows_of_mine = rows16(sub * T, T)
-    enc = [
-        net.here(r.enc, r.enc_o.at[rows_of_mine]),
-        net.send(r.enc, r.enc_o.at[rows_of_mine], "y"),
-    ]
-    up_sum = bucket_sum(net, r.g_up, r.got_up, r.done_up, 2, ["c"] + dims[1:] + dims[:1] + ["y"])
-    advance(up_sum)
-
+    up_sum = summed("up", 2)
+    advance(up_sum, down_sum)
+    enc = []
+
+    def send_enc():
+        enc.append(net.here(r.enc, r.enc_o.at[rows_of_mine]))
+        enc.append(net.send(r.enc, r.enc_o.at[rows_of_mine], "y"))
+
+    moves = {
+        1: (up_sum,),
+        4: (down_sum,),
+        6: (up_sum, down_sum),
+        9: (up_sum, down_sum),
+        12: (up_sum, down_sum),
+        13: (up_sum, down_sum),
+        14: (up_sum, down_sum),
+        15: (up_sum, down_sum),
+        16: (up_sum, down_sum),
+    }
     turn = [0]
 
     def hook():
         turn[0] += 1
-        advance(down_sum if turn[0] % 2 else up_sum)
-
-    def halves(ref):
-        return [ref.at[0], ref.at[1]]
+        advance(*moves.get(turn[0], ()))
+        if turn[0] == 4:
+            send_enc()
 
     pull_block(r, 3, r.part_a, hook)
-    to_c = [net.send(r.part_a, r.from_d, "c")]
+    to_c = net.send(r.part_a, r.from_d, "c")
     pull_block(r, 2, r.part_y, hook)
-    wait_all(to_c)
+    to_c.wait()
 
     def join(i, carry):
         for part in range(2):
@@ -670,30 +792,31 @@
     r.dkb, r.dvb = r.part_o.at[0], r.part_o.at[1]
 
     stage_qkv_weights(r)
-    qkv_sum = bucket_sum(net, r.g_qkv, r.got_qkv, r.done_qkv, 2, ["c"] + dims[1:] + dims[:1] + ["y"])
-    advance(qkv_sum, down_sum)
+    qkv_sum = summed("qkv", 2)
+    advance(qkv_sum, up_sum)
     stage_qkv_pull(r)
     rim = [net.send(r.sg.at[0:16], r.slots.at[0, i], dim) for i, dim in enumerate(("c", "y"))]
+    advance(qkv_sum)
     stage_conv2_weights(r)
-    c2_sum = bucket_sum(net, r.g_c2, r.got_c2, r.done_c2, 1, ["c"] + dims + ["y"])
-    advance(c2_sum, qkv_sum, up_sum)
+    c2a_sum, c2b_sum = summed("c2a", 1), summed("c2b", 1)
+    advance(c2a_sum, c2b_sum)
     wait_all(rim)
     stage_conv2_pull(r, pick_next(net, r.slots.at[0]))
     rim = [net.send(r.fe.at[0:16], r.slots.at[1, i], dim) for i, dim in enumerate(("c", "y"))]
     rim += [net.send(r.fo.at[T - 16 : T], r.slots.at[2, i], dim) for i, dim in enumerate(("c", "y"))]
+    advance(c2a_sum, c2b_sum, qkv_sum)
     stage_conv1_weights(r)
-    c1_sum = bucket_sum(net, r.g_c1, r.got_c1, r.done_c1, 1, ["c"] + dims + ["y"])
-    vec_sum = small_sum(net, r.small, r.got_small, ["c"] + dims + ["y"])
-    advance(c1_sum, vec_sum, c2_sum, qkv_sum, down_sum)
+    c1_sum = summed("c1", 1)
+    vec_sum = small_sum(net, r.small, r.got_small, order["vec"])
+    advance(c1_sum, vec_sum)
     wait_all(rim)
     stage_mel(r, pick_next(net, r.slots.at[1]), pick_prev(net, r.slots.at[2]))
     ends = [
         net.here(r.melg, r.mel_o.at[rows_of_mine]),
         net.send(r.melg, r.mel_o.at[rows_of_mine], "y"),
     ]
-    drain(c2_sum, qkv_sum, c1_sum, vec_sum, up_sum, down_sum)
-
-    side = F2 // D
+    drain(c1_sum, vec_sum, c2a_sum, c2b_sum, qkv_sum, up_sum, down_sum)
+
     ends.append(net.here(r.done_down, r.down_o))
     for j in range(side):
         ends.append(net.here(r.done_up.at[j * D : (j + 1) * D], r.up_o.at[:, j * D : (j + 1) * D]))
@@ -706,7 +829,8 @@
                     r.qkv_o.at[part, j * half : (j + 1) * half],
                 )
             )
-    ends.append(net.here(r.done_c2, r.c2_o))
+    ends.append(net.here(r.done_c2a, r.c2_o.at[0 : 3 * half]))
+    ends.append(net.here(r.done_c2b, r.c2_o.at[3 * half : 6 * half]))
     ends.append(net.here(r.done_c1, r.c1_o))
     ends.append(net.here(r.small, r.small_o))
     wait_all(enc)
@@ -716,21 +840,23 @@
 def run_layer(bits, near, far, outs, T, D, F2, lanes):
     half, H = D // 2, D // HEAD
     td, dt = (T, D), (D, T)
-    dims = list(range(bits))
-    first, second = ["c"] + dims + ["y"], ["c"] + dims[1:] + dims[:1] + ["y"]
-    buckets = dict(
-        down=(F2, 2, first),
-        up=(F2 + half, 2, second),
-        qkv=(3 * half, 2, second),
-        c2=(3 * D, 1, first),
-        c1=(lanes, 1, first),
-    )
+    order = orders(bits)
+    buckets = dict(down=(F2, 2), up=(F2 + half, 2), qkv=(3 * half, 2), c2a=(3 * half, 1), c2b=(3 * half, 1), c1=(lanes, 1))
     scratch = dict(
+        melbuf=((128, 4 * T + 256), BF),
+        mele=((T + 24, 128), F32),
+        melo=((T + 24, 128), F32),
+        xe=((T, 384), BF),
+        xo=((T, 384), BF),
+        w1p=((384, D), BF),
+        w2=((3, D, D), BF),
+        bg=(td, BF),
         wqkv=((2, 3, D, half), BF),
         wo=((D, D), BF),
         up=((2, D, F2), BF),
         down=((2 * F2, D), BF),
         vecs=((16, D), F32),
+        vec_mine=((8, D), F32),
         vec_got=((8, D), F32),
         stream=(td, F32),
         he=(td, BF),
@@ -767,16 +893,19 @@
         from_y=((2, D, T), BF),
         from_s=((2, D, T), BF),
         enc=(td, BF),
-        melg=((T, 256), F32),
+        melg=((T, 256), BF),
         small=((16, D), F32),
         got_small=((bits + 2, 16, D), F32),
         slots=((3, 2, 16, D), BF),
     )
-    for n, (rows, halves, order) in buckets.items():
-        if n not in ("qkv", "c2") or T != D:
+    alias = T == D
+    for n, (rows, halves) in buckets.items():
+        if n == "c1" or n in ("down", "up"):
             scratch["g_" + n] = ((rows * halves, D), BF)
-        scratch["got_" + n] = ((sum_plan(rows, halves, order)[1], D), BF)
+        scratch["got_" + n] = ((sum_plan(rows, halves, order[n])[1], D), BF)
         scratch["done_" + n] = ((rows, D), BF)
+    if not alias:
+        scratch.update(g_qkv=((6 * half, D), BF), g_c2=((6 * half, D), BF))
     names = list(near) + list(far) + list(outs) + list(scratch) + ["send", "recv", "own"]
 
     def kernel(*refs):
@@ -784,8 +913,9 @@
         for n, ref in zip(names, refs):
             setattr(r, n, ref)
         r.odd, r.smg, r.sg, r.fe, r.fo, r.dqt = r.shift, r.mid, r.ntwo, r.act, r.ing, r.ffo
-        if T == D:
-            r.g_qkv, r.g_c2 = r.kv.at[0 : 6 * half], r.kv.at[3 * D : 6 * D]
+        if alias:
+            r.g_qkv, r.g_c2 = r.kv.at[0 : 6 * half], r.kv.at[6 * half : 12 * half]
+        r.g_c2a, r.g_c2b = r.g_c2.at[0 : 3 * half], r.g_c2.at[3 * half : 6 * half]
         layer(r, bits)
 
     vmem, anywhere = pl.BlockSpec(memory_space=pltpu.VMEM), pl.BlockSpec(memory_space=pl.ANY)
@@ -796,7 +926,7 @@
         in_specs=[vmem] * len(near) + [anywhere] * len(far),
         out_specs=[anywhere] * len(outs),
         scratch_shapes=[pltpu.VMEM(*s) for s in scratch.values()]
-        + [pltpu.SemaphoreType.DMA((160,)), pltpu.SemaphoreType.DMA((160,)), pltpu.SemaphoreType.DMA((32,))],
+        + [pltpu.SemaphoreType.DMA((200,)), pltpu.SemaphoreType.DMA((200,)), pltpu.SemaphoreType.DMA((40,))],
         compiler_params=pltpu.CompilerParams(
             vmem_limit_bytes=VMEM_LIMIT, collective_id=1, has_side_effects=True
         ),
@@ -804,12 +934,71 @@
     return dict(zip(outs, got))
 
 
-def sinusoids(positions, channels):
+def run_finish(got, mels, side):
+    T2, D = got["enc_o"].shape
+    half = D // 2
+    ins = list(got)
+    outs = dict(
+        enc=((1, T2, D), BF),
+        mel=((1, mels, 2 * T2), F32),
+        c1=((3, mels, D), F32),
+        c2=((3, D, D), F32),
+        qkv=((3, D, half), F32),
+        out=((half, D), F32),
+        up=((D, side * D), F32),
+        down=((side * D, D), F32),
+    )
+
+    def kernel(*refs):
+        r = Box()
+        for n, ref in zip(ins + list(outs) + ["sem"], refs):
+            setattr(r, n, ref)
+        copy = pltpu.make_async_copy(r.enc_o, r.enc.at[0], r.sem)
+        copy.start()
+
+        def cast(src, dst):
+            def one(rows):
+                dst[rows, :] = src[rows, :].astype(F32)
+
+            rows_loop(src.shape[0], 64, one)
+
+        cast(r.down_o, r.down)
+        cast(r.up_o, r.up)
+        cast(r.out_o, r.out)
+        for o in range(3):
+            cast(r.qkv_o.at[o], r.qkv.at[o])
+            cast(r.c2_o.at[o * D : (o + 1) * D], r.c2.at[o])
+            r.c1[o] = r.c1_o[o * mels : (o + 1) * mels, :].astype(F32)
+        row = lax.broadcasted_iota(jnp.int32, (128, 256), 0)
+        lane = lax.broadcasted_iota(jnp.int32, (128, 256), 1)
+        even = jnp.where(lane == 2 * row, 1.0, 0.0).astype(BF)
+        odd = jnp.where(lane == 2 * row + 1, 1.0, 0.0).astype(BF)
+        for k in range(T2 // 128):
+            rows = slice(k * 128, (k + 1) * 128)
+            value = tn(r.mel_o[rows, 0:128], even) + tn(r.mel_o[rows, 128:256], odd)
+            r.mel[0, :, k * 256 : (k + 1) * 256] = value[0:mels, :]
+        copy.wait()
+
+    vmem, anywhere = pl.BlockSpec(memory_space=pltpu.VMEM), pl.BlockSpec(memory_space=pl.ANY)
+    done = pl.pallas_call(
+        kernel,
+        name="finish",
+        out_shape=[jax.ShapeDtypeStruct(*o) for o in outs.values()],
+        in_specs=[anywhere if n == "enc_o" else vmem for n in ins],
+        out_specs=[anywhere if n == "enc" else vmem for n in outs],
+        scratch_shapes=[pltpu.SemaphoreType.DMA],
+        compiler_params=pltpu.CompilerParams(vmem_limit_bytes=VMEM_LIMIT),
+    )(*got.values())
+    return dict(zip(outs, done))
+
+
+def sine_tables(frames, channels, fine):
     half_width = channels // 2
-    increment = math.log(10000.0) / (half_width - 1)
-    inverse = jnp.exp(-increment * jnp.arange(half_width, dtype=F32))
-    angles = positions.astype(F32)[:, None] * inverse[None, :]
-    return jnp.concatenate([jnp.sin(angles), jnp.cos(angles)], axis=1)
+    rate = np.exp(-(math.log(10000.0) / (half_width - 1)) * np.arange(half_width))
+    small = np.arange(fine)[:, None] * rate[None, :]
+    large = np.arange(0, frames, fine)[:, None] * rate[None, :]
+    table = dict(fine_s=np.sin(small), fine_c=np.cos(small), coarse_s=np.sin(large), coarse_c=np.cos(large))
+    return {n: jnp.asarray(t, F32) for n, t in table.items()}
 
 
 def on_device(
@@ -833,50 +1022,43 @@
     cotangent,
     speech_mask,
 ):
-    mel = mel_input[0]
-    mels = mel.shape[0]
+    mels = mel_input.shape[1]
     T, D = cotangent.shape[1] // 2, cotangent.shape[2]
     F2 = up_weight.shape[1]
     side, half = F2 // D, D // 2
     bits = (lax.axis_size("dp") - 1).bit_length()
-    c, m = lax.axis_index("seq"), lax.axis_index("mp")
-    sub = jnp.bitwise_xor(c, m)
-
-    low = lax.ppermute(mel[:, -2:], "seq", [(0, 1)])
-    high = lax.ppermute(mel[:, :2], "seq", [(1, 0)])
-    window = lax.dynamic_slice_in_dim(
-        jnp.concatenate([low, mel, high], axis=1), sub * 2 * T, 2 * T + 4, axis=1
+    m = lax.axis_index("mp")
+    lanes = -(-3 * mels // 128) * 128
+    near = dict(
+        w1=conv1_weight,
+        mask=speech_mask,
+        qkvb=qkv_bias,
+        upb=up_bias,
+        c1b=conv1_bias,
+        c2b=conv2_bias,
+        n1g=norm1_gain,
+        n1b=norm1_bias,
+        oub=out_bias,
+        n2g=norm2_gain,
+        n2b=norm2_bias,
+        dnb=down_bias,
     )
-    pairs = window.T.reshape(T + 2, 2 * mels)
-    xe = jnp.concatenate([pairs[0:T, mels:], pairs[1 : T + 1]], axis=1)
-    xo = jnp.concatenate([pairs[1 : T + 1], pairs[2 : T + 2, :mels]], axis=1)
-    xh = jnp.concatenate([pairs[0:1], pairs[1:2, :mels]], axis=1)
-    lanes = -(-3 * mels // 128) * 128
-    xe = jnp.pad(xe, ((0, 0), (0, lanes - 3 * mels)))
-    xo = jnp.pad(xo, ((0, 0), (0, lanes - 3 * mels)))
-    xh = jnp.pad(xh, ((7, 8), (0, lanes - 3 * mels)))
-    w1 = jnp.pad(conv1_weight.reshape(3 * mels, D), ((0, lanes - 3 * mels), (0, 0)))
-    w1p = jnp.pad(conv1_weight, ((0, 0), (0, 128 - mels), (0, 0)))
-    pos = sinusoids((c * 2 + sub) * T + jnp.arange(T, dtype=jnp.int32), D)
-
-    table = [conv1_bias, conv2_bias, norm1_gain, norm1_bias, out_bias, norm2_gain, norm2_bias]
-    table = jnp.stack(table + [down_bias]).astype(F32)
-    mine = jnp.zeros((8, D), F32)
-    mine = lax.dynamic_update_slice(mine, qkv_bias.astype(F32), (0, m * half))
-    mine = lax.dynamic_update_slice(mine, up_bias.astype(F32).reshape(side, D), (2 + m * side, 0))
-    vecs = jnp.concatenate([table, mine], axis=0)
-
-    cot = lax.dynamic_slice_in_dim(cotangent[0], sub * T, T, axis=0)
-    mask = lax.dynamic_slice_in_dim(speech_mask[0], sub * T, T, axis=0)
-    bg = cot * mask.astype(BF)[:, None]
-
+    near.update(sine_tables(4 * T, D, 32))
     got = run_layer(
         bits,
-        dict(xe=xe, xo=xo, xh=xh, w1=w1, w1p=w1p, w2=conv2_weight, vecs_in=vecs, bg=bg),
-        dict(pos=pos, wqkv_l=qkv_weight, wo_l=out_weight, up_l=up_weight, down_l=down_weight),
+        near,
+        dict(
+            mel=mel_input,
+            cot=cotangent,
+            w2_l=conv2_weight,
+            wqkv_l=qkv_weight,
+            wo_l=out_weight,
+            up_l=up_weight,
+            down_l=down_weight,
+        ),
         dict(
             enc_o=((2 * T, D), BF),
-            mel_o=((2 * T, 256), F32),
+            mel_o=((2 * T, 256), BF),
             down_o=((F2, D), BF),
             up_o=((D, F2), BF),
             out_o=((half, D), BF),
@@ -890,28 +1072,28 @@
         F2,
         lanes,
     )
-    small = got["small_o"]
+    small = got.pop("small_o")
     own_half = lax.dynamic_slice_in_dim(small[QB : QB + 2], m * half, half, axis=1)
     own_up = lax.dynamic_slice_in_dim(small[UPB : UPB + 2 * side], m * side, side, axis=0).reshape(-1)
-    melg = got["mel_o"].reshape(4 * T, 128)[:, :mels].T[None]
+    done = run_finish(got, mels, side)
     return (
-        got["enc_o"][None],
-        melg,
-        got["c1_o"][: 3 * mels].astype(F32).reshape(3, mels, D),
+        done["enc"],
+        done["mel"],
+        done["c1"],
         small[C1B],
-        got["c2_o"].astype(F32).reshape(3, D, D),
+        done["c2"],
         small[C2B],
         small[N1G],
         small[N1B],
-        got["qkv_o"].astype(F32),
+        done["qkv"],
         own_half,
-        got["out_o"].astype(F32),
+        done["out"],
         small[OUB],
         small[N2G],
         small[N2B],
-        got["up_o"].astype(F32),
+        done["up"],
         own_up,
-        got["down_o"].astype(F32),
+        done["down"],
         small[DNB],
     )
 

time: 254 us -> 259 us (1.020)
  Pallas kernels: 214 us -> 254 us
  other arithmetic: 18.6 us -> 0 us
  local copies, waits for them, and re-layouts: 16.5 us -> 4.24 us
  starting transfers between devices: 3.64 us -> 0 us
    pallas_call x0 -> x1, Pallas kernels: none -> 39.4 us  [run_finish(): pl.pallas_call(kernel, name='finish', out_shape=[jax.ShapeDtypeStruct(*o)...]
    convert_element_type x7 -> x0, other arithmetic: 6.02 us -> none  [the longest x1 1.61 us: on_device(): got['down_o'].astype(F32)]
    another operation x9 -> x0, local copies, waits for them, and re-layouts: 5.49 us -> none  [on_device(): table = jnp.stack(table + [down_bias]).astype(F32)]
    reshape x2 -> x0, other arithmetic: 4.44 us -> none  [the longest x1 3.6 us: on_device(): got['c2_o'].astype(F32).reshape(3, D, D)]
    ppermute x2 -> x0, starting transfers between devices: 3.64 us -> none  [the longest x1 2.35 us: on_device(): low = lax.ppermute(mel[:, -2:], 'seq', [(0, 1)])]
    concatenate x4 -> x0, other arithmetic: 3.46 us -> none  [the longest x1 1.13 us: sinusoids(): return jnp.concatenate([jnp.sin(angles), jnp.cos(angles)], axis=1)]
  transfers between devices with their start and end apart: 2 -> 0, of which waited for: 0 -> 0; matrix products, arithmetic and copies ran while one was open for 6% -> 0% of each run, Pallas kernels for 0% -> 0%
where the time goes in v3:
time: 259 us
  Pallas kernels  254 us (98%)
  local copies, waits for them, and re-layouts  4.24 us (2%)
    pallas_call x1, Pallas kernels, run_layer(): pl.pallas_call(kernel, name='layer', out_shape=[jax.ShapeDtypeStruct(*o)...  214 us
    pallas_call x1, Pallas kernels, run_finish(): pl.pallas_call(kernel, name='finish', out_shape=[jax.ShapeDtypeStruct(*o)...  39.4 us

profile of v3, /device:TPU:0, one launch (start us, length us, event | category | flops | bytes accessed | tf_op | source)
XLA Modules:
  0.0 258.7 jit_solution(5785648891407486493)
XLA Ops:
  0.7 214.2 %layer.1 = (bf16[1024,512]{1,0:T(8,128)(2,1)}, bf16[1024,256]{1,0:T(8,128)(2,1)}, bf16[1024,512]{1,0:T(8,128)(2,1)}, bf16[512,1024]{1,0:T(8,128)(2,1)}, bf16[256...) custom-call(bf16[3,80,512]{2,1,0:T(8,128)(2,1)} %refs_0_.1, ...), custom_call_target="tpu_custom_call" | custom-call | tf_op jit(solution)/shard_map/layer/pallas_call | solution.py:922
  214.8 0.7 slice.34
  215.6 0.6 constant_dynamic-slice_fusion
  216.1 0.7 slice.38
  216.9 1.6 fusion
  218.5 0.6 copy.41
  219.1 39.4 %finish.1 = (bf16[1,1024,512]{2,1,0:T(8,128)(2,1)}, f32[1,80,2048]{2,1,0:T(8,128)}, f32[3,80,512]{2,1,0:T(8,128)}, f32[3,512,512]{2,1,0:T(8,128)}, f32[3,512,256...) custom-call(bf16[1024,512]{1,0:T(8,128)(2,1)} %get-tuple-element.35.refs_0_, ...), custom_call_target="tpu_custom_call" | custom-call | tf_op jit(solution)/shard_map/finish/pallas_call | solution.py:983
  (1 shorter events, 0.0 us)

commit v4 on v3

--- a/solution.py
+++ b/solution.py
@@ -13,7 +13,7 @@
 BF = jnp.bfloat16
 F32 = jnp.float32
 MESH = pl.DeviceIdType.MESH
-VMEM_LIMIT = 60 * 1024 * 1024
+VMEM_LIMIT = 61 * 1024 * 1024
 C1B, C2B, N1G, N1B, OUB, N2G, N2B, DNB, QB, VB, UPB = range(11)
 
 
@@ -313,10 +313,11 @@
     def one(i, accs):
         rows = pl.ds(pl.multiple_of(i * 32, 32), 32)
         mid = r.mid[rows, :]
-        r.enc[rows, :] = (mid + r.ffo[rows, :] + vec(r, DNB)).astype(BF)
+        enc = (mid + r.ffo[rows, :] + vec(r, DNB)).astype(BF)
         hat, inv = normal(mid)
         grad = r.ntg[rows, :]
         smg = r.bg[rows, :].astype(F32) + normal_pull(grad * vec(r, N2G), hat, inv)
+        r.enc[rows, :] = enc
         r.smg[rows, :] = smg
         attg = smg.astype(BF)
         r.attg[rows, :] = attg
@@ -646,52 +647,47 @@
         r.vecs[k : k + 1, :] = getattr(r, n)[...].astype(F32).reshape(1, D)
     net.greet()
     mel_own = net.here(r.mel.at[0], r.melbuf.at[0:mels, 128 : 128 + span])
-    src = pl.ds(pl.multiple_of((1 - c) * (span - 128), 128), 128)
-    dst = pl.ds(pl.multiple_of(c * (span + 128), 128), 128)
-    mel_rim = net.send(r.mel.at[0, :, src], r.melbuf.at[0:mels, dst], "c")
-    piece = rows16(c * half, half)
-    qkv_y = net.send(r.wqkv_l.at[:, piece], r.wqkv.at[m, :, piece], "y")
-    vec_copy = net.send(r.vec_mine, r.vec_got, "y")
+    qkv_own = net.here(r.wqkv_l, r.wqkv.at[m])
     w2_own = net.here(r.w2_l, r.w2)
     own = [
-        net.here(r.wqkv_l, r.wqkv.at[m]),
-        net.here(r.cot.at[0, rows_of_mine], r.bg),
         net.here(r.wo_l, r.wo.at[rows16(m * half, half)]),
         net.here(r.up_l, r.up.at[m]),
         net.here(r.down_l, r.down.at[rows16(m * F2, F2)]),
+        net.here(r.cot.at[0, rows_of_mine], r.bg),
     ]
+    vec_copy = net.send(r.vec_mine, r.vec_got, "y")
+    mel_own.wait()
+    src = pl.ds(pl.multiple_of(128 + (1 - c) * (span - 128), 128), 128)
+    dst = pl.ds(pl.multiple_of(c * (span + 128), 128), 128)
+    mel_rim = net.send(r.melbuf.at[0:mels, src], r.melbuf.at[0:mels, dst], "c")
+    piece = rows16(c * half, half)
+    qkv_own.wait()
+    mine = r.wqkv.at[m, :, piece]
+    qkv_y = net.send(mine, mine, "y")
 
     p = 4 * c + 2 * net.bit(0) + net.bit(1) if bits > 1 else 2 * c + net.bit(0)
     cuts = 8 if bits > 1 else 4
 
-    def ff_parts(of, at, count, local):
+    def pass_on(of, at, count, dim):
         def cut(n, base):
             return rows16(base + at * (n // cuts), count * (n // cuts))
 
-        if local:
-            return [r.wo_l.at[cut(half, 0)], r.up_l.at[cut(D, 0)], r.down_l.at[cut(F2, 0)]]
-        return [r.wo.at[cut(half, of * half)], r.up.at[of, cut(D, 0)], r.down.at[cut(F2, of * F2)]]
-
-    def pass_on(at, count, dim):
-        return [net.send(x, x, dim) for x in ff_parts(1 - m, at, count, False)]
+        parts = [r.wo.at[cut(half, of * half)], r.up.at[of, cut(D, 0)], r.down.at[cut(F2, of * F2)]]
+        return [net.send(x, x, dim) for x in parts]
 
     r.small[...] = jnp.zeros_like(r.small)
-    mel_own.wait()
     mel_rim.wait()
     stage_mel_rows(r, sub)
     stage_first(r, jnp.logical_and(c == 0, m == 0))
     qkv_y.wait()
     arrived = r.wqkv.at[1 - m, :, piece]
     qkv_c = net.send(arrived, arrived, "c")
-    ff = [
-        net.send(a, b, "y")
-        for a, b in zip(ff_parts(m, p, 1, True), ff_parts(m, p, 1, False))
-    ]
+    wait_all(own)
+    ff = pass_on(m, p, 1, "y")
     w2_own.wait()
     stage_second(r, quarter(net))
     vec_copy.wait()
     r.vecs[8:16, :] = r.vec_mine[...] + r.vec_got[...]
-    wait_all(own[0:1])
     qkv_c.wait()
 
     def block(slot, part):
@@ -700,27 +696,25 @@
     kv_y, kv_c = [], []
     for part in range(2):
         stage_qkv(r, (1 + part,))
+        kv_c.append(net.send(block(0, part), block(1, part), "c"))
         kv_y.append(net.send(block(0, part), block(2, part), "y"))
-        kv_c.append(net.send(block(0, part), block(1, part), "c"))
     stage_qkv(r, (0,))
     wait_all(ff)
-    ff = pass_on(p, 1, 1) if bits > 1 else []
-    wait_all(own[1:2])
+    ff = pass_on(1 - m, p, 1, 1) if bits > 1 else []
     stage_mask(r, sub)
     attend_block(r, 0)
     wait_all(ff)
-    ff = pass_on((p // 2) * 2 if bits > 1 else p, 2 if bits > 1 else 1, 0)
+    ff = pass_on(1 - m, (p // 2) * 2 if bits > 1 else p, 2 if bits > 1 else 1, 0)
     wait_all(kv_c)
     attend_block(r, 1)
     wait_all(ff)
-    ff = pass_on(c * (cuts // 2), cuts // 2, "c")
+    ff = pass_on(1 - m, c * (cuts // 2), cuts // 2, "c")
     wait_all(kv_y)
     kv_d = [net.send(block(2, part), block(3, part), "c") for part in range(2)]
     attend_block(r, 2)
     wait_all(kv_d)
     attend_block(r, 3)
     attend_end(r)
-    wait_all(own[2:])
     wait_all(ff)
     stage_mid(r)
     stage_ff(r)
@@ -739,7 +733,7 @@
 
     def send_enc():
         enc.append(net.here(r.enc, r.enc_o.at[rows_of_mine]))
-        enc.append(net.send(r.enc, r.enc_o.at[rows_of_mine], "y"))
+        enc.append(net.send(r.enc, r.enc_got, "y"))
 
     moves = {
         1: (up_sum,),
@@ -811,9 +805,12 @@
     advance(c1_sum, vec_sum)
     wait_all(rim)
     stage_mel(r, pick_next(net, r.slots.at[1]), pick_prev(net, r.slots.at[2]))
+    rows_of_yours = rows16((1 - sub) * T, T)
+    mel_y = net.send(r.melg, r.melg_got, "y")
+    wait_all(enc)
     ends = [
+        net.here(r.enc_got, r.enc_o.at[rows_of_yours]),
         net.here(r.melg, r.mel_o.at[rows_of_mine]),
-        net.send(r.melg, r.mel_o.at[rows_of_mine], "y"),
     ]
     drain(c1_sum, vec_sum, c2a_sum, c2b_sum, qkv_sum, up_sum, down_sum)
 
@@ -833,7 +830,8 @@
     ends.append(net.here(r.done_c2b, r.c2_o.at[3 * half : 6 * half]))
     ends.append(net.here(r.done_c1, r.c1_o))
     ends.append(net.here(r.small, r.small_o))
-    wait_all(enc)
+    mel_y.wait()
+    ends.append(net.here(r.melg_got, r.mel_o.at[rows_of_yours]))
     wait_all(ends)
 
 
@@ -892,8 +890,9 @@
         from_d=((2, D, T), BF),
         from_y=((2, D, T), BF),
         from_s=((2, D, T), BF),
-        enc=(td, BF),
+        enc_got=(td, BF),
         melg=((T, 256), BF),
+        melg_got=((T, 256), BF),
         small=((16, D), F32),
         got_small=((bits + 2, 16, D), F32),
         slots=((3, 2, 16, D), BF),
@@ -912,7 +911,7 @@
         r = Box()
         for n, ref in zip(names, refs):
             setattr(r, n, ref)
-        r.odd, r.smg, r.sg, r.fe, r.fo, r.dqt = r.shift, r.mid, r.ntwo, r.act, r.ing, r.ffo
+        r.odd, r.smg, r.sg, r.fe, r.fo, r.dqt, r.enc = r.shift, r.mid, r.ntwo, r.act, r.ing, r.ffo, r.bg
         if alias:
             r.g_qkv, r.g_c2 = r.kv.at[0 : 6 * half], r.kv.at[6 * half : 12 * half]
         r.g_c2a, r.g_c2b = r.g_c2.at[0 : 3 * half], r.g_c2.at[3 * half : 6 * half]
@@ -944,24 +943,27 @@
         c1=((3, mels, D), F32),
         c2=((3, D, D), F32),
         qkv=((3, D, half), F32),
+        qkvb=((2, half), F32),
         out=((half, D), F32),
         up=((D, side * D), F32),
+        upb=((side * D,), F32),
         down=((side * D, D), F32),
     )
+    outs.update({n: ((D,), F32) for n in ROW_BIASES})
 
     def kernel(*refs):
         r = Box()
-        for n, ref in zip(ins + list(outs) + ["sem"], refs):
+        for n, ref in zip(ins + list(outs), refs):
             setattr(r, n, ref)
-        copy = pltpu.make_async_copy(r.enc_o, r.enc.at[0], r.sem)
-        copy.start()
+        m = lax.axis_index("mp")
 
         def cast(src, dst):
             def one(rows):
-                dst[rows, :] = src[rows, :].astype(F32)
-
-            rows_loop(src.shape[0], 64, one)
-
+                dst[rows, :] = src[rows, :].astype(dst.dtype)
+
+            rows_loop(src.shape[0], 256, one)
+
+        cast(r.enc_o, r.enc.at[0])
         cast(r.down_o, r.down)
         cast(r.up_o, r.up)
         cast(r.out_o, r.out)
@@ -977,16 +979,19 @@
             rows = slice(k * 128, (k + 1) * 128)
             value = tn(r.mel_o[rows, 0:128], even) + tn(r.mel_o[rows, 128:256], odd)
             r.mel[0, :, k * 256 : (k + 1) * 256] = value[0:mels, :]
-        copy.wait()
-
-    vmem, anywhere = pl.BlockSpec(memory_space=pltpu.VMEM), pl.BlockSpec(memory_space=pl.ANY)
+        for k, n in enumerate(ROW_BIASES):
+            getattr(r, n)[...] = r.small_o[k : k + 1, :].reshape(D)
+        r.qkvb[...] = r.small_o[QB : QB + 2, pl.ds(pl.multiple_of(m * half, 128), half)]
+        for k in range(side):
+            r.upb[k * D : (k + 1) * D] = r.small_o[pl.ds(UPB + m * side + k, 1), :].reshape(D)
+
+    vmem = pl.BlockSpec(memory_space=pltpu.VMEM)
     done = pl.pallas_call(
         kernel,
         name="finish",
         out_shape=[jax.ShapeDtypeStruct(*o) for o in outs.values()],
-        in_specs=[anywhere if n == "enc_o" else vmem for n in ins],
-        out_specs=[anywhere if n == "enc" else vmem for n in outs],
-        scratch_shapes=[pltpu.SemaphoreType.DMA],
+        in_specs=[vmem] * len(ins),
+        out_specs=[vmem] * len(outs),
         compiler_params=pltpu.CompilerParams(vmem_limit_bytes=VMEM_LIMIT),
     )(*got.values())
     return dict(zip(outs, done))
@@ -1027,7 +1032,6 @@
     F2 = up_weight.shape[1]
     side, half = F2 // D, D // 2
     bits = (lax.axis_size("dp") - 1).bit_length()
-    m = lax.axis_index("mp")
     lanes = -(-3 * mels // 128) * 128
     near = dict(
         w1=conv1_weight,
@@ -1072,30 +1076,10 @@
         F2,
         lanes,
     )
-    small = got.pop("small_o")
-    own_half = lax.dynamic_slice_in_dim(small[QB : QB + 2], m * half, half, axis=1)
-    own_up = lax.dynamic_slice_in_dim(small[UPB : UPB + 2 * side], m * side, side, axis=0).reshape(-1)
     done = run_finish(got, mels, side)
-    return (
-        done["enc"],
-        done["mel"],
-        done["c1"],
-        small[C1B],
-        done["c2"],
-        small[C2B],
-        small[N1G],
-        small[N1B],
-        done["qkv"],
-        own_half,
-        done["out"],
-        small[OUB],
-        small[N2G],
-        small[N2B],
-        done["up"],
-        own_up,
-        done["down"],
-        small[DNB],
-    )
+    names = ("enc", "mel", "c1", "c1b", "c2", "c2b", "n1g", "n1b", "qkv", "qkvb")
+    names += ("out", "oub", "n2g", "n2b", "up", "upb", "down", "dnb")
+    return tuple(done[n] for n in names)
 
 
 def solution(mesh):

time: 259 us -> 224 us (0.86)
  Pallas kernels: 254 us -> 223 us
  local copies, waits for them, and re-layouts: 4.24 us -> 0 us
    pallas_call x1, Pallas kernels: 39.4 us -> 7.97 us  [run_finish(): pl.pallas_call(kernel, name='finish', out_shape=[jax.ShapeDtypeStruct(*o)...]
    slice x3 -> x0, local copies, waits for them, and re-layouts: 3.06 us -> none  [the longest x1 1.62 us: on_device(): small[DNB]]
where the time goes in v4:
time: 224 us; the launch traced here: 223 us
  Pallas kernels  223 us (100%)
    pallas_call x1, Pallas kernels, run_layer(): pl.pallas_call(kernel, name='layer', out_shape=[jax.ShapeDtypeStruct(*o)...  215 us
    pallas_call x1, Pallas kernels, run_finish(): pl.pallas_call(kernel, name='finish', out_shape=[jax.ShapeDtypeStruct(*o)...  7.97 us

profile of v4, /device:TPU:0, one launch (start us, length us, event | category | flops | bytes accessed | tf_op | source)
XLA Modules:
  0.0 223.3 jit_solution(5554009931220781394)
XLA Ops:
  0.7 214.6 %layer.1 = (bf16[1024,512]{1,0:T(8,128)(2,1)}, bf16[1024,256]{1,0:T(8,128)(2,1)}, bf16[1024,512]{1,0:T(8,128)(2,1)}, bf16[512,1024]{1,0:T(8,128)(2,1)}, bf16[256...) custom-call(bf16[3,80,512]{2,1,0:T(8,128)(2,1)} %refs_0_.1, ...), custom_call_target="tpu_custom_call" | custom-call | tf_op jit(solution)/shard_map/layer/pallas_call | solution.py:921
  215.2 8.0 %finish.1 = (bf16[1,1024,512]{2,1,0:T(8,128)(2,1)}, f32[1,80,2048]{2,1,0:T(8,128)}, f32[3,80,512]{2,1,0:T(8,128)}, f32[3,512,512]{2,1,0:T(8,128)}, f32[3,512,256...) custom-call(bf16[1024,512]{1,0:T(8,128)(2,1)} %get-tuple-element.45., ...), custom_call_target="tpu_custom_call" | custom-call | tf_op jit(solution)/shard_map/finish/pallas_call | solution.py:989

commit v5 on v4

--- a/solution.py
+++ b/solution.py
@@ -182,76 +182,88 @@
     rows_loop(T, 32, one)
 
 
-def stage_qkv(r, parts):
+def stage_qkv(r, part):
     T, D = r.stream.shape
-    half = D // 2
-    normed = r.normed[...]
-    for part in parts:
-        bias, scale = ((QB, HEAD**-0.5), (None, 1.0), (VB, 1.0))[part]
-        for m in range(2):
-            value = nn(normed, r.wqkv[m, part])
-            if bias is not None:
-                value = value + r.vecs[bias : bias + 1, m * half : (m + 1) * half]
-            value = (value.astype(BF).astype(F32) * scale).T.astype(BF)
-            if part == 0:
-                r.qt[m * half : (m + 1) * half, :] = value
-            else:
-                at = (part - 1) * D + m * half
-                r.kv[at : at + half, :] = value
-
-
-def head_rows(h):
-    return pl.ds(pl.multiple_of(h * HEAD, HEAD), HEAD)
-
-
-def block_rows(r, slot, part, h):
-    D = r.qt.shape[0]
-    return pl.ds(pl.multiple_of((2 * slot + part) * D + h * HEAD, HEAD), HEAD)
-
-
-def attend_block(r, slot):
-    D, T = r.qt.shape
-    first = slot == 0
+    half, qr = D // 2, D // 4
+    bias, scale = ((QB, HEAD**-0.5), (None, 1.0), (VB, 1.0))[part]
+    for h in range(2):
+        value = nn(r.normed[...], r.wqkv[h, part])
+        if bias is not None:
+            value = value + r.vecs[bias : bias + 1, h * half : (h + 1) * half]
+        value = (value.astype(BF).astype(F32) * scale).T.astype(BF)
+        for k in range(2):
+            at = (3 * (3 + k) + part) * half + h * qr
+            r.kv[at : at + qr, :] = value[k * qr : (k + 1) * qr, :]
+
+
+def at_head(start, h):
+    return pl.ds(pl.multiple_of(start + h * HEAD, HEAD), HEAD)
+
+
+def head_loop(steps, hooks, body):
+    def one(step, carry):
+        for at, todo in hooks.items():
+
+            @pl.when(step == at)
+            def _(todo=todo):
+                for act in todo:
+                    act()
+
+        body(step)
+        return carry
+
+    lax.fori_loop(0, steps, one, 0)
+
+
+def attend(r, c, hooks):
+    S, T = r.kv.shape[0] // 15, r.kv.shape[1]
+    heads = S // HEAD
+    r.top[...] = jnp.full(r.top.shape, -jnp.inf, F32)
+    r.total[...] = jnp.zeros(r.total.shape, F32)
+    r.mixt[...] = jnp.zeros(r.mixt.shape, F32)
+
+    def body(step):
+        g, h = step // heads, step % heads
+        own = (3 - g) // 3
+        slot = own * (3 + c) + (1 - own) * ((g + 1) % 3)
+        k = r.kv[at_head((3 * slot + 1) * S, h), :]
+        v = r.kv[at_head((3 * slot + 2) * S, h), :]
+        for i, home in enumerate((3 + c, 2)):
+            q = r.kv[at_head(3 * home * S, h), :]
+            s = tn(k, q)
+            before = r.top[i * heads + h]
+            top = jnp.maximum(before, jnp.max(s, axis=0, keepdims=True))
+            p = jnp.exp(s - top)
+            keep = jnp.exp(before - top)
+            rows = at_head(i * S, h)
+            r.top[i * heads + h] = top
+            r.total[i * heads + h] = keep * r.total[i * heads + h] + jnp.sum(p, axis=0, keepdims=True)
+            r.mixt[rows, :] = keep * r.mixt[rows, :] + nn(v, p.astype(BF))
+
+    head_loop(4 * heads, hooks, body)
+
+
+def attend_end(r, i):
+    S = r.kv.shape[0] // 15
+    heads = S // HEAD
 
     def one(h, carry):
-        rows = head_rows(h)
-        s = tn(r.kv[block_rows(r, slot, 0, h), :], r.qt[rows, :])
-        top = jnp.max(s, axis=0, keepdims=True)
-        if not first:
-            top = jnp.maximum(top, r.top[h])
-        p = jnp.exp(s - top)
-        total = jnp.sum(p, axis=0, keepdims=True)
-        mixed = nn(r.kv[block_rows(r, slot, 1, h), :], p.astype(BF))
-        if not first:
-            keep = jnp.exp(r.top[h] - top)
-            total = total + keep * r.total[h]
-            mixed = mixed + keep * r.mixt[rows, :]
-        r.top[h] = top
-        r.total[h] = total
-        r.mixt[rows, :] = mixed
-        return carry
-
-    lax.fori_loop(0, D // HEAD, one, 0)
-
-
-def attend_end(r):
-    D, T = r.qt.shape
-
-    def one(h, carry):
-        rows = head_rows(h)
-        total = r.total[h]
+        rows = at_head(i * S, h)
+        total = r.total[i * heads + h]
         value = r.mixt[rows, :] * (1.0 / total)
         r.mixt[rows, :] = value
         r.mixb[rows, :] = value.astype(BF)
-        r.top[h] = r.top[h] + jnp.log(total)
+        r.top[i * heads + h] = r.top[i * heads + h] + jnp.log(total)
         return carry
 
-    lax.fori_loop(0, D // HEAD, one, 0)
-
-
-def stage_mid(r):
+    lax.fori_loop(0, heads, one, 0)
+
+
+def stage_mid(r, c):
     T, D = r.stream.shape
-    r.tmp[...] = tn(r.mixb[...], r.wo[...])
+    half = D // 2
+    r.tmp[...] = tn(r.mixb[0:half, :], r.wo[rows16(c * half, half), :])
+    r.tmp[...] += tn(r.mix_got[...], r.wo[rows16((1 - c) * half, half), :])
 
     def one(rows):
         mid = r.stream[rows, :] + r.tmp[rows, :] + vec(r, OUB)
@@ -328,68 +340,96 @@
     add_small(r, N2G, gain)
     add_small(r, N2B, bias)
     add_small(r, OUB, out_bias)
-    attg = r.attg[...]
-    r.dot[...] = nt(r.wo[...], attg).astype(BF)
-    gout = nn(r.mixb[...], attg).astype(BF)
-    rows, half = r.g_up.shape[0] // 2, D // 2
-    r.g_up[rows - half : rows, :] = gout[0:half, :]
-    r.g_up[2 * rows - half : 2 * rows, :] = gout[half:D, :]
-
-    def head(h, carry):
-        rows = head_rows(h)
-        r.diag[h] = jnp.sum(r.dot[rows, :].astype(F32) * r.mixt[rows, :], axis=0, keepdims=True)
+
+
+def stage_do(r, c, own):
+    half = r.attg.shape[1] // 2
+    k = c if own else 1 - c
+    value = nt(r.wo[rows16(k * half, half), :], r.attg[...]).astype(BF)
+    if own:
+        r.dot[0:half, :] = value
+    else:
+        r.dot_out[...] = value
+
+
+def stage_out_weights(r, c):
+    D = r.attg.shape[1]
+    half, qr = D // 2, D // 4
+    rows = r.g_up.shape[0] // 2
+    for k, mix in ((c, r.mixb[0:half, :]), (1 - c, r.mix_got[...])):
+        value = nn(mix, r.attg[...]).astype(BF)
+        for h in range(2):
+            r.g_up[rows16(h * rows + rows - half + k * qr, qr), :] = value[h * qr : (h + 1) * qr, :]
+
+
+def stage_diag(r, i):
+    S = r.kv.shape[0] // 15
+    heads = S // HEAD
+
+    def one(h, carry):
+        rows = at_head(i * S, h)
+        value = r.dot[rows, :].astype(F32) * r.mixt[rows, :]
+        r.diag[i * heads + h] = jnp.sum(value, axis=0, keepdims=True)
         return carry
 
-    lax.fori_loop(0, D // HEAD, head, 0)
-
-
-def pull_block(r, slot, dkv, hook):
-    D, T = r.qt.shape
-    first = slot == 3
-    H = D // HEAD
-
-    def one(h, carry):
-        rows = head_rows(h)
-        k, v = r.kv[block_rows(r, slot, 0, h), :], r.kv[block_rows(r, slot, 1, h), :]
-        q, do = r.qt[rows, :], r.dot[rows, :]
-        p = jnp.exp(tn(k, q) - r.top[h])
-        ds = (p * (tn(v, do) - r.diag[h])).astype(BF)
-        dkv[1, rows, :] = nt(do, p.astype(BF)).astype(dkv.dtype)
-        dkv[0, rows, :] = nt(q, ds).astype(dkv.dtype)
-        dq = nn(k, ds)
-        if first:
-            r.dqt[rows, :] = dq
-        else:
-            r.dqt[rows, :] += dq
-        return carry
-
-    for part in range(4):
-        lax.fori_loop(part * H // 4, (part + 1) * H // 4, one, 0)
-        hook()
+    lax.fori_loop(0, heads, one, 0)
+
+
+def attend_pull(r, c, hooks):
+    S, T = r.kv.shape[0] // 15, r.kv.shape[1]
+    heads = S // HEAD
+    r.dqt[...] = jnp.zeros(r.dqt.shape, F32)
+
+    def body(step):
+        g, h = step // heads, step % heads
+        slot = g + (g // 3) * c
+        k = r.kv[at_head((3 * slot + 1) * S, h), :]
+        v = r.kv[at_head((3 * slot + 2) * S, h), :]
+        dk, dv = None, None
+        for i, home in enumerate((3 + c, 2)):
+            q = r.kv[at_head(3 * home * S, h), :]
+            rows = at_head(i * S, h)
+            do = r.dot[rows, :]
+            p = jnp.exp(tn(k, q) - r.top[i * heads + h])
+            ds = (p * (tn(v, do) - r.diag[i * heads + h])).astype(BF)
+            dv_i, dk_i = nt(do, p.astype(BF)), nt(q, ds)
+            dk, dv = (dk_i, dv_i) if dk is None else (dk + dk_i, dv + dv_i)
+            r.dqt[rows, :] += nn(k, ds)
+        r.dkv[at_head(2 * g * S, h), :] = dk.astype(BF)
+        r.dkv[at_head((2 * g + 1) * S, h), :] = dv.astype(BF)
+
+    head_loop(4 * heads, hooks, body)
+
+
+def piece_of(r, part, h):
+    D, qr = r.attg.shape[1], r.attg.shape[1] // 4
+    at = part * D + h * qr
+    return jnp.concatenate([r.dsum[at : at + qr, :], r.dsum[at + 2 * qr : at + 3 * qr, :]], axis=0)
 
 
 def stage_qkv_weights(r):
     T, D = r.stream.shape
     half = D // 2
-    normedt = r.normed[...].astype(F32).T.astype(BF)
+    r.normedt[...] = r.normed[...].astype(F32).T.astype(BF)
     ones = jnp.ones((8, T), BF)
-    for part, ref in enumerate((r.dqb, r.dkb, r.dvb)):
-        if part != 1:
-            add_small(r, QB if part == 0 else VB, nt(ones, ref[...])[0:1, :])
-        for m in range(2):
-            grad = nt(normedt, ref[m * half : (m + 1) * half, :]).astype(BF)
-            at = (3 * m + part) * half
+    for part in range(3):
+        for h in range(2):
+            piece = piece_of(r, part, h)
+            if part != 1:
+                row = QB if part == 0 else VB
+                r.small[row : row + 1, h * half : (h + 1) * half] = nt(ones, piece)[0:1, :]
+            grad = nt(r.normedt[...], piece).astype(BF)
+            at = (3 * h + part) * half
             r.g_qkv[at : at + half, 0:half] = grad[0:half, :]
             r.g_qkv[at : at + half, half:D] = grad[half:D, :]
 
 
 def stage_qkv_pull(r):
     T, D = r.stream.shape
-    half = D // 2
     total = None
-    for part, ref in enumerate((r.dqb, r.dkb, r.dvb)):
-        for m in range(2):
-            back = nn(r.wqkv[m, part], ref[m * half : (m + 1) * half, :])
+    for part in range(3):
+        for h in range(2):
+            back = nn(r.wqkv[h, part], piece_of(r, part, h))
             total = back if total is None else total + back
     r.tmp[...] = total.T
 
@@ -473,20 +513,22 @@
             return (self.d, 1 - self.c, self.m)
         if dim == "y":
             return (self.d, self.c, 1 - self.m)
+        if dim == "cy":
+            return (self.d, 1 - self.c, 1 - self.m)
         step = 1 << dim
         return (self.d + step - 2 * step * self.bit(dim), self.c, self.m)
 
     def greet(self):
         barrier = pltpu.get_barrier_semaphore()
-        dims = ["c", "y"] + list(range(self.bits))
+        dims = ["c", "y", "cy"] + list(range(self.bits))
         for dim in dims:
             pl.semaphore_signal(barrier, inc=1, device_id=self.peer(dim), device_id_type=MESH)
         pl.semaphore_wait(barrier, len(dims))
 
-    def send(self, src, dst, dim):
+    def copy(self, src, dst, dim):
         i = self.used
         self.used += 1
-        copy = pltpu.make_async_remote_copy(
+        return pltpu.make_async_remote_copy(
             src_ref=src,
             dst_ref=dst,
             send_sem=self.r.send.at[i],
@@ -494,6 +536,9 @@
             device_id=self.peer(dim),
             device_id_type=MESH,
         )
+
+    def send(self, src, dst, dim):
+        copy = self.copy(src, dst, dim)
         copy.start()
         return copy
 
@@ -503,6 +548,11 @@
         copy = pltpu.make_async_copy(src, dst, self.r.own.at[i])
         copy.start()
         return copy
+
+
+def start_all(copies):
+    for copy in copies:
+        copy.start()
 
 
 def wait_all(copies):
@@ -529,10 +579,45 @@
     return steps, need
 
 
+class Track:
+    def __init__(self, acts):
+        self.acts = list(acts)
+
+    def take(self):
+        return [self.acts.pop(0)] if self.acts else []
+
+
 def bucket_sum(net, g, got, done, halves, order):
     R = g.shape[0] // halves
     lo, rows, at, bases = 0, R, 0, [h * R for h in range(halves)]
-    back = []
+    acts, back, end = [], [], None
+
+    def start_after(end, copies):
+        def act():
+            if end is not None:
+                end()
+            for copy in copies:
+                copy.start()
+
+        return act
+
+    def adder(copies, places, n):
+        step = 64 if n % 64 == 0 else 32 if n % 32 == 0 else 16
+
+        def end():
+            wait_all(copies)
+            for to, of in places:
+
+                def add(k, carry, to=to, of=of):
+                    mine = rows16(to + k * step, step)
+                    value = g[mine, :].astype(F32) + got[rows16(of + k * step, step), :].astype(F32)
+                    g[mine, :] = value.astype(BF)
+                    return carry
+
+                lax.fori_loop(0, n // step, add, 0)
+
+        return end
+
     for dim, kind, n in sum_plan(R, halves, order)[0]:
         b = net.bit(dim)
         keep = give = lo
@@ -543,50 +628,56 @@
         if kind == "other":
             givers, bases = [(1 - b) * R], [b * R]
         copies = [
-            net.send(g.at[rows16(base + give, n)], got.at[rows16(at + i * n, n)], dim)
+            net.copy(g.at[rows16(base + give, n)], got.at[rows16(at + i * n, n)], dim)
             for i, base in enumerate(givers)
         ]
-        yield
-        wait_all(copies)
-        step = 32 if n % 32 == 0 else 16
-        for i, base in enumerate(bases):
-
-            def add(k, carry, base=base, keep=keep, at=at, i=i, n=n):
-                mine = rows16(base + keep + k * step, step)
-                value = g[mine, :].astype(F32) + got[rows16(at + i * n + k * step, step), :].astype(F32)
-                g[mine, :] = value.astype(BF)
-                return carry
-
-            lax.fori_loop(0, n // step, add, 0)
+        acts.append(start_after(end, copies))
+        end = adder(copies, [(base + keep, at + i * n) for i, base in enumerate(bases)], n)
         at += n * len(bases)
         lo, rows = keep, n
-    for k in range(rows // 16):
-        done[rows16(lo + 16 * k, 16), :] = g[rows16(bases[0] + lo + 16 * k, 16), :]
+
+    def settle(end=end, lo=lo, base=bases[0], rows=rows):
+        end()
+        for k in range(rows // 16):
+            done[rows16(lo + 16 * k, 16), :] = g[rows16(base + lo + 16 * k, 16), :]
+
+    end = settle
     for dim, n, before in reversed(back):
         part = rows16(lo, n)
-        copy = net.send(done.at[part], done.at[part], dim)
-        yield
-        copy.wait()
+        copy = net.copy(done.at[part], done.at[part], dim)
+        acts.append(start_after(end, [copy]))
+        end = copy.wait
         lo = before
+    return Track(acts + [end])
 
 
 def small_sum(net, value, slots, order):
+    acts, end = [], None
     for i, dim in enumerate(order):
-        copy = net.send(value, slots.at[i], dim)
-        yield
-        copy.wait()
-        value[...] += slots[i]
+        copy = net.copy(value, slots.at[i], dim)
+
+        def act(end=end, copy=copy):
+            if end is not None:
+                end()
+            copy.start()
+
+        def end(copy=copy, i=i):
+            copy.wait()
+            value[...] += slots[i]
+
+        acts.append(act)
+    return Track(acts + [end])
 
 
 def advance(*sums):
     for one in sums:
-        next(one, None)
+        for act in one.take():
+            act()
 
 
 def drain(*sums):
-    left = list(sums)
-    while left:
-        left = [one for one in left if next(one, left) is not left]
+    while any(one.acts for one in sums):
+        advance(*sums)
 
 
 def quarter(net):
@@ -650,7 +741,8 @@
     qkv_own = net.here(r.wqkv_l, r.wqkv.at[m])
     w2_own = net.here(r.w2_l, r.w2)
     own = [
-        net.here(r.wo_l, r.wo.at[rows16(m * half, half)]),
+        net.here(r.wo_l.at[0 : D // 4], r.wo.at[rows16(m * (D // 4), D // 4)]),
+        net.here(r.wo_l.at[D // 4 : half], r.wo.at[rows16(half + m * (D // 4), D // 4)]),
         net.here(r.up_l, r.up.at[m]),
         net.here(r.down_l, r.down.at[rows16(m * F2, F2)]),
         net.here(r.cot.at[0, rows_of_mine], r.bg),
@@ -672,8 +764,9 @@
         def cut(n, base):
             return rows16(base + at * (n // cuts), count * (n // cuts))
 
-        parts = [r.wo.at[cut(half, of * half)], r.up.at[of, cut(D, 0)], r.down.at[cut(F2, of * F2)]]
-        return [net.send(x, x, dim) for x in parts]
+        wo = rows16(c * half + of * (D // 4) + (at - c * (cuts // 2)) * (half // cuts), count * (half // cuts))
+        parts = [r.wo.at[wo], r.up.at[of, cut(D, 0)], r.down.at[cut(F2, of * F2)]]
+        return [net.copy(x, x, dim) for x in parts]
 
     r.small[...] = jnp.zeros_like(r.small)
     mel_rim.wait()
@@ -683,107 +776,108 @@
     arrived = r.wqkv.at[1 - m, :, piece]
     qkv_c = net.send(arrived, arrived, "c")
     wait_all(own)
-    ff = pass_on(m, p, 1, "y")
+    ff_y = pass_on(m, p, 1, "y")
+    start_all(ff_y)
     w2_own.wait()
     stage_second(r, quarter(net))
     vec_copy.wait()
     r.vecs[8:16, :] = r.vec_mine[...] + r.vec_got[...]
     qkv_c.wait()
 
-    def block(slot, part):
-        return r.kv.at[(2 * slot + part) * D : (2 * slot + part + 1) * D]
-
-    kv_y, kv_c = [], []
-    for part in range(2):
-        stage_qkv(r, (1 + part,))
-        kv_c.append(net.send(block(0, part), block(1, part), "c"))
-        kv_y.append(net.send(block(0, part), block(2, part), "y"))
-    stage_qkv(r, (0,))
-    wait_all(ff)
-    ff = pass_on(1 - m, p, 1, 1) if bits > 1 else []
+    def block(slot, part, parts=1):
+        return r.kv.at[rows16((3 * slot + part) * half, parts * half)]
+
+    to_c, to_y, to_d = [], [], []
+    for part in (0, 1, 2):
+        stage_qkv(r, part)
+        to_c.append(net.send(block(4 - c, part), block(2, part), "c"))
+        if part > 0:
+            to_y.append(net.send(block(3 + c, part), block(0, part), "y"))
+            to_d.append(net.send(block(4 - c, part), block(1, part), "cy"))
+    wait_all(ff_y)
+    ff_z = pass_on(1 - m, p, 1, 1) if bits > 1 else []
+    start_all(ff_z)
+    ff_x = pass_on(1 - m, (p // 2) * 2 if bits > 1 else p, 2 if bits > 1 else 1, 0)
+    ff_c = pass_on(1 - m, c * (cuts // 2), cuts // 2, "c")
     stage_mask(r, sub)
-    attend_block(r, 0)
-    wait_all(ff)
-    ff = pass_on(1 - m, (p // 2) * 2 if bits > 1 else p, 2 if bits > 1 else 1, 0)
-    wait_all(kv_c)
-    attend_block(r, 1)
-    wait_all(ff)
-    ff = pass_on(1 - m, c * (cuts // 2), cuts // 2, "c")
-    wait_all(kv_y)
-    kv_d = [net.send(block(2, part), block(3, part), "c") for part in range(2)]
-    attend_block(r, 2)
-    wait_all(kv_d)
-    attend_block(r, 3)
-    attend_end(r)
-    wait_all(ff)
-    stage_mid(r)
+    to_c[0].wait()
+    heads = half // HEAD
+    attend(
+        r,
+        c,
+        {
+            heads: [lambda: wait_all(to_c[1:]), lambda: wait_all(ff_z), lambda: start_all(ff_x)],
+            2 * heads: [lambda: wait_all(ff_x), lambda: start_all(ff_c), lambda: wait_all(to_y)],
+            3 * heads: [lambda: wait_all(to_d)],
+        },
+    )
+    attend_end(r, 1)
+    mix_c = net.send(r.mixb.at[half:D], r.mix_got, "c")
+    attend_end(r, 0)
+    wait_all(ff_c)
+    mix_c.wait()
+    stage_mid(r, c)
     stage_ff(r)
 
     def summed(n, halves):
-        return bucket_sum(
-            net, getattr(r, "g_" + n), getattr(r, "got_" + n), getattr(r, "done_" + n), halves, order[n]
-        )
+        refs = [getattr(r, kind + n) for kind in ("g_", "got_", "done_")]
+        return bucket_sum(net, *refs, halves, order[n])
 
     down_sum = summed("down", 2)
     advance(down_sum)
     stage_mid_pull(r)
+    stage_do(r, c, False)
+    do_c = net.send(r.dot_out, r.dot.at[half:D], "c")
+    stage_out_weights(r, c)
     up_sum = summed("up", 2)
     advance(up_sum, down_sum)
-    enc = []
-
-    def send_enc():
-        enc.append(net.here(r.enc, r.enc_o.at[rows_of_mine]))
-        enc.append(net.send(r.enc, r.enc_got, "y"))
-
-    moves = {
-        1: (up_sum,),
-        4: (down_sum,),
-        6: (up_sum, down_sum),
-        9: (up_sum, down_sum),
-        12: (up_sum, down_sum),
-        13: (up_sum, down_sum),
-        14: (up_sum, down_sum),
-        15: (up_sum, down_sum),
-        16: (up_sum, down_sum),
-    }
-    turn = [0]
-
-    def hook():
-        turn[0] += 1
-        advance(*moves.get(turn[0], ()))
-        if turn[0] == 4:
-            send_enc()
-
-    pull_block(r, 3, r.part_a, hook)
-    to_c = net.send(r.part_a, r.from_d, "c")
-    pull_block(r, 2, r.part_y, hook)
-    to_c.wait()
-
-    def join(i, carry):
-        for part in range(2):
-            rows = rows16(i * 32, 32)
-            value = r.part_y[part, rows, :].astype(F32) + r.from_d[part, rows, :].astype(F32)
-            r.part_y[part, rows, :] = value.astype(BF)
-        return carry
-
-    lax.fori_loop(0, D // 32, join, 0)
-    to_y = net.send(r.part_y, r.from_y, "y")
-    pull_block(r, 1, r.part_a, hook)
-    to_s = net.send(r.part_a, r.from_s, "c")
-    pull_block(r, 0, r.part_o, hook)
-    r.dqb[...] = (r.dqt[...] * HEAD**-0.5).astype(BF)
-    to_s.wait()
-    to_y.wait()
+    stage_do(r, c, True)
+    stage_diag(r, 0)
+    do_c.wait()
+    stage_diag(r, 1)
+    enc = [
+        net.copy(r.enc, r.enc_got, "y"),
+        pltpu.make_async_copy(r.enc, r.enc_o.at[rows_of_mine], r.own.at[39]),
+    ]
+
+    both = half * 2
+    home_y = net.copy(r.dkv.at[0:both], r.from_y, "y")
+    home_d = net.copy(r.dkv.at[both : 2 * both], r.from_d, "cy")
+    home_c = net.copy(r.dkv.at[2 * both : 3 * both], r.from_c.at[half:], "c")
+    hooks = {}
+
+    def at_step(step, *acts):
+        hooks.setdefault(step * heads // 4, []).extend(acts)
+
+    at_step(1, *up_sum.take())
+    at_step(4, home_y.start, *down_sum.take())
+    at_step(6, *up_sum.take(), *down_sum.take())
+    at_step(8, home_d.start)
+    at_step(9, *up_sum.take(), *down_sum.take())
+    at_step(11, lambda: start_all(enc))
+    at_step(12, home_c.start, *up_sum.take(), *down_sum.take())
+    for step in (13, 14, 15):
+        at_step(step, *up_sum.take(), *down_sum.take())
+    attend_pull(r, c, hooks)
+    r.dq_out[...] = (r.dqt[half:D, :] * HEAD**-0.5).astype(BF)
+    dq_c = net.send(r.dq_out, r.from_c.at[0:half], "c")
+    r.dsum[rows16(c * half, half), :] = (r.dqt[0:half, :] * HEAD**-0.5).astype(BF)
+    home_y.wait()
+    home_d.wait()
+    home_c.wait()
 
     def total(i, carry):
         for part in range(2):
-            rows = rows16(i * 32, 32)
-            value = r.part_o[part, rows, :].astype(F32) + r.from_s[part, rows, :].astype(F32)
-            r.part_o[part, rows, :] = (value + r.from_y[part, rows, :].astype(F32)).astype(BF)
+            rows = rows16(part * half + i * 32, 32)
+            mine = r.dkv[rows16(3 * both + part * half + i * 32, 32), :].astype(F32) + r.from_y[rows, :].astype(F32)
+            r.dsum[rows16((1 + part) * D + c * half + i * 32, 32), :] = mine.astype(BF)
+            other = r.from_c[rows16((1 + part) * half + i * 32, 32), :].astype(F32) + r.from_d[rows, :].astype(F32)
+            r.dsum[rows16((1 + part) * D + (1 - c) * half + i * 32, 32), :] = other.astype(BF)
         return carry
 
-    lax.fori_loop(0, D // 32, total, 0)
-    r.dkb, r.dvb = r.part_o.at[0], r.part_o.at[1]
+    lax.fori_loop(0, half // 32, total, 0)
+    dq_c.wait()
+    r.dsum[rows16((1 - c) * half, half), :] = r.from_c[0:half, :]
 
     stage_qkv_weights(r)
     qkv_sum = summed("qkv", 2)
@@ -864,11 +958,12 @@
         dgo=(td, F32),
         dg2=(td, F32),
         normed=(td, BF),
-        qt=(dt, BF),
-        kv=((8 * D, T), BF),
+        kv=((15 * half, T), BF),
         mixt=(dt, F32),
         mixb=(dt, BF),
+        mix_got=((half, T), BF),
         dot=(dt, BF),
+        dot_out=((half, T), BF),
         top=((H, 1, T), F32),
         total=((H, 1, T), F32),
         diag=((H, 1, T), F32),
@@ -883,13 +978,13 @@
         ffo=(td, F32),
         ntg=(td, F32),
         attg=(td, BF),
-        dqb=(dt, BF),
-        part_a=((2, D, T), BF),
-        part_y=((2, D, T), BF),
-        part_o=((2, D, T), BF),
-        from_d=((2, D, T), BF),
-        from_y=((2, D, T), BF),
-        from_s=((2, D, T), BF),
+        dqt=(dt, F32),
+        dq_out=((half, T), BF),
+        dkv=((8 * half, T), BF),
+        from_y=((2 * half, T), BF),
+        from_d=((2 * half, T), BF),
+        from_c=((3 * half, T), BF),
+        dsum=((3 * D, T), BF),
         enc_got=(td, BF),
         melg=((T, 256), BF),
         melg_got=((T, 256), BF),
@@ -904,14 +999,15 @@
         scratch["got_" + n] = ((sum_plan(rows, halves, order[n])[1], D), BF)
         scratch["done_" + n] = ((rows, D), BF)
     if not alias:
-        scratch.update(g_qkv=((6 * half, D), BF), g_c2=((6 * half, D), BF))
+        scratch.update(g_qkv=((6 * half, D), BF), g_c2=((6 * half, D), BF), normedt=(dt, BF))
     names = list(near) + list(far) + list(outs) + list(scratch) + ["send", "recv", "own"]
 
     def kernel(*refs):
         r = Box()
         for n, ref in zip(names, refs):
             setattr(r, n, ref)
-        r.odd, r.smg, r.sg, r.fe, r.fo, r.dqt, r.enc = r.shift, r.mid, r.ntwo, r.act, r.ing, r.ffo, r.bg
+        r.odd, r.smg, r.sg, r.fe, r.fo, r.enc = r.shift, r.mid, r.ntwo, r.act, r.ing, r.bg
+        r.normedt = r.mixb if alias else r.normedt
         if alias:
             r.g_qkv, r.g_c2 = r.kv.at[0 : 6 * half], r.kv.at[6 * half : 12 * half]
         r.g_c2a, r.g_c2b = r.g_c2.at[0 : 3 * half], r.g_c2.at[3 * half : 6 * half]

time: 224 us -> 219 us (0.978)
  Pallas kernels: 223 us -> 218 us
    pallas_call x1, Pallas kernels: 215 us -> 210 us  [run_layer(): pl.pallas_call(kernel, name='layer', out_shape=[jax.ShapeDtypeStruct(*o)...]
where the time goes in v5:
time: 219 us
  Pallas kernels  218 us (100%)
    pallas_call x1, Pallas kernels, run_layer(): pl.pallas_call(kernel, name='layer', out_shape=[jax.ShapeDtypeStruct(*o)...  210 us
    pallas_call x1, Pallas kernels, run_finish(): pl.pallas_call(kernel, name='finish', out_shape=[jax.ShapeDtypeStruct(*o)...  7.97 us

profile of v5, /device:TPU:0, one launch (start us, length us, event | category | flops | bytes accessed | tf_op | source)
XLA Modules:
  0.0 218.7 jit_solution(18219640066628884685)
XLA Ops:
  0.7 209.9 %layer.1 = (bf16[1024,512]{1,0:T(8,128)(2,1)}, bf16[1024,256]{1,0:T(8,128)(2,1)}, bf16[1024,512]{1,0:T(8,128)(2,1)}, bf16[512,1024]{1,0:T(8,128)(2,1)}, bf16[256...) custom-call(bf16[3,80,512]{2,1,0:T(8,128)(2,1)} %refs_0_.1, ...), custom_call_target="tpu_custom_call" | custom-call | tf_op jit(solution)/shard_map/layer/pallas_call | solution.py:1017
  210.6 8.0 %finish.1 = (bf16[1,1024,512]{2,1,0:T(8,128)(2,1)}, f32[1,80,2048]{2,1,0:T(8,128)}, f32[3,80,512]{2,1,0:T(8,128)}, f32[3,512,512]{2,1,0:T(8,128)}, f32[3,512,256...) custom-call(bf16[1024,512]{1,0:T(8,128)(2,1)} %get-tuple-element.45., ...), custom_call_target="tpu_custom_call" | custom-call | tf_op jit(solution)/shard_map/finish/pallas_call | solution.py:1085

commit v6 on v5

--- a/solution.py
+++ b/solution.py
@@ -508,24 +508,24 @@
             return self.m
         return (self.d // (1 << dim)) % 2
 
-    def peer(self, dim):
-        if dim == "c":
-            return (self.d, 1 - self.c, self.m)
-        if dim == "y":
-            return (self.d, self.c, 1 - self.m)
-        if dim == "cy":
-            return (self.d, 1 - self.c, 1 - self.m)
-        step = 1 << dim
-        return (self.d + step - 2 * step * self.bit(dim), self.c, self.m)
-
-    def greet(self):
+    def peer(self, dims):
+        d = self.d
+        for k in dims:
+            if k not in ("c", "y"):
+                d = d + (1 << k) - 2 * (1 << k) * self.bit(k)
+        return (
+            d,
+            1 - self.c if "c" in dims else self.c,
+            1 - self.m if "y" in dims else self.m,
+        )
+
+    def greet(self, partners):
         barrier = pltpu.get_barrier_semaphore()
-        dims = ["c", "y", "cy"] + list(range(self.bits))
-        for dim in dims:
-            pl.semaphore_signal(barrier, inc=1, device_id=self.peer(dim), device_id_type=MESH)
-        pl.semaphore_wait(barrier, len(dims))
-
-    def copy(self, src, dst, dim):
+        for dims in partners:
+            pl.semaphore_signal(barrier, inc=1, device_id=self.peer(dims), device_id_type=MESH)
+        pl.semaphore_wait(barrier, len(partners))
+
+    def copy(self, src, dst, *dims):
         i = self.used
         self.used += 1
         return pltpu.make_async_remote_copy(
@@ -533,12 +533,12 @@
             dst_ref=dst,
             send_sem=self.r.send.at[i],
             recv_sem=self.r.recv.at[i],
-            device_id=self.peer(dim),
+            device_id=self.peer(dims),
             device_id_type=MESH,
         )
 
-    def send(self, src, dst, dim):
-        copy = self.copy(src, dst, dim)
+    def send(self, src, dst, *dims):
+        copy = self.copy(src, dst, *dims)
         copy.start()
         return copy
 
@@ -564,18 +564,25 @@
     return pl.ds(pl.multiple_of(start, 16), size)
 
 
+def subsets(dims):
+    found = [()]
+    for dim in dims:
+        found += [one + (dim,) for one in found]
+    return found[1:]
+
+
 def sum_plan(rows, halves, order):
     steps, need = [], 0
-    for dim in order:
-        if dim == "y" and halves == 2:
-            steps.append((dim, "other", rows))
+    for dims in order:
+        by_half = halves == 2 and "y" in dims
+        cutting = [dim for dim in dims if not (by_half and dim == "y")]
+        if rows % (16 << len(cutting)):
+            cutting = []
+        rows >>= len(cutting)
+        if by_half:
             halves = 1
-        elif rows % 32 == 0:
-            rows //= 2
-            steps.append((dim, "halve", rows))
-        else:
-            steps.append((dim, "swap", rows))
-        need += rows * halves
+        steps.append((dims, cutting, rows, halves, by_half))
+        need += rows * halves * len(subsets(dims))
     return steps, need
 
 
@@ -606,11 +613,13 @@
 
         def end():
             wait_all(copies)
-            for to, of in places:
-
-                def add(k, carry, to=to, of=of):
+            for to, ofs in places:
+
+                def add(k, carry, to=to, ofs=ofs):
                     mine = rows16(to + k * step, step)
-                    value = g[mine, :].astype(F32) + got[rows16(of + k * step, step), :].astype(F32)
+                    value = g[mine, :].astype(F32)
+                    for of in ofs:
+                        value = value + got[rows16(of + k * step, step), :].astype(F32)
                     g[mine, :] = value.astype(BF)
                     return carry
 
@@ -618,22 +627,30 @@
 
         return end
 
-    for dim, kind, n in sum_plan(R, halves, order)[0]:
-        b = net.bit(dim)
-        keep = give = lo
-        givers = bases
-        if kind == "halve":
-            keep, give = lo + b * n, lo + (1 - b) * n
-            back.append((dim, n, lo))
-        if kind == "other":
-            givers, bases = [(1 - b) * R], [b * R]
-        copies = [
-            net.copy(g.at[rows16(base + give, n)], got.at[rows16(at + i * n, n)], dim)
-            for i, base in enumerate(givers)
-        ]
+    for dims, cutting, n, _, by_half in sum_plan(R, halves, order)[0]:
+
+        def part_of(other):
+            start = lo
+            for i, dim in enumerate(reversed(cutting)):
+                b = net.bit(dim)
+                start = start + (1 - b if dim in other else b) * (n << i)
+            return start
+
+        keep = part_of(())
+        if by_half:
+            bases = [net.m * R]
+        copies, ofs = [], [[] for _ in bases]
+        for other in subsets(dims):
+            sources = [(1 - net.m) * R] if by_half and "y" in other else bases
+            for i, base in enumerate(sources):
+                src = g.at[rows16(base + part_of(other), n)]
+                copies.append(net.copy(src, got.at[rows16(at, n)], *other))
+                ofs[i].append(at)
+                at += n
         acts.append(start_after(end, copies))
-        end = adder(copies, [(base + keep, at + i * n) for i, base in enumerate(bases)], n)
-        at += n * len(bases)
+        end = adder(copies, [(base + keep, of) for base, of in zip(bases, ofs)], n)
+        if cutting:
+            back.append((cutting, n, lo))
         lo, rows = keep, n
 
     def settle(end=end, lo=lo, base=bases[0], rows=rows):
@@ -642,29 +659,33 @@
             done[rows16(lo + 16 * k, 16), :] = g[rows16(base + lo + 16 * k, 16), :]
 
     end = settle
-    for dim, n, before in reversed(back):
+    for cutting, n, before in reversed(back):
         part = rows16(lo, n)
-        copy = net.copy(done.at[part], done.at[part], dim)
-        acts.append(start_after(end, [copy]))
-        end = copy.wait
+        copies = [net.copy(done.at[part], done.at[part], *other) for other in subsets(cutting)]
+        acts.append(start_after(end, copies))
+        end = functools.partial(wait_all, copies)
         lo = before
     return Track(acts + [end])
 
 
 def small_sum(net, value, slots, order):
-    acts, end = [], None
-    for i, dim in enumerate(order):
-        copy = net.copy(value, slots.at[i], dim)
-
-        def act(end=end, copy=copy):
+    acts, end, at = [], None, 0
+    for dims in order:
+        copies = [net.copy(value, slots.at[at + i], *other) for i, other in enumerate(subsets(dims))]
+
+        def act(end=end, copies=copies):
             if end is not None:
                 end()
-            copy.start()
-
-        def end(copy=copy, i=i):
-            copy.wait()
-            value[...] += slots[i]
-
+            start_all(copies)
+
+        def end(copies=copies, at=at):
+            wait_all(copies)
+            total = value[...]
+            for i in range(len(copies)):
+                total = total + slots[at + i]
+            value[...] = total
+
+        at += len(copies)
         acts.append(act)
     return Track(acts + [end])
 
@@ -704,16 +725,15 @@
 
 
 def orders(bits):
-    dims = list(range(bits))
-    z_first = dims[1:2] + dims[:1] + dims[2:]
+    pairs = [tuple(range(k, min(k + 2, bits))) for k in range(1, bits, 2)]
+    wide, near = [("c",), ("y", 0)], [("c", "y", 0)]
     return dict(
-        down=["c", "y"] + dims,
-        up=["c"] + dims + ["y"],
-        qkv=["c"] + z_first + ["y"],
-        c2a=["c", "y"] + dims,
-        c2b=["c"] + dims[:1] + ["y"] + dims[1:],
-        c1=["c"] + dims + ["y"],
-        vec=["c"] + dims + ["y"],
+        down=wide + pairs,
+        up=[("c",)] + pairs + [("y", 0)],
+        qkv=wide + pairs,
+        c2=wide + pairs,
+        c1=near + pairs,
+        vec=near + pairs,
     )
 
 
@@ -729,14 +749,6 @@
     rows_of_mine = rows16(sub * T, T)
 
     r.melbuf[...] = jnp.zeros_like(r.melbuf)
-    r.vec_mine[...] = jnp.zeros_like(r.vec_mine)
-    own_lanes = pl.ds(pl.multiple_of(m * half, 128), half)
-    r.vec_mine[0:2, own_lanes] = r.qkvb[...].astype(F32)
-    for k in range(side):
-        r.vec_mine[pl.ds(2 + m * side + k, 1), :] = r.upb[k * D : (k + 1) * D].astype(F32).reshape(1, D)
-    for k, n in enumerate(ROW_BIASES):
-        r.vecs[k : k + 1, :] = getattr(r, n)[...].astype(F32).reshape(1, D)
-    net.greet()
     mel_own = net.here(r.mel.at[0], r.melbuf.at[0:mels, 128 : 128 + span])
     qkv_own = net.here(r.wqkv_l, r.wqkv.at[m])
     w2_own = net.here(r.w2_l, r.w2)
@@ -747,6 +759,15 @@
         net.here(r.down_l, r.down.at[rows16(m * F2, F2)]),
         net.here(r.cot.at[0, rows_of_mine], r.bg),
     ]
+    r.vec_mine[...] = jnp.zeros_like(r.vec_mine)
+    own_lanes = pl.ds(pl.multiple_of(m * half, 128), half)
+    r.vec_mine[0:2, own_lanes] = r.qkvb[...].astype(F32)
+    for k in range(side):
+        r.vec_mine[pl.ds(2 + m * side + k, 1), :] = r.upb[k * D : (k + 1) * D].astype(F32).reshape(1, D)
+    for k, n in enumerate(ROW_BIASES):
+        r.vecs[k : k + 1, :] = getattr(r, n)[...].astype(F32).reshape(1, D)
+    partners = [one for dims in order["c1"] for one in subsets(dims)]
+    net.greet(partners)
     vec_copy = net.send(r.vec_mine, r.vec_got, "y")
     mel_own.wait()
     src = pl.ds(pl.multiple_of(128 + (1 - c) * (span - 128), 128), 128)
@@ -788,12 +809,12 @@
         return r.kv.at[rows16((3 * slot + part) * half, parts * half)]
 
     to_c, to_y, to_d = [], [], []
-    for part in (0, 1, 2):
+    for part in (1, 2, 0):
         stage_qkv(r, part)
-        to_c.append(net.send(block(4 - c, part), block(2, part), "c"))
+        to_c.insert(0, net.send(block(4 - c, part), block(2, part), "c"))
         if part > 0:
             to_y.append(net.send(block(3 + c, part), block(0, part), "y"))
-            to_d.append(net.send(block(4 - c, part), block(1, part), "cy"))
+            to_d.append(net.send(block(4 - c, part), block(1, part), "c", "y"))
     wait_all(ff_y)
     ff_z = pass_on(1 - m, p, 1, 1) if bits > 1 else []
     start_all(ff_z)
@@ -842,7 +863,7 @@
 
     both = half * 2
     home_y = net.copy(r.dkv.at[0:both], r.from_y, "y")
-    home_d = net.copy(r.dkv.at[both : 2 * both], r.from_d, "cy")
+    home_d = net.copy(r.dkv.at[both : 2 * both], r.from_d, "c", "y")
     home_c = net.copy(r.dkv.at[2 * both : 3 * both], r.from_c.at[half:], "c")
     hooks = {}
 
@@ -851,13 +872,11 @@
 
     at_step(1, *up_sum.take())
     at_step(4, home_y.start, *down_sum.take())
-    at_step(6, *up_sum.take(), *down_sum.take())
-    at_step(8, home_d.start)
-    at_step(9, *up_sum.take(), *down_sum.take())
-    at_step(11, lambda: start_all(enc))
-    at_step(12, home_c.start, *up_sum.take(), *down_sum.take())
-    for step in (13, 14, 15):
-        at_step(step, *up_sum.take(), *down_sum.take())
+    at_step(8, home_d.start, *down_sum.take())
+    at_step(11, lambda: start_all(enc), *up_sum.take(), *down_sum.take())
+    at_step(12, home_c.start)
+    at_step(13, *up_sum.take(), *down_sum.take())
+    at_step(15, *up_sum.take(), *down_sum.take())
     attend_pull(r, c, hooks)
     r.dq_out[...] = (r.dqt[half:D, :] * HEAD**-0.5).astype(BF)
     dq_c = net.send(r.dq_out, r.from_c.at[0:half], "c")
@@ -886,17 +905,17 @@
     rim = [net.send(r.sg.at[0:16], r.slots.at[0, i], dim) for i, dim in enumerate(("c", "y"))]
     advance(qkv_sum)
     stage_conv2_weights(r)
-    c2a_sum, c2b_sum = summed("c2a", 1), summed("c2b", 1)
-    advance(c2a_sum, c2b_sum)
+    c2_sum = summed("c2", 1)
+    advance(c2_sum)
     wait_all(rim)
     stage_conv2_pull(r, pick_next(net, r.slots.at[0]))
     rim = [net.send(r.fe.at[0:16], r.slots.at[1, i], dim) for i, dim in enumerate(("c", "y"))]
     rim += [net.send(r.fo.at[T - 16 : T], r.slots.at[2, i], dim) for i, dim in enumerate(("c", "y"))]
-    advance(c2a_sum, c2b_sum, qkv_sum)
+    advance(c2_sum)
     stage_conv1_weights(r)
     c1_sum = summed("c1", 1)
     vec_sum = small_sum(net, r.small, r.got_small, order["vec"])
-    advance(c1_sum, vec_sum)
+    advance(c1_sum, vec_sum, qkv_sum)
     wait_all(rim)
     stage_mel(r, pick_next(net, r.slots.at[1]), pick_prev(net, r.slots.at[2]))
     rows_of_yours = rows16((1 - sub) * T, T)
@@ -906,7 +925,7 @@
         net.here(r.enc_got, r.enc_o.at[rows_of_yours]),
         net.here(r.melg, r.mel_o.at[rows_of_mine]),
     ]
-    drain(c1_sum, vec_sum, c2a_sum, c2b_sum, qkv_sum, up_sum, down_sum)
+    drain(c1_sum, vec_sum, c2_sum, qkv_sum, up_sum, down_sum)
 
     ends.append(net.here(r.done_down, r.down_o))
     for j in range(side):
@@ -920,8 +939,7 @@
                     r.qkv_o.at[part, j * half : (j + 1) * half],
                 )
             )
-    ends.append(net.here(r.done_c2a, r.c2_o.at[0 : 3 * half]))
-    ends.append(net.here(r.done_c2b, r.c2_o.at[3 * half : 6 * half]))
+    ends.append(net.here(r.done_c2, r.c2_o))
     ends.append(net.here(r.done_c1, r.c1_o))
     ends.append(net.here(r.small, r.small_o))
     mel_y.wait()
@@ -933,7 +951,7 @@
     half, H = D // 2, D // HEAD
     td, dt = (T, D), (D, T)
     order = orders(bits)
-    buckets = dict(down=(F2, 2), up=(F2 + half, 2), qkv=(3 * half, 2), c2a=(3 * half, 1), c2b=(3 * half, 1), c1=(lanes, 1))
+    buckets = dict(down=(F2, 2), up=(F2 + half, 2), qkv=(3 * half, 2), c2=(6 * half, 1), c1=(lanes, 1))
     scratch = dict(
         melbuf=((128, 4 * T + 256), BF),
         mele=((T + 24, 128), F32),
@@ -989,7 +1007,7 @@
         melg=((T, 256), BF),
         melg_got=((T, 256), BF),
         small=((16, D), F32),
-        got_small=((bits + 2, 16, D), F32),
+        got_small=((sum(len(subsets(dims)) for dims in order["vec"]), 16, D), F32),
         slots=((3, 2, 16, D), BF),
     )
     alias = T == D
@@ -1010,7 +1028,6 @@
         r.normedt = r.mixb if alias else r.normedt
         if alias:
             r.g_qkv, r.g_c2 = r.kv.at[0 : 6 * half], r.kv.at[6 * half : 12 * half]
-        r.g_c2a, r.g_c2b = r.g_c2.at[0 : 3 * half], r.g_c2.at[3 * half : 6 * half]
         layer(r, bits)
 
     vmem, anywhere = pl.BlockSpec(memory_space=pltpu.VMEM), pl.BlockSpec(memory_space=pl.ANY)

time: 219 us -> 234 us (1.068)
  Pallas kernels: 218 us -> 231 us
    pallas_call x1, Pallas kernels: 210 us -> 223 us  [run_layer(): pl.pallas_call(kernel, name='layer', out_shape=[jax.ShapeDtypeStruct(*o)...]
where the time goes in v6:
time: 234 us; the launch traced here: 232 us
  Pallas kernels  231 us (99%)
    pallas_call x1, Pallas kernels, run_layer(): pl.pallas_call(kernel, name='layer', out_shape=[jax.ShapeDtypeStruct(*o)...  223 us
    pallas_call x1, Pallas kernels, run_finish(): pl.pallas_call(kernel, name='finish', out_shape=[jax.ShapeDtypeStruct(*o)...  7.97 us

profile of v6, /device:TPU:0, one launch (start us, length us, event | category | flops | bytes accessed | tf_op | source)
XLA Modules:
  0.0 232.3 jit_solution(585302053146826075)
XLA Ops:
  0.7 223.5 %layer.1 = (bf16[1024,512]{1,0:T(8,128)(2,1)}, bf16[1024,256]{1,0:T(8,128)(2,1)}, bf16[1024,512]{1,0:T(8,128)(2,1)}, bf16[512,1024]{1,0:T(8,128)(2,1)}, bf16[256...) custom-call(bf16[3,80,512]{2,1,0:T(8,128)(2,1)} %refs_0_.1, ...), custom_call_target="tpu_custom_call" | custom-call | tf_op jit(solution)/shard_map/layer/pallas_call | solution.py:1034
  224.1 8.0 %finish.1 = (bf16[1,1024,512]{2,1,0:T(8,128)(2,1)}, f32[1,80,2048]{2,1,0:T(8,128)}, f32[3,80,512]{2,1,0:T(8,128)}, f32[3,512,512]{2,1,0:T(8,128)}, f32[3,512,256...) custom-call(bf16[1024,512]{1,0:T(8,128)(2,1)} %get-tuple-element.45., ...), custom_call_target="tpu_custom_call" | custom-call | tf_op jit(solution)/shard_map/finish/pallas_call | solution.py:1102

commit v7 on v6

--- a/solution.py
+++ b/solution.py
@@ -273,14 +273,15 @@
     rows_loop(T, 32, one)
 
 
-def stage_ff(r):
+def stage_ff(r, hooks):
     T, D = r.stream.shape
     side = r.up.shape[2] // D
     parts, width = 2 * side, D
     add_small(r, DNB, col(r.bg[...].astype(F32)))
 
-    def chunk(j, carry):
-        into, at = j // side, j % side
+    def chunk(t):
+        into, at = t % 2, t // 2
+        j = into * side + at
         up = r.up[into, :, pl.ds(pl.multiple_of(at * D, D), D)]
         down = r.down[pl.ds(pl.multiple_of(j * D, D), D), :]
         r.tmp[...] = nn(r.ntwo[...], up)
@@ -301,22 +302,15 @@
         out = nn(act, down)
         back = nt(ing, up)
 
-        @pl.when(j == 0)
-        def _():
-            r.ffo[...] = out
-            r.ntg[...] = back
-
-        @pl.when(j > 0)
-        def _():
-            r.ffo[...] += out
-            r.ntg[...] += back
-
-        r.g_down[pl.ds(pl.multiple_of(j * D, D), D), :] = tn(act, r.bg[...]).astype(BF)
-        base = into * (r.g_up.shape[0] // 2) + at * D
-        r.g_up[pl.ds(pl.multiple_of(base, 16), D), :] = tn(r.ntwo[...], ing).astype(BF)
-        return carry
-
-    lax.fori_loop(0, parts, chunk, 0)
+        r.ffo[...] += out
+        r.ntg[...] += back
+        rows = pl.ds(pl.multiple_of(t * D, D), D)
+        r.g_down[rows, :] = tn(act, r.bg[...]).astype(BF)
+        r.g_up[rows, :] = tn(r.ntwo[...], ing).astype(BF)
+
+    r.ffo[...] = jnp.zeros_like(r.ffo)
+    r.ntg[...] = jnp.zeros_like(r.ntg)
+    head_loop(parts, hooks, chunk)
 
 
 def stage_mid_pull(r):
@@ -355,11 +349,10 @@
 def stage_out_weights(r, c):
     D = r.attg.shape[1]
     half, qr = D // 2, D // 4
-    rows = r.g_up.shape[0] // 2
     for k, mix in ((c, r.mixb[0:half, :]), (1 - c, r.mix_got[...])):
         value = nn(mix, r.attg[...]).astype(BF)
         for h in range(2):
-            r.g_up[rows16(h * rows + rows - half + k * qr, qr), :] = value[h * qr : (h + 1) * qr, :]
+            r.g_out[rows16(h * half + k * qr, qr), :] = value[h * qr : (h + 1) * qr, :]
 
 
 def stage_diag(r, i):
@@ -407,21 +400,19 @@
     return jnp.concatenate([r.dsum[at : at + qr, :], r.dsum[at + 2 * qr : at + 3 * qr, :]], axis=0)
 
 
-def stage_qkv_weights(r):
+def stage_qkv_weights(r, part):
     T, D = r.stream.shape
     half = D // 2
-    r.normedt[...] = r.normed[...].astype(F32).T.astype(BF)
     ones = jnp.ones((8, T), BF)
-    for part in range(3):
-        for h in range(2):
-            piece = piece_of(r, part, h)
-            if part != 1:
-                row = QB if part == 0 else VB
-                r.small[row : row + 1, h * half : (h + 1) * half] = nt(ones, piece)[0:1, :]
-            grad = nt(r.normedt[...], piece).astype(BF)
-            at = (3 * h + part) * half
-            r.g_qkv[at : at + half, 0:half] = grad[0:half, :]
-            r.g_qkv[at : at + half, half:D] = grad[half:D, :]
+    for h in range(2):
+        piece = piece_of(r, part, h)
+        if part != 1:
+            row = QB if part == 0 else VB
+            r.small[row : row + 1, h * half : (h + 1) * half] = nt(ones, piece)[0:1, :]
+        grad = nt(r.normedt[...], piece).astype(BF)
+        at = (2 * part + h) * half
+        r.g_qkv[at : at + half, 0:half] = grad[0:half, :]
+        r.g_qkv[at : at + half, half:D] = grad[half:D, :]
 
 
 def stage_qkv_pull(r):
@@ -432,6 +423,10 @@
             back = nn(r.wqkv[h, part], piece_of(r, part, h))
             total = back if total is None else total + back
     r.tmp[...] = total.T
+
+
+def stage_norm_pull(r):
+    T, D = r.stream.shape
 
     def one(i, accs):
         rows = pl.ds(pl.multiple_of(i * 32, 32), 32)
@@ -457,6 +452,10 @@
     r.tmp[...] = nt(sg, r.w2[1])
     r.tmp2[...] = nt(sg, r.w2[2]) + r.shift[1 : T + 1, :]
 
+
+def stage_first_pull(r):
+    T, D = r.stream.shape
+
     def one(i, acc):
         rows = pl.ds(pl.multiple_of(i * 32, 32), 32)
         even = (r.tmp[rows, :] * r.dge[rows, :]).astype(BF)
@@ -468,12 +467,10 @@
     add_small(r, C1B, lax.fori_loop(0, T // 32, one, jnp.zeros((1, D), F32)))
 
 
-def stage_conv2_weights(r):
+def stage_conv2_weights(r, i):
     D = r.stream.shape[1]
-    sg = r.sg[...]
-    for i, tap in enumerate((r.hp, r.he, r.ho)):
-        value = tn(tap[...], sg).astype(BF)
-        r.g_c2[i * D : (i + 1) * D, :] = value
+    tap = (r.hp, r.he, r.ho)[i]
+    r.g_c2[i * D : (i + 1) * D, :] = tn(tap[...], r.sg[...]).astype(BF)
 
 
 def stage_conv1_weights(r):
@@ -724,17 +721,20 @@
 ROW_BIASES = ("c1b", "c2b", "n1g", "n1b", "oub", "n2g", "n2b", "dnb")
 
 
-def orders(bits):
-    pairs = [tuple(range(k, min(k + 2, bits))) for k in range(1, bits, 2)]
-    wide, near = [("c",), ("y", 0)], [("c", "y", 0)]
-    return dict(
-        down=wide + pairs,
-        up=[("c",)] + pairs + [("y", 0)],
-        qkv=wide + pairs,
-        c2=wide + pairs,
-        c1=near + pairs,
-        vec=near + pairs,
-    )
+ORDERS = dict(
+    down=("xczwy", "zcxwy"),
+    up=("xyzwc", "zyxwc"),
+    out=("cxzwy",),
+    qkv=("xczwy", "zxcwy", "ycxzw"),
+    c2=("cxyzw", "yzcxw", "xyzcw"),
+    c1=("zcxyw",),
+    vec=("cyxzw",),
+)
+
+
+def orders(name, bits):
+    dims = dict(c=["c"], y=["y"], x=[0], z=list(range(1, min(2, bits))), w=list(range(2, bits)))
+    return [[(dim,) for ch in spec for dim in dims[ch]] for spec in ORDERS[name]]
 
 
 def layer(r, bits):
@@ -745,7 +745,6 @@
     net = Net(r, bits)
     c, m = net.c, net.m
     sub = c + m - 2 * c * m
-    order = orders(bits)
     rows_of_mine = rows16(sub * T, T)
 
     r.melbuf[...] = jnp.zeros_like(r.melbuf)
@@ -766,8 +765,7 @@
         r.vec_mine[pl.ds(2 + m * side + k, 1), :] = r.upb[k * D : (k + 1) * D].astype(F32).reshape(1, D)
     for k, n in enumerate(ROW_BIASES):
         r.vecs[k : k + 1, :] = getattr(r, n)[...].astype(F32).reshape(1, D)
-    partners = [one for dims in order["c1"] for one in subsets(dims)]
-    net.greet(partners)
+    net.greet([("c",), ("y",), ("c", "y")] + [(k,) for k in range(bits)])
     vec_copy = net.send(r.vec_mine, r.vec_got, "y")
     mel_own.wait()
     src = pl.ds(pl.multiple_of(128 + (1 - c) * (span - 128), 128), 128)
@@ -808,13 +806,13 @@
     def block(slot, part, parts=1):
         return r.kv.at[rows16((3 * slot + part) * half, parts * half)]
 
-    to_c, to_y, to_d = [], [], []
-    for part in (1, 2, 0):
+    to_y, to_d = [], []
+    for part in (1, 2):
         stage_qkv(r, part)
-        to_c.insert(0, net.send(block(4 - c, part), block(2, part), "c"))
-        if part > 0:
-            to_y.append(net.send(block(3 + c, part), block(0, part), "y"))
-            to_d.append(net.send(block(4 - c, part), block(1, part), "c", "y"))
+        to_y.append(net.send(block(3 + c, part), block(0, part), "y"))
+        to_d.append(net.send(block(4 - c, part), block(1, part), "c", "y"))
+    stage_qkv(r, 0)
+    to_c = [net.send(block(4 - c, part), block(2, part), "c") for part in range(3)]
     wait_all(ff_y)
     ff_z = pass_on(1 - m, p, 1, 1) if bits > 1 else []
     start_all(ff_z)
@@ -838,20 +836,28 @@
     wait_all(ff_c)
     mix_c.wait()
     stage_mid(r, c)
-    stage_ff(r)
-
-    def summed(n, halves):
-        refs = [getattr(r, kind + n) for kind in ("g_", "got_", "done_")]
-        return bucket_sum(net, *refs, halves, order[n])
-
-    down_sum = summed("down", 2)
-    advance(down_sum)
+
+    def summed(n, part, rows, halves):
+        views = [
+            getattr(r, "g_" + n).at[part * rows * halves : (part + 1) * rows * halves],
+            getattr(r, "got_%s%d" % (n, part)),
+            getattr(r, "done_" + n).at[part * rows : (part + 1) * rows],
+        ]
+        return bucket_sum(net, *views, halves, orders(n, bits)[part])
+
+    down = [summed("down", part, D, 2) for part in range(side)]
+    up = [summed("up", part, D, 2) for part in range(side)]
+    hooks = {}
+    for part in range(side - 1):
+        hooks[2 * part + 2] = down[part].take() + up[part].take()
+    stage_ff(r, hooks)
     stage_mid_pull(r)
     stage_do(r, c, False)
     do_c = net.send(r.dot_out, r.dot.at[half:D], "c")
+    advance(down[-1], up[-1])
     stage_out_weights(r, c)
-    up_sum = summed("up", 2)
-    advance(up_sum, down_sum)
+    out = summed("out", 0, half, 2)
+    advance(out)
     stage_do(r, c, True)
     stage_diag(r, 0)
     do_c.wait()
@@ -870,13 +876,14 @@
     def at_step(step, *acts):
         hooks.setdefault(step * heads // 4, []).extend(acts)
 
-    at_step(1, *up_sum.take())
-    at_step(4, home_y.start, *down_sum.take())
-    at_step(8, home_d.start, *down_sum.take())
-    at_step(11, lambda: start_all(enc), *up_sum.take(), *down_sum.take())
+    at_step(4, home_y.start)
+    at_step(8, home_d.start)
+    at_step(11, lambda: start_all(enc))
     at_step(12, home_c.start)
-    at_step(13, *up_sum.take(), *down_sum.take())
-    at_step(15, *up_sum.take(), *down_sum.take())
+    tracks = (down[:1] + up[:1], down[1:] + up[1:] + [out])
+    for step in range(1, 16):
+        for one in tracks[(step + 1) % 2]:
+            at_step(step, *one.take())
     attend_pull(r, c, hooks)
     r.dq_out[...] = (r.dqt[half:D, :] * HEAD**-0.5).astype(BF)
     dq_c = net.send(r.dq_out, r.from_c.at[0:half], "c")
@@ -898,24 +905,31 @@
     dq_c.wait()
     r.dsum[rows16((1 - c) * half, half), :] = r.from_c[0:half, :]
 
-    stage_qkv_weights(r)
-    qkv_sum = summed("qkv", 2)
-    advance(qkv_sum, up_sum)
+    qkv = [summed("qkv", part, half, 2) for part in range(3)]
+    c2 = [summed("c2", part, D, 1) for part in range(3)]
+    c1 = summed("c1", 0, r.g_c1.shape[0], 1)
+    vecs = small_sum(net, r.small, r.got_small, orders("vec", bits)[0])
+    rest = down + up + [out]
+    r.normedt[...] = r.normed[...].astype(F32).T.astype(BF)
+    for part in (1, 2, 0):
+        stage_qkv_weights(r, part)
+        advance(qkv[part])
     stage_qkv_pull(r)
+    advance(*qkv, *rest)
+    stage_norm_pull(r)
     rim = [net.send(r.sg.at[0:16], r.slots.at[0, i], dim) for i, dim in enumerate(("c", "y"))]
-    advance(qkv_sum)
-    stage_conv2_weights(r)
-    c2_sum = summed("c2", 1)
-    advance(c2_sum)
+    for part in range(3):
+        stage_conv2_weights(r, part)
+        advance(c2[part])
+    advance(*qkv)
     wait_all(rim)
     stage_conv2_pull(r, pick_next(net, r.slots.at[0]))
+    advance(*c2, *qkv, *rest)
+    stage_first_pull(r)
     rim = [net.send(r.fe.at[0:16], r.slots.at[1, i], dim) for i, dim in enumerate(("c", "y"))]
     rim += [net.send(r.fo.at[T - 16 : T], r.slots.at[2, i], dim) for i, dim in enumerate(("c", "y"))]
-    advance(c2_sum)
     stage_conv1_weights(r)
-    c1_sum = summed("c1", 1)
-    vec_sum = small_sum(net, r.small, r.got_small, order["vec"])
-    advance(c1_sum, vec_sum, qkv_sum)
+    advance(c1, vecs, *c2, *qkv)
     wait_all(rim)
     stage_mel(r, pick_next(net, r.slots.at[1]), pick_prev(net, r.slots.at[2]))
     rows_of_yours = rows16((1 - sub) * T, T)
@@ -925,12 +939,12 @@
         net.here(r.enc_got, r.enc_o.at[rows_of_yours]),
         net.here(r.melg, r.mel_o.at[rows_of_mine]),
     ]
-    drain(c1_sum, vec_sum, c2_sum, qkv_sum, up_sum, down_sum)
+    drain(c1, vecs, *c2, *qkv, *rest)
 
     ends.append(net.here(r.done_down, r.down_o))
     for j in range(side):
         ends.append(net.here(r.done_up.at[j * D : (j + 1) * D], r.up_o.at[:, j * D : (j + 1) * D]))
-    ends.append(net.here(r.done_up.at[side * D : side * D + half], r.out_o))
+    ends.append(net.here(r.done_out, r.out_o))
     for part in range(3):
         for j in range(2):
             ends.append(
@@ -950,8 +964,7 @@
 def run_layer(bits, near, far, outs, T, D, F2, lanes):
     half, H = D // 2, D // HEAD
     td, dt = (T, D), (D, T)
-    order = orders(bits)
-    buckets = dict(down=(F2, 2), up=(F2 + half, 2), qkv=(3 * half, 2), c2=(6 * half, 1), c1=(lanes, 1))
+    buckets = dict(down=(D, 2, F2 // D), up=(D, 2, F2 // D), out=(half, 2, 1), qkv=(half, 2, 3), c2=(D, 1, 3), c1=(lanes, 1, 1))
     scratch = dict(
         melbuf=((128, 4 * T + 256), BF),
         mele=((T + 24, 128), F32),
@@ -1007,15 +1020,17 @@
         melg=((T, 256), BF),
         melg_got=((T, 256), BF),
         small=((16, D), F32),
-        got_small=((sum(len(subsets(dims)) for dims in order["vec"]), 16, D), F32),
+        got_small=((bits + 2, 16, D), F32),
         slots=((3, 2, 16, D), BF),
     )
     alias = T == D
-    for n, (rows, halves) in buckets.items():
-        if n == "c1" or n in ("down", "up"):
-            scratch["g_" + n] = ((rows * halves, D), BF)
-        scratch["got_" + n] = ((sum_plan(rows, halves, order[n])[1], D), BF)
-        scratch["done_" + n] = ((rows, D), BF)
+    for n, (rows, halves, parts) in buckets.items():
+        if n not in ("qkv", "c2"):
+            scratch["g_" + n] = ((rows * halves * parts, D), BF)
+        for part in range(parts):
+            need = sum_plan(rows, halves, orders(n, bits)[part])[1]
+            scratch["got_%s%d" % (n, part)] = ((need, D), BF)
+        scratch["done_" + n] = ((rows * parts, D), BF)
     if not alias:
         scratch.update(g_qkv=((6 * half, D), BF), g_c2=((6 * half, D), BF), normedt=(dt, BF))
     names = list(near) + list(far) + list(outs) + list(scratch) + ["send", "recv", "own"]
@@ -1038,7 +1053,7 @@
         in_specs=[vmem] * len(near) + [anywhere] * len(far),
         out_specs=[anywhere] * len(outs),
         scratch_shapes=[pltpu.VMEM(*s) for s in scratch.values()]
-        + [pltpu.SemaphoreType.DMA((200,)), pltpu.SemaphoreType.DMA((200,)), pltpu.SemaphoreType.DMA((40,))],
+        + [pltpu.SemaphoreType.DMA((256,)), pltpu.SemaphoreType.DMA((256,)), pltpu.SemaphoreType.DMA((40,))],
         compiler_params=pltpu.CompilerParams(
             vmem_limit_bytes=VMEM_LIMIT, collective_id=1, has_side_effects=True
         ),

time: 234 us -> 233 us (level)
  no operation moved by 1% of the time
where the time goes in v7:
time: 233 us
  Pallas kernels  232 us (100%)
    pallas_call x1, Pallas kernels, run_layer(): pl.pallas_call(kernel, name='layer', out_shape=[jax.ShapeDtypeStruct(*o)...  224 us
    pallas_call x1, Pallas kernels, run_finish(): pl.pallas_call(kernel, name='finish', out_shape=[jax.ShapeDtypeStruct(*o)...  7.97 us

profile of v7, /device:TPU:0, one launch (start us, length us, event | category | flops | bytes accessed | tf_op | source)
XLA Modules:
  0.0 233.1 jit_solution(11616709571740722785)
XLA Ops:
  0.7 224.3 %layer.1 = (bf16[1024,512]{1,0:T(8,128)(2,1)}, bf16[1024,256]{1,0:T(8,128)(2,1)}, bf16[1024,512]{1,0:T(8,128)(2,1)}, bf16[512,1024]{1,0:T(8,128)(2,1)}, bf16[256...) custom-call(bf16[3,80,512]{2,1,0:T(8,128)(2,1)} %refs_0_.1, ...), custom_call_target="tpu_custom_call" | custom-call | tf_op jit(solution)/shard_map/layer/pallas_call | solution.py:1049
  225.0 8.0 %finish.1 = (bf16[1,1024,512]{2,1,0:T(8,128)(2,1)}, f32[1,80,2048]{2,1,0:T(8,128)}, f32[3,80,512]{2,1,0:T(8,128)}, f32[3,512,512]{2,1,0:T(8,128)}, f32[3,512,256...) custom-call(bf16[1024,512]{1,0:T(8,128)(2,1)} %get-tuple-element.45., ...), custom_call_target="tpu_custom_call" | custom-call | tf_op jit(solution)/shard_map/finish/pallas_call | solution.py:1117

commit v8 on v7

--- a/solution.py
+++ b/solution.py
@@ -139,7 +139,11 @@
         r.dge[rows, :] = slope
 
     rows_loop(T, 32, even)
-    r.tmp[...] = nn(r.xo[...], w1)
+
+
+def stage_odd(r):
+    T, D = r.stream.shape
+    r.tmp[...] = nn(r.xo[...], r.w1p[...])
 
     def odd(rows):
         value, slope = gelu_both(r.tmp[rows, :] + vec(r, C1B))
@@ -182,18 +186,16 @@
     rows_loop(T, 32, one)
 
 
-def stage_qkv(r, part):
+def stage_qkv(r, part, h):
     T, D = r.stream.shape
     half, qr = D // 2, D // 4
     bias, scale = ((QB, HEAD**-0.5), (None, 1.0), (VB, 1.0))[part]
-    for h in range(2):
-        value = nn(r.normed[...], r.wqkv[h, part])
-        if bias is not None:
-            value = value + r.vecs[bias : bias + 1, h * half : (h + 1) * half]
-        value = (value.astype(BF).astype(F32) * scale).T.astype(BF)
-        for k in range(2):
-            at = (3 * (3 + k) + part) * half + h * qr
-            r.kv[at : at + qr, :] = value[k * qr : (k + 1) * qr, :]
+    value = nn(r.normed[...], r.wqkv[h, part])
+    if bias is not None:
+        value = value + r.vecs[bias : bias + 1, pl.ds(pl.multiple_of(h * half, half), half)]
+    value = (value.astype(BF).astype(F32) * scale).T.astype(BF)
+    for k in range(2):
+        r.kv[rows16((3 * (3 + k) + part) * half + h * qr, qr), :] = value[k * qr : (k + 1) * qr, :]
 
 
 def at_head(start, h):
@@ -203,6 +205,8 @@
 def head_loop(steps, hooks, body):
     def one(step, carry):
         for at, todo in hooks.items():
+            if not todo:
+                continue
 
             @pl.when(step == at)
             def _(todo=todo):
@@ -215,7 +219,7 @@
     lax.fori_loop(0, steps, one, 0)
 
 
-def attend(r, c, hooks):
+def attend(r, c, m, hooks):
     S, T = r.kv.shape[0] // 15, r.kv.shape[1]
     heads = S // HEAD
     r.top[...] = jnp.full(r.top.shape, -jnp.inf, F32)
@@ -223,7 +227,9 @@
     r.mixt[...] = jnp.zeros(r.mixt.shape, F32)
 
     def body(step):
-        g, h = step // heads, step % heads
+        quarter, u, pair = step // heads, step % heads, heads // 2
+        g = 2 * (quarter // 2) + u // pair
+        h = (m + (1 - 2 * m) * ((quarter + 1) // 2 % 2)) * pair + u % pair
         own = (3 - g) // 3
         slot = own * (3 + c) + (1 - own) * ((g + 1) % 3)
         k = r.kv[at_head((3 * slot + 1) * S, h), :]
@@ -687,6 +693,10 @@
     return Track(acts + [end])
 
 
+def ready(*names):
+    pass
+
+
 def advance(*sums):
     for one in sums:
         for act in one.take():
@@ -722,13 +732,51 @@
 
 
 ORDERS = dict(
-    down=("xczwy", "zcxwy"),
-    up=("xyzwc", "zyxwc"),
-    out=("cxzwy",),
-    qkv=("xczwy", "zxcwy", "ycxzw"),
-    c2=("cxyzw", "yzcxw", "xyzcw"),
-    c1=("zcxyw",),
+    down=("ycwzx", "cyxzw"),
+    up=("cxzyw", "cyzwx"),
+    out=("cyzxw",),
+    qkv=("cyzxw", "czyxw", "cxzyw"),
+    c2=("cxywz", "cyzxw", "czxyw"),
+    c1=("cxyzw",),
     vec=("cyxzw",),
+)
+SCHEDULE = dict(
+    ff2=("down0", "up0"),
+    ff3=("up0",),
+    ffo=("down1", "up1"),
+    out=("down1", "up0", "up1", "out0"),
+    pull0=("down0",),
+    pull1=("down0", "up0", "out0"),
+    pull4=("down0", "up0"),
+    pull6=("down0", "down1", "up0", "up1", "out0"),
+    pull7=("down0",),
+    pull8=("down0", "down1", "up0", "out0"),
+    pull9=("up1", "out0"),
+    pull11=("down0", "down1", "up0", "out0"),
+    pull12=("up1",),
+    pull13=("down1", "up0", "up1", "out0"),
+    pull14=("up0",),
+    pull15=("down0", "down1", "up1", "out0"),
+    home=("down0",),
+    qkvw1=("qkv1",),
+    qkvw2=("qkv2",),
+    qkvw0=("down1", "up1", "out0", "qkv0"),
+    norm=("qkv1", "qkv2"),
+    c2=("out0", "qkv0"),
+    c2w0=("c20",),
+    c2w1=("down1", "c21"),
+    c2w2=("up1", "c22"),
+    first=("qkv1", "qkv2", "c20"),
+    c1=("down1", "up1", "qkv0", "c21", "c22"),
+    c1w=("qkv1", "qkv2", "c10", "vec"),
+    mel=("qkv0", "qkv1", "c20", "c10", "vec"),
+    end=(
+        "qkv2", "c21", "c22", "qkv0", "qkv1", "qkv2", "c10", "vec", "c22", "c20", "vec", "qkv0",
+        "qkv1", "qkv2", "c21", "c10", "c22", "c20", "qkv1", "c21", "qkv0", "c10", "vec", "c22",
+        "qkv0", "qkv2", "c20", "c21", "c10", "qkv2", "c22", "qkv2", "c20", "c21", "c10", "vec",
+        "c22", "qkv1", "c21", "qkv0", "c10", "c20", "qkv1", "c22", "qkv0", "c21", "c20", "c10",
+        "c10", "c22", "c21", "c20", "c22", "c21", "c20",
+    ),
 )
 
 
@@ -771,11 +819,6 @@
     src = pl.ds(pl.multiple_of(128 + (1 - c) * (span - 128), 128), 128)
     dst = pl.ds(pl.multiple_of(c * (span + 128), 128), 128)
     mel_rim = net.send(r.melbuf.at[0:mels, src], r.melbuf.at[0:mels, dst], "c")
-    piece = rows16(c * half, half)
-    qkv_own.wait()
-    mine = r.wqkv.at[m, :, piece]
-    qkv_y = net.send(mine, mine, "y")
-
     p = 4 * c + 2 * net.bit(0) + net.bit(1) if bits > 1 else 2 * c + net.bit(0)
     cuts = 8 if bits > 1 else 4
 
@@ -787,49 +830,84 @@
         parts = [r.wo.at[wo], r.up.at[of, cut(D, 0)], r.down.at[cut(F2, of * F2)]]
         return [net.copy(x, x, dim) for x in parts]
 
+    def pass_qkv(of, at, count, dim):
+        rows = r.wqkv.at[of, :, rows16(at * (D // cuts), count * (D // cuts))]
+        return net.copy(rows, rows, dim)
+
+    two = 2 if bits > 1 else 1
+    qkv_y = pass_qkv(m, p, 1, "y")
+    qkv_z = [pass_qkv(1 - m, p, 1, 1)] if bits > 1 else []
+    qkv_x = pass_qkv(1 - m, (p // two) * two, two, 0)
+    qkv_c = pass_qkv(1 - m, c * (cuts // 2), cuts // 2, "c")
+    ff_y = pass_on(m, p, 1, "y")
+    ff_z = pass_on(1 - m, p, 1, 1) if bits > 1 else []
+    ff_x = pass_on(1 - m, (p // two) * two, two, 0)
+    ff_c = pass_on(1 - m, c * (cuts // 2), cuts // 2, "c")
+    qkv_own.wait()
+    qkv_y.start()
+    wait_all(own)
     r.small[...] = jnp.zeros_like(r.small)
     mel_rim.wait()
     stage_mel_rows(r, sub)
+    start_all(ff_y)
     stage_first(r, jnp.logical_and(c == 0, m == 0))
     qkv_y.wait()
-    arrived = r.wqkv.at[1 - m, :, piece]
-    qkv_c = net.send(arrived, arrived, "c")
-    wait_all(own)
-    ff_y = pass_on(m, p, 1, "y")
-    start_all(ff_y)
+    start_all(qkv_z)
+    stage_odd(r)
+    wait_all(qkv_z)
+    qkv_x.start()
+    wait_all(ff_y)
+    start_all(ff_z)
     w2_own.wait()
     stage_second(r, quarter(net))
     vec_copy.wait()
     r.vecs[8:16, :] = r.vec_mine[...] + r.vec_got[...]
-    qkv_c.wait()
-
-    def block(slot, part, parts=1):
-        return r.kv.at[rows16((3 * slot + part) * half, parts * half)]
-
-    to_y, to_d = [], []
-    for part in (1, 2):
-        stage_qkv(r, part)
-        to_y.append(net.send(block(3 + c, part), block(0, part), "y"))
-        to_d.append(net.send(block(4 - c, part), block(1, part), "c", "y"))
-    stage_qkv(r, 0)
-    to_c = [net.send(block(4 - c, part), block(2, part), "c") for part in range(3)]
-    wait_all(ff_y)
-    ff_z = pass_on(1 - m, p, 1, 1) if bits > 1 else []
-    start_all(ff_z)
-    ff_x = pass_on(1 - m, (p // 2) * 2 if bits > 1 else p, 2 if bits > 1 else 1, 0)
-    ff_c = pass_on(1 - m, c * (cuts // 2), cuts // 2, "c")
+    qkv_x.wait()
+    qkv_c.start()
+
+    def block(slot, part, h):
+        return r.kv.at[rows16((3 * slot + part) * half + h * (half // 2), half // 2)]
+
+    def project(h):
+        far = []
+        for part in (1, 2):
+            stage_qkv(r, part, h)
+            far.append(net.copy(block(3 + c, part, h), block(0, part, h), "y"))
+            far.append(net.copy(block(4 - c, part, h), block(1, part, h), "c", "y"))
+            start_all(far[-2:])
+        stage_qkv(r, 0, h)
+        near = [net.copy(block(4 - c, part, h), block(2, part, h), "c") for part in range(3)]
+        start_all(near)
+        return far, near
+
+    far_own, near_own = project(m)
     stage_mask(r, sub)
-    to_c[0].wait()
+    wait_all(near_own)
     heads = half // HEAD
-    attend(
-        r,
-        c,
-        {
-            heads: [lambda: wait_all(to_c[1:]), lambda: wait_all(ff_z), lambda: start_all(ff_x)],
-            2 * heads: [lambda: wait_all(ff_x), lambda: start_all(ff_c), lambda: wait_all(to_y)],
-            3 * heads: [lambda: wait_all(to_d)],
-        },
-    )
+    far_other = [
+        net.copy(block(own, part, 1 - m), block(to, part, 1 - m), *dims)
+        for part in (1, 2)
+        for own, to, dims in ((3 + c, 0, ("y",)), (4 - c, 1, ("c", "y")))
+    ]
+    near_other = [net.copy(block(4 - c, part, 1 - m), block(2, part, 1 - m), "c") for part in range(3)]
+
+    def project_other():
+        qkv_c.wait()
+        stage_qkv(r, 1, 1 - m)
+        start_all(far_other[0:2])
+        stage_qkv(r, 2, 1 - m)
+        start_all(far_other[2:4])
+        stage_qkv(r, 0, 1 - m)
+        start_all(near_other)
+
+    hooks = {
+        heads - 1: [project_other],
+        heads: [lambda: wait_all(near_other), lambda: wait_all(ff_z), lambda: start_all(ff_x)],
+        2 * heads: [lambda: wait_all(far_own)],
+        5 * heads // 2: [lambda: wait_all(ff_x), lambda: start_all(ff_c)],
+        3 * heads: [lambda: wait_all(far_other)],
+    }
+    attend(r, c, m, hooks)
     attend_end(r, 1)
     mix_c = net.send(r.mixb.at[half:D], r.mix_got, "c")
     attend_end(r, 0)
@@ -845,19 +923,41 @@
         ]
         return bucket_sum(net, *views, halves, orders(n, bits)[part])
 
-    down = [summed("down", part, D, 2) for part in range(side)]
-    up = [summed("up", part, D, 2) for part in range(side)]
+    tracks = {}
+    for n, rows, halves, parts in (
+        ("down", D, 2, side),
+        ("up", D, 2, side),
+        ("out", half, 2, 1),
+        ("qkv", half, 2, 3),
+        ("c2", D, 1, 3),
+        ("c1", r.g_c1.shape[0], 1, 1),
+    ):
+        for part in range(parts):
+            tracks["%s%d" % (n, part)] = summed(n, part, rows, halves)
+    tracks["vec"] = small_sum(net, r.small, r.got_small, orders("vec", bits)[0])
+
+    def acts_at(name):
+        return [act for n in SCHEDULE.get(name, ()) if n in tracks for act in tracks[n].take()]
+
+    def point(name):
+        for act in acts_at(name):
+            act()
+
     hooks = {}
-    for part in range(side - 1):
-        hooks[2 * part + 2] = down[part].take() + up[part].take()
+    for step in range(2 * side):
+        if step and step % 2 == 0:
+            ready("down%d" % (step // 2 - 1), "up%d" % (step // 2 - 1))
+        hooks[step] = acts_at("ff%d" % step)
     stage_ff(r, hooks)
+    ready("down%d" % (side - 1), "up%d" % (side - 1))
+    point("ffo")
     stage_mid_pull(r)
     stage_do(r, c, False)
     do_c = net.send(r.dot_out, r.dot.at[half:D], "c")
-    advance(down[-1], up[-1])
+    point("mid")
     stage_out_weights(r, c)
-    out = summed("out", 0, half, 2)
-    advance(out)
+    ready("out0")
+    point("out")
     stage_do(r, c, True)
     stage_diag(r, 0)
     do_c.wait()
@@ -880,14 +980,13 @@
     at_step(8, home_d.start)
     at_step(11, lambda: start_all(enc))
     at_step(12, home_c.start)
-    tracks = (down[:1] + up[:1], down[1:] + up[1:] + [out])
-    for step in range(1, 16):
-        for one in tracks[(step + 1) % 2]:
-            at_step(step, *one.take())
+    for step in range(16):
+        at_step(step, *acts_at("pull%d" % step))
     attend_pull(r, c, hooks)
     r.dq_out[...] = (r.dqt[half:D, :] * HEAD**-0.5).astype(BF)
     dq_c = net.send(r.dq_out, r.from_c.at[0:half], "c")
     r.dsum[rows16(c * half, half), :] = (r.dqt[0:half, :] * HEAD**-0.5).astype(BF)
+    point("home")
     home_y.wait()
     home_d.wait()
     home_c.wait()
@@ -905,41 +1004,42 @@
     dq_c.wait()
     r.dsum[rows16((1 - c) * half, half), :] = r.from_c[0:half, :]
 
-    qkv = [summed("qkv", part, half, 2) for part in range(3)]
-    c2 = [summed("c2", part, D, 1) for part in range(3)]
-    c1 = summed("c1", 0, r.g_c1.shape[0], 1)
-    vecs = small_sum(net, r.small, r.got_small, orders("vec", bits)[0])
-    rest = down + up + [out]
     r.normedt[...] = r.normed[...].astype(F32).T.astype(BF)
     for part in (1, 2, 0):
         stage_qkv_weights(r, part)
-        advance(qkv[part])
+        ready("qkv%d" % part)
+        point("qkvw%d" % part)
     stage_qkv_pull(r)
-    advance(*qkv, *rest)
+    point("norm")
     stage_norm_pull(r)
     rim = [net.send(r.sg.at[0:16], r.slots.at[0, i], dim) for i, dim in enumerate(("c", "y"))]
+    point("c2")
     for part in range(3):
         stage_conv2_weights(r, part)
-        advance(c2[part])
-    advance(*qkv)
+        ready("c2%d" % part)
+        point("c2w%d" % part)
     wait_all(rim)
     stage_conv2_pull(r, pick_next(net, r.slots.at[0]))
-    advance(*c2, *qkv, *rest)
+    point("first")
     stage_first_pull(r)
     rim = [net.send(r.fe.at[0:16], r.slots.at[1, i], dim) for i, dim in enumerate(("c", "y"))]
     rim += [net.send(r.fo.at[T - 16 : T], r.slots.at[2, i], dim) for i, dim in enumerate(("c", "y"))]
+    point("c1")
     stage_conv1_weights(r)
-    advance(c1, vecs, *c2, *qkv)
+    ready("c10", "vec")
+    point("c1w")
     wait_all(rim)
     stage_mel(r, pick_next(net, r.slots.at[1]), pick_prev(net, r.slots.at[2]))
     rows_of_yours = rows16((1 - sub) * T, T)
     mel_y = net.send(r.melg, r.melg_got, "y")
+    point("mel")
     wait_all(enc)
     ends = [
         net.here(r.enc_got, r.enc_o.at[rows_of_yours]),
         net.here(r.melg, r.mel_o.at[rows_of_mine]),
     ]
-    drain(c1, vecs, *c2, *qkv, *rest)
+    point("end")
+    drain(*tracks.values())
 
     ends.append(net.here(r.done_down, r.down_o))
     for j in range(side):

time: 233 us -> 196 us (0.84)
  Pallas kernels: 232 us -> 195 us
    pallas_call x1, Pallas kernels: 224 us -> 187 us  [run_layer(): pl.pallas_call(kernel, name='layer', out_shape=[jax.ShapeDtypeStruct(*o)...]
where the time goes in v8:
time: 196 us; the launch traced here: 195 us
  Pallas kernels  195 us (99%)
    pallas_call x1, Pallas kernels, run_layer(): pl.pallas_call(kernel, name='layer', out_shape=[jax.ShapeDtypeStruct(*o)...  187 us
    pallas_call x1, Pallas kernels, run_finish(): pl.pallas_call(kernel, name='finish', out_shape=[jax.ShapeDtypeStruct(*o)...  7.97 us

profile of v8, /device:TPU:0, one launch (start us, length us, event | category | flops | bytes accessed | tf_op | source)
XLA Modules:
  0.0 195.4 jit_solution(6526847567190498443)
XLA Ops:
  0.7 186.6 %layer.1 = (bf16[1024,512]{1,0:T(8,128)(2,1)}, bf16[1024,256]{1,0:T(8,128)(2,1)}, bf16[1024,512]{1,0:T(8,128)(2,1)}, bf16[512,1024]{1,0:T(8,128)(2,1)}, bf16[256...) custom-call(bf16[3,80,512]{2,1,0:T(8,128)(2,1)} %refs_0_.1, ...), custom_call_target="tpu_custom_call" | custom-call | tf_op jit(solution)/shard_map/layer/pallas_call | solution.py:1149
  187.3 8.0 %finish.1 = (bf16[1,1024,512]{2,1,0:T(8,128)(2,1)}, f32[1,80,2048]{2,1,0:T(8,128)}, f32[3,80,512]{2,1,0:T(8,128)}, f32[3,512,512]{2,1,0:T(8,128)}, f32[3,512,256...) custom-call(bf16[1024,512]{1,0:T(8,128)(2,1)} %get-tuple-element.45., ...), custom_call_target="tpu_custom_call" | custom-call | tf_op jit(solution)/shard_map/finish/pallas_call | solution.py:1217

commit v9 on v8

--- a/solution.py
+++ b/solution.py
@@ -90,7 +90,7 @@
     return jnp.sum(value, axis=0, keepdims=True)
 
 
-def stage_mel_rows(r, sub):
+def stage_mel_rows(r, sub, rim_came):
     T, D = r.stream.shape
     row = lax.broadcasted_iota(jnp.int32, (256, 256), 0)
     lane = lax.broadcasted_iota(jnp.int32, (256, 256), 1)
@@ -106,14 +106,15 @@
     def select(at, to):
         return jnp.where(jnp.logical_and(row == to, lane == at), 1.0, 0.0).astype(BF)
 
+    for k in range(T // 128):
+        both = nt(pick, lanes(128 + 256 * k, 256))
+        r.mele[8 + 128 * k : 136 + 128 * k, :] = both[0:128, :]
+        r.melo[8 + 128 * k : 136 + 128 * k, :] = both[128:256, :]
+    rim_came()
     before, after = lanes(0, 128), lanes(128 + 2 * T, 128)
     r.mele[0:8, :] = nt(select(126, 7), before)[0:8, :]
     r.melo[0:8, :] = nt(select(127, 7), before)[0:8, :]
     r.mele[T + 8 : T + 16, :] = nt(select(0, 0), after)[0:8, :]
-    for k in range(T // 128):
-        both = nt(pick, lanes(128 + 256 * k, 256))
-        r.mele[8 + 128 * k : 136 + 128 * k, :] = both[0:128, :]
-        r.melo[8 + 128 * k : 136 + 128 * k, :] = both[128:256, :]
 
 
 def three(a, b, c):
@@ -265,10 +266,12 @@
     lax.fori_loop(0, heads, one, 0)
 
 
-def stage_mid(r, c):
+def stage_mid(r, c, mix_came, weights_came):
     T, D = r.stream.shape
     half = D // 2
+    weights_came()
     r.tmp[...] = tn(r.mixb[0:half, :], r.wo[rows16(c * half, half), :])
+    mix_came()
     r.tmp[...] += tn(r.mix_got[...], r.wo[rows16((1 - c) * half, half), :])
 
     def one(rows):
@@ -283,7 +286,6 @@
     T, D = r.stream.shape
     side = r.up.shape[2] // D
     parts, width = 2 * side, D
-    add_small(r, DNB, col(r.bg[...].astype(F32)))
 
     def chunk(t):
         into, at = t % 2, t // 2
@@ -732,57 +734,68 @@
 
 
 ORDERS = dict(
-    down=("ycwzx", "cyxzw"),
-    up=("cxzyw", "cyzwx"),
-    out=("cyzxw",),
-    qkv=("cyzxw", "czyxw", "cxzyw"),
-    c2=("cxywz", "cyzxw", "czxyw"),
-    c1=("cxyzw",),
-    vec=("cyxzw",),
+    down=("c x y w z", "c zy w x"),
+    up=("c xy wz", "c zy x w"),
+    out=("c zy wx",),
+    qkv=("c y z x w", "c xz yw", "c z x y w"),
+    c2=("c z xy w", "c yx z w", "c x zy w"),
+    c1=("c y xz w",),
+    vec=("c w x y z",),
 )
 SCHEDULE = dict(
     ff2=("down0", "up0"),
-    ff3=("up0",),
-    ffo=("down1", "up1"),
-    out=("down1", "up0", "up1", "out0"),
-    pull0=("down0",),
-    pull1=("down0", "up0", "out0"),
-    pull4=("down0", "up0"),
-    pull6=("down0", "down1", "up0", "up1", "out0"),
-    pull7=("down0",),
-    pull8=("down0", "down1", "up0", "out0"),
-    pull9=("up1", "out0"),
-    pull11=("down0", "down1", "up0", "out0"),
-    pull12=("up1",),
-    pull13=("down1", "up0", "up1", "out0"),
-    pull14=("up0",),
-    pull15=("down0", "down1", "up1", "out0"),
+    ffo=("down0", "down1", "up0", "up1"),
+    out=("down1", "up1", "out0"),
+    pull1=("out0",),
+    pull2=("down0",),
+    pull4=("up0",),
+    pull6=("down1", "up1", "out0"),
+    pull7=("down0", "up0"),
+    pull8=("up1", "out0"),
+    pull10=("down1",),
+    pull11=("up0", "up1", "out0"),
+    pull12=("down0", "down1"),
+    pull13=("up0", "up1", "out0"),
+    pull14=("down0", "down1"),
+    pull15=("up0", "up1", "out0"),
     home=("down0",),
-    qkvw1=("qkv1",),
+    qkvw1=("down1", "up1", "qkv1"),
     qkvw2=("qkv2",),
-    qkvw0=("down1", "up1", "out0", "qkv0"),
-    norm=("qkv1", "qkv2"),
-    c2=("out0", "qkv0"),
+    qkvw0=("down0", "qkv0"),
+    norm=("up1", "qkv1"),
+    c2=("down1", "qkv0", "qkv2"),
     c2w0=("c20",),
-    c2w1=("down1", "c21"),
-    c2w2=("up1", "c22"),
-    first=("qkv1", "qkv2", "c20"),
-    c1=("down1", "up1", "qkv0", "c21", "c22"),
-    c1w=("qkv1", "qkv2", "c10", "vec"),
-    mel=("qkv0", "qkv1", "c20", "c10", "vec"),
+    c2w1=("c21",),
+    c2w2=("c22",),
+    first=("down0", "down1", "qkv1", "c20", "c21", "c22"),
+    c1=("qkv0", "qkv2"),
+    c1w=("down0", "c10", "vec"),
+    mel=("qkv0", "qkv1", "qkv2", "c20", "c21", "c10", "vec"),
     end=(
-        "qkv2", "c21", "c22", "qkv0", "qkv1", "qkv2", "c10", "vec", "c22", "c20", "vec", "qkv0",
-        "qkv1", "qkv2", "c21", "c10", "c22", "c20", "qkv1", "c21", "qkv0", "c10", "vec", "c22",
-        "qkv0", "qkv2", "c20", "c21", "c10", "qkv2", "c22", "qkv2", "c20", "c21", "c10", "vec",
-        "c22", "qkv1", "c21", "qkv0", "c10", "c20", "qkv1", "c22", "qkv0", "c21", "c20", "c10",
-        "c10", "c22", "c21", "c20", "c22", "c21", "c20",
+        "c22", "qkv1", "qkv0", "c21", "vec", "qkv2", "c20", "c22", "qkv0", "qkv1", "c10", "c21",
+        "vec", "qkv2", "c20", "qkv1", "c22", "qkv0", "vec", "c10", "c21", "qkv2", "c20", "c22",
+        "qkv0", "c10", "vec", "c21", "qkv2", "c20", "c22", "c10", "qkv0", "c21", "qkv2", "qkv0",
+        "c10", "c20", "c22", "c21", "qkv2", "c10", "c20", "c22",
     ),
 )
 
 
 def orders(name, bits):
-    dims = dict(c=["c"], y=["y"], x=[0], z=list(range(1, min(2, bits))), w=list(range(2, bits)))
-    return [[(dim,) for ch in spec for dim in dims[ch]] for spec in ORDERS[name]]
+    dims = dict(c=["c"], y=["y"], x=[0], z=list(range(1, min(2, bits))), w=list(range(2, min(3, bits))))
+    found = []
+    for spec in ORDERS[name]:
+        groups = [tuple(dim for ch in group for dim in dims[ch]) for group in spec.split()]
+        found.append([group for group in groups if group] + [(dim,) for dim in range(3, bits)])
+    return found
+
+
+def partners(bits):
+    found = [("c",), ("y",), ("c", "y")] + [(dim,) for dim in range(bits)]
+    for name in ORDERS:
+        for order in orders(name, bits):
+            for dims in order:
+                found += [one for one in subsets(dims) if set(one) not in [set(x) for x in found]]
+    return found
 
 
 def layer(r, bits):
@@ -813,7 +826,7 @@
         r.vec_mine[pl.ds(2 + m * side + k, 1), :] = r.upb[k * D : (k + 1) * D].astype(F32).reshape(1, D)
     for k, n in enumerate(ROW_BIASES):
         r.vecs[k : k + 1, :] = getattr(r, n)[...].astype(F32).reshape(1, D)
-    net.greet([("c",), ("y",), ("c", "y")] + [(k,) for k in range(bits)])
+    net.greet(partners(bits))
     vec_copy = net.send(r.vec_mine, r.vec_got, "y")
     mel_own.wait()
     src = pl.ds(pl.multiple_of(128 + (1 - c) * (span - 128), 128), 128)
@@ -831,14 +844,13 @@
         return [net.copy(x, x, dim) for x in parts]
 
     def pass_qkv(of, at, count, dim):
-        rows = r.wqkv.at[of, :, rows16(at * (D // cuts), count * (D // cuts))]
+        rows = r.wqkv.at[of, :, rows16(at * (D // 4), count * (D // 4))]
         return net.copy(rows, rows, dim)
 
     two = 2 if bits > 1 else 1
-    qkv_y = pass_qkv(m, p, 1, "y")
-    qkv_z = [pass_qkv(1 - m, p, 1, 1)] if bits > 1 else []
-    qkv_x = pass_qkv(1 - m, (p // two) * two, two, 0)
-    qkv_c = pass_qkv(1 - m, c * (cuts // 2), cuts // 2, "c")
+    qkv_y = pass_qkv(m, 2 * c + net.bit(0), 1, "y")
+    qkv_x = pass_qkv(1 - m, 2 * c + net.bit(0), 1, 0)
+    qkv_c = pass_qkv(1 - m, 2 * c, 2, "c")
     ff_y = pass_on(m, p, 1, "y")
     ff_z = pass_on(1 - m, p, 1, 1) if bits > 1 else []
     ff_x = pass_on(1 - m, (p // two) * two, two, 0)
@@ -847,41 +859,38 @@
     qkv_y.start()
     wait_all(own)
     r.small[...] = jnp.zeros_like(r.small)
-    mel_rim.wait()
-    stage_mel_rows(r, sub)
+    stage_mel_rows(r, sub, mel_rim.wait)
     start_all(ff_y)
     stage_first(r, jnp.logical_and(c == 0, m == 0))
+    stage_odd(r)
     qkv_y.wait()
-    start_all(qkv_z)
-    stage_odd(r)
-    wait_all(qkv_z)
     qkv_x.start()
+    w2_own.wait()
+    stage_second(r, quarter(net))
     wait_all(ff_y)
     start_all(ff_z)
-    w2_own.wait()
-    stage_second(r, quarter(net))
     vec_copy.wait()
     r.vecs[8:16, :] = r.vec_mine[...] + r.vec_got[...]
+
+    def block(slot, part, h):
+        return r.kv.at[rows16((3 * slot + part) * half + h * (half // 2), half // 2)]
+
+    def project(h):
+        far, near = [], []
+        for part in (1, 2, 0):
+            stage_qkv(r, part, h)
+            if part:
+                far.append(net.send(block(3 + c, part, h), block(0, part, h), "y"))
+                far.append(net.send(block(4 - c, part, h), block(1, part, h), "c", "y"))
+            near.append(net.send(block(4 - c, part, h), block(2, part, h), "c"))
+        return far, near
+
+    far_own, near_own = project(m)
     qkv_x.wait()
     qkv_c.start()
-
-    def block(slot, part, h):
-        return r.kv.at[rows16((3 * slot + part) * half + h * (half // 2), half // 2)]
-
-    def project(h):
-        far = []
-        for part in (1, 2):
-            stage_qkv(r, part, h)
-            far.append(net.copy(block(3 + c, part, h), block(0, part, h), "y"))
-            far.append(net.copy(block(4 - c, part, h), block(1, part, h), "c", "y"))
-            start_all(far[-2:])
-        stage_qkv(r, 0, h)
-        near = [net.copy(block(4 - c, part, h), block(2, part, h), "c") for part in range(3)]
-        start_all(near)
-        return far, near
-
-    far_own, near_own = project(m)
     stage_mask(r, sub)
+    add_small(r, DNB, col(r.bg[...].astype(F32)))
+    r.normedt[...] = r.normed[...].astype(F32).T.astype(BF)
     wait_all(near_own)
     heads = half // HEAD
     far_other = [
@@ -911,9 +920,7 @@
     attend_end(r, 1)
     mix_c = net.send(r.mixb.at[half:D], r.mix_got, "c")
     attend_end(r, 0)
-    wait_all(ff_c)
-    mix_c.wait()
-    stage_mid(r, c)
+    stage_mid(r, c, mix_c.wait, lambda: wait_all(ff_c))
 
     def summed(n, part, rows, halves):
         views = [
@@ -1004,7 +1011,6 @@
     dq_c.wait()
     r.dsum[rows16((1 - c) * half, half), :] = r.from_c[0:half, :]
 
-    r.normedt[...] = r.normed[...].astype(F32).T.astype(BF)
     for part in (1, 2, 0):
         stage_qkv_weights(r, part)
         ready("qkv%d" % part)
@@ -1092,6 +1098,7 @@
         kv=((15 * half, T), BF),
         mixt=(dt, F32),
         mixb=(dt, BF),
+        normedt=(dt, BF),
         mix_got=((half, T), BF),
         dot=(dt, BF),
         dot_out=((half, T), BF),
@@ -1120,7 +1127,7 @@
         melg=((T, 256), BF),
         melg_got=((T, 256), BF),
         small=((16, D), F32),
-        got_small=((bits + 2, 16, D), F32),
+        got_small=((sum(len(subsets(dims)) for dims in orders("vec", bits)[0]), 16, D), F32),
         slots=((3, 2, 16, D), BF),
     )
     alias = T == D
@@ -1132,7 +1139,7 @@
             scratch["got_%s%d" % (n, part)] = ((need, D), BF)
         scratch["done_" + n] = ((rows * parts, D), BF)
     if not alias:
-        scratch.update(g_qkv=((6 * half, D), BF), g_c2=((6 * half, D), BF), normedt=(dt, BF))
+        scratch.update(g_qkv=((6 * half, D), BF), g_c2=((6 * half, D), BF))
     names = list(near) + list(far) + list(outs) + list(scratch) + ["send", "recv", "own"]
 
     def kernel(*refs):
@@ -1140,7 +1147,6 @@
         for n, ref in zip(names, refs):
             setattr(r, n, ref)
         r.odd, r.smg, r.sg, r.fe, r.fo, r.enc = r.shift, r.mid, r.ntwo, r.act, r.ing, r.bg
-        r.normedt = r.mixb if alias else r.normedt
         if alias:
             r.g_qkv, r.g_c2 = r.kv.at[0 : 6 * half], r.kv.at[6 * half : 12 * half]
         layer(r, bits)

time: 196 us -> 184 us (0.939)
  Pallas kernels: 195 us -> 183 us
    pallas_call x1, Pallas kernels: 187 us -> 175 us  [run_layer(): pl.pallas_call(kernel, name='layer', out_shape=[jax.ShapeDtypeStruct(*o)...]
where the time goes in v9:
time: 184 us; the launch traced here: 183 us
  Pallas kernels  183 us (99%)
    pallas_call x1, Pallas kernels, run_layer(): pl.pallas_call(kernel, name='layer', out_shape=[jax.ShapeDtypeStruct(*o)...  175 us
    pallas_call x1, Pallas kernels, run_finish(): pl.pallas_call(kernel, name='finish', out_shape=[jax.ShapeDtypeStruct(*o)...  7.97 us

profile of v9, /device:TPU:0, one launch (start us, length us, event | category | flops | bytes accessed | tf_op | source)
XLA Modules:
  0.0 183.4 jit_solution(14562160240226959876)
XLA Ops:
  0.7 174.6 %layer.1 = (bf16[1024,512]{1,0:T(8,128)(2,1)}, bf16[1024,256]{1,0:T(8,128)(2,1)}, bf16[1024,512]{1,0:T(8,128)(2,1)}, bf16[512,1024]{1,0:T(8,128)(2,1)}, bf16[256...) custom-call(bf16[3,80,512]{2,1,0:T(8,128)(2,1)} %refs_0_.1, ...), custom_call_target="tpu_custom_call" | custom-call | tf_op jit(solution)/shard_map/layer/pallas_call | solution.py:1155
  175.2 8.0 %finish.1 = (bf16[1,1024,512]{2,1,0:T(8,128)(2,1)}, f32[1,80,2048]{2,1,0:T(8,128)}, f32[3,80,512]{2,1,0:T(8,128)}, f32[3,512,512]{2,1,0:T(8,128)}, f32[3,512,256...) custom-call(bf16[1024,512]{1,0:T(8,128)(2,1)} %get-tuple-element.45., ...), custom_call_target="tpu_custom_call" | custom-call | tf_op jit(solution)/shard_map/finish/pallas_call | solution.py:1223

commit v10 on v9

--- a/solution.py
+++ b/solution.py
@@ -386,18 +386,21 @@
         slot = g + (g // 3) * c
         k = r.kv[at_head((3 * slot + 1) * S, h), :]
         v = r.kv[at_head((3 * slot + 2) * S, h), :]
-        dk, dv = None, None
-        for i, home in enumerate((3 + c, 2)):
-            q = r.kv[at_head(3 * home * S, h), :]
-            rows = at_head(i * S, h)
-            do = r.dot[rows, :]
-            p = jnp.exp(tn(k, q) - r.top[i * heads + h])
-            ds = (p * (tn(v, do) - r.diag[i * heads + h])).astype(BF)
-            dv_i, dk_i = nt(do, p.astype(BF)), nt(q, ds)
-            dk, dv = (dk_i, dv_i) if dk is None else (dk + dk_i, dv + dv_i)
-            r.dqt[rows, :] += nn(k, ds)
-        r.dkv[at_head(2 * g * S, h), :] = dk.astype(BF)
-        r.dkv[at_head((2 * g + 1) * S, h), :] = dv.astype(BF)
+        qs = [r.kv[at_head(3 * home * S, h), :] for home in (3 + c, 2)]
+        dos = [r.dot[at_head(i * S, h), :] for i in range(2)]
+        for i in range(2):
+            top, diag = r.top[i * heads + h], r.diag[i * heads + h]
+            for at in range(0, T, 128):
+                rows, cols = slice(at, at + 128), slice(i * T, (i + 1) * T)
+                p = jnp.exp(tn(k[:, rows], qs[i]) - top)
+                r.pb[rows, cols] = p.astype(BF)
+                r.ds[rows, cols] = (p * (tn(v[:, rows], dos[i]) - diag)).astype(BF)
+        both = [jnp.concatenate(one, axis=1) for one in (qs, dos)]
+        r.dkv[at_head(2 * g * S, h), :] = nt(both[0], r.ds[...]).astype(BF)
+        r.dkv[at_head((2 * g + 1) * S, h), :] = nt(both[1], r.pb[...]).astype(BF)
+        dq = nn(k, r.ds[...])
+        for i in range(2):
+            r.dqt[at_head(i * S, h), :] += dq[:, i * T : (i + 1) * T]
 
     head_loop(4 * heads, hooks, body)
 
@@ -734,13 +737,13 @@
 
 
 ORDERS = dict(
-    down=("c x y w z", "c zy w x"),
-    up=("c xy wz", "c zy x w"),
-    out=("c zy wx",),
-    qkv=("c y z x w", "c xz yw", "c z x y w"),
-    c2=("c z xy w", "c yx z w", "c x zy w"),
-    c1=("c y xz w",),
-    vec=("c w x y z",),
+    down=("c-x-y-w-z", "c-zy-w-x"),
+    up=("c-xy-wz", "c-zy-x-w"),
+    out=("c-zy-wx",),
+    qkv=("c-y-z-x-w", "c-xz-yw", "c-z-x-y-w"),
+    c2=("c-z-xy-w", "c-yx-z-w", "c-x-zy-w"),
+    c1=("c-y-xz-w",),
+    vec=("c-w-x-y-z",),
 )
 SCHEDULE = dict(
     ff2=("down0", "up0"),
@@ -784,7 +787,7 @@
     dims = dict(c=["c"], y=["y"], x=[0], z=list(range(1, min(2, bits))), w=list(range(2, min(3, bits))))
     found = []
     for spec in ORDERS[name]:
-        groups = [tuple(dim for ch in group for dim in dims[ch]) for group in spec.split()]
+        groups = [tuple(dim for ch in group for dim in dims[ch]) for group in spec.split("-")]
         found.append([group for group in groups if group] + [(dim,) for dim in range(3, bits)])
     return found
 
@@ -1118,6 +1121,8 @@
         attg=(td, BF),
         dqt=(dt, F32),
         dq_out=((half, T), BF),
+        pb=((T, 2 * T), BF),
+        ds=((T, 2 * T), BF),
         dkv=((8 * half, T), BF),
         from_y=((2 * half, T), BF),
         from_d=((2 * half, T), BF),

time: 184 us -> 184 us (level)
  no operation moved by 1% of the time
where the time goes in v10:
time: 184 us; the launch traced here: 183 us
  Pallas kernels  183 us (99%)
    pallas_call x1, Pallas kernels, run_layer(): pl.pallas_call(kernel, name='layer', out_shape=[jax.ShapeDtypeStruct(*o)...  175 us
    pallas_call x1, Pallas kernels, run_finish(): pl.pallas_call(kernel, name='finish', out_shape=[jax.ShapeDtypeStruct(*o)...  7.97 us

profile of v10, /device:TPU:0, one launch (start us, length us, event | category | flops | bytes accessed | tf_op | source)
XLA Modules:
  0.0 183.4 jit_solution(1852314828035526916)
XLA Ops:
  0.7 174.6 %layer.1 = (bf16[1024,512]{1,0:T(8,128)(2,1)}, bf16[1024,256]{1,0:T(8,128)(2,1)}, bf16[1024,512]{1,0:T(8,128)(2,1)}, bf16[512,1024]{1,0:T(8,128)(2,1)}, bf16[256...) custom-call(bf16[3,80,512]{2,1,0:T(8,128)(2,1)} %refs_0_.1, ...), custom_call_target="tpu_custom_call" | custom-call | tf_op jit(solution)/shard_map/layer/pallas_call | solution.py:1160
  175.2 8.0 %finish.1 = (bf16[1,1024,512]{2,1,0:T(8,128)(2,1)}, f32[1,80,2048]{2,1,0:T(8,128)}, f32[3,80,512]{2,1,0:T(8,128)}, f32[3,512,512]{2,1,0:T(8,128)}, f32[3,512,256...) custom-call(bf16[1024,512]{1,0:T(8,128)(2,1)} %get-tuple-element.45., ...), custom_call_target="tpu_custom_call" | custom-call | tf_op jit(solution)/shard_map/finish/pallas_call | solution.py:1228

commit v11 on v10

--- a/solution.py
+++ b/solution.py
@@ -426,10 +426,12 @@
         r.g_qkv[at : at + half, half:D] = grad[half:D, :]
 
 
-def stage_qkv_pull(r):
+def stage_qkv_pull(r, queries_came):
     T, D = r.stream.shape
     total = None
-    for part in range(3):
+    for part in (1, 2, 0):
+        if part == 0:
+            queries_came()
         for h in range(2):
             back = nn(r.wqkv[h, part], piece_of(r, part, h))
             total = back if total is None else total + back
@@ -459,8 +461,8 @@
     T, D = r.stream.shape
     sg = r.sg[...]
     r.shift[0:T, :] = nt(sg, r.w2[0])
-    r.shift[T : T + 16, :] = nt(next_row, r.w2[0])
     r.tmp[...] = nt(sg, r.w2[1])
+    r.shift[T : T + 16, :] = nt(next_row(), r.w2[0])
     r.tmp2[...] = nt(sg, r.w2[2]) + r.shift[1 : T + 1, :]
 
 
@@ -550,10 +552,13 @@
         copy.start()
         return copy
 
-    def here(self, src, dst):
+    def here_later(self, src, dst):
         i = self.used_here
         self.used_here += 1
-        copy = pltpu.make_async_copy(src, dst, self.r.own.at[i])
+        return pltpu.make_async_copy(src, dst, self.r.own.at[i])
+
+    def here(self, src, dst):
+        copy = self.here_later(src, dst)
         copy.start()
         return copy
 
@@ -600,6 +605,15 @@
 
     def take(self):
         return [self.acts.pop(0)] if self.acts else []
+
+    def then(self, more):
+        last = self.acts.pop()
+
+        def act():
+            last()
+            more()
+
+        self.acts.append(act)
 
 
 def bucket_sum(net, g, got, done, halves, order):
@@ -737,48 +751,46 @@
 
 
 ORDERS = dict(
-    down=("c-x-y-w-z", "c-zy-w-x"),
-    up=("c-xy-wz", "c-zy-x-w"),
-    out=("c-zy-wx",),
-    qkv=("c-y-z-x-w", "c-xz-yw", "c-z-x-y-w"),
-    c2=("c-z-xy-w", "c-yx-z-w", "c-x-zy-w"),
-    c1=("c-y-xz-w",),
-    vec=("c-w-x-y-z",),
+    down=("c-yx-zw", "c-xz-wy"),
+    up=("c-z-x-y-w", "c-xz-w-y"),
+    out=("c-zx-y-w",),
+    qkv=("c-z-x-y-w", "c-xy-w-z", "c-z-x-y-w"),
+    c2=("c-z-xy-w", "c-yx-w-z", "c-xy-w-z"),
+    c1=("cy-xz-w",),
+    vec=("z-w-c-x-y",),
 )
 SCHEDULE = dict(
     ff2=("down0", "up0"),
     ffo=("down0", "down1", "up0", "up1"),
     out=("down1", "up1", "out0"),
     pull1=("out0",),
-    pull2=("down0",),
-    pull4=("up0",),
-    pull6=("down1", "up1", "out0"),
-    pull7=("down0", "up0"),
-    pull8=("up1", "out0"),
-    pull10=("down1",),
-    pull11=("up0", "up1", "out0"),
-    pull12=("down0", "down1"),
-    pull13=("up0", "up1", "out0"),
-    pull14=("down0", "down1"),
-    pull15=("up0", "up1", "out0"),
+    pull2=("down0", "up0"),
+    pull6=("out0",),
+    pull7=("down0", "down1", "up0", "up1"),
+    pull8=("out0",),
+    pull10=("up0",),
+    pull11=("out0",),
+    pull12=("down0", "down1", "up0", "up1"),
+    pull13=("out0",),
+    pull14=("down0", "down1", "up0", "up1"),
+    pull15=("out0",),
     home=("down0",),
-    qkvw1=("down1", "up1", "qkv1"),
+    qkvw1=("down1", "up0", "up1", "out0", "qkv1"),
     qkvw2=("qkv2",),
-    qkvw0=("down0", "qkv0"),
-    norm=("up1", "qkv1"),
-    c2=("down1", "qkv0", "qkv2"),
+    c2=("down1", "qkv1", "qkv2"),
     c2w0=("c20",),
     c2w1=("c21",),
-    c2w2=("c22",),
-    first=("down0", "down1", "qkv1", "c20", "c21", "c22"),
-    c1=("qkv0", "qkv2"),
-    c1w=("down0", "c10", "vec"),
-    mel=("qkv0", "qkv1", "qkv2", "c20", "c21", "c10", "vec"),
+    c2w2=("up1", "c22"),
+    qkvw0=("qkv0",),
+    first=("up0", "c20", "c21"),
+    c1=("up1", "qkv0", "qkv1", "qkv2", "c22"),
+    c1w=("up0", "c10", "vec"),
+    mel=("qkv1", "qkv2", "c20", "c21"),
     end=(
-        "c22", "qkv1", "qkv0", "c21", "vec", "qkv2", "c20", "c22", "qkv0", "qkv1", "c10", "c21",
-        "vec", "qkv2", "c20", "qkv1", "c22", "qkv0", "vec", "c10", "c21", "qkv2", "c20", "c22",
-        "qkv0", "c10", "vec", "c21", "qkv2", "c20", "c22", "c10", "qkv0", "c21", "qkv2", "qkv0",
-        "c10", "c20", "c22", "c21", "qkv2", "c10", "c20", "c22",
+        "vec", "qkv0", "c22", "qkv1", "c10", "c21", "qkv2", "c20", "vec", "qkv0", "qkv1", "c10",
+        "c22", "c21", "vec", "qkv2", "c20", "qkv0", "vec", "qkv1", "c10", "c22", "c21", "qkv2",
+        "c20", "qkv0", "vec", "c10", "c22", "c21", "qkv0", "qkv1", "qkv2", "c20", "c22", "qkv1",
+        "qkv0", "c10", "qkv2", "c21", "c20", "qkv0", "c22", "qkv2", "c21", "c20", "qkv0", "c22",
     ),
 )
 
@@ -863,17 +875,19 @@
     wait_all(own)
     r.small[...] = jnp.zeros_like(r.small)
     stage_mel_rows(r, sub, mel_rim.wait)
-    start_all(ff_y)
     stage_first(r, jnp.logical_and(c == 0, m == 0))
-    stage_odd(r)
     qkv_y.wait()
     qkv_x.start()
+    start_all(ff_y)
+    stage_odd(r)
     w2_own.wait()
     stage_second(r, quarter(net))
+    vec_copy.wait()
+    r.vecs[8:16, :] = r.vec_mine[...] + r.vec_got[...]
+    qkv_x.wait()
+    qkv_c.start()
     wait_all(ff_y)
     start_all(ff_z)
-    vec_copy.wait()
-    r.vecs[8:16, :] = r.vec_mine[...] + r.vec_got[...]
 
     def block(slot, part, h):
         return r.kv.at[rows16((3 * slot + part) * half + h * (half // 2), half // 2)]
@@ -889,35 +903,17 @@
         return far, near
 
     far_own, near_own = project(m)
-    qkv_x.wait()
-    qkv_c.start()
     stage_mask(r, sub)
     add_small(r, DNB, col(r.bg[...].astype(F32)))
     r.normedt[...] = r.normed[...].astype(F32).T.astype(BF)
+    qkv_c.wait()
+    far_other, near_other = project(1 - m)
     wait_all(near_own)
     heads = half // HEAD
-    far_other = [
-        net.copy(block(own, part, 1 - m), block(to, part, 1 - m), *dims)
-        for part in (1, 2)
-        for own, to, dims in ((3 + c, 0, ("y",)), (4 - c, 1, ("c", "y")))
-    ]
-    near_other = [net.copy(block(4 - c, part, 1 - m), block(2, part, 1 - m), "c") for part in range(3)]
-
-    def project_other():
-        qkv_c.wait()
-        stage_qkv(r, 1, 1 - m)
-        start_all(far_other[0:2])
-        stage_qkv(r, 2, 1 - m)
-        start_all(far_other[2:4])
-        stage_qkv(r, 0, 1 - m)
-        start_all(near_other)
-
     hooks = {
-        heads - 1: [project_other],
         heads: [lambda: wait_all(near_other), lambda: wait_all(ff_z), lambda: start_all(ff_x)],
         2 * heads: [lambda: wait_all(far_own)],
-        5 * heads // 2: [lambda: wait_all(ff_x), lambda: start_all(ff_c)],
-        3 * heads: [lambda: wait_all(far_other)],
+        3 * heads: [lambda: wait_all(far_other), lambda: wait_all(ff_x), lambda: start_all(ff_c)],
     }
     attend(r, c, m, hooks)
     attend_end(r, 1)
@@ -933,7 +929,21 @@
         ]
         return bucket_sum(net, *views, halves, orders(n, bits)[part])
 
-    tracks = {}
+    def leave(n, part):
+        done = getattr(r, "done_" + n)
+        size = half if n == "qkv" else D
+        rows = done if n in ("out", "c1") else done.at[part * size : (part + 1) * size]
+        if n == "qkv":
+            pairs = [(rows.at[:, j * half : (j + 1) * half], r.qkv_o.at[part, j * half : (j + 1) * half]) for j in range(2)]
+        elif n == "up":
+            pairs = [(rows, r.up_o.at[:, part * D : (part + 1) * D])]
+        elif n in ("down", "c2"):
+            pairs = [(rows, getattr(r, n + "_o").at[part * D : (part + 1) * D])]
+        else:
+            pairs = [(done, getattr(r, n + "_o"))]
+        return [net.here_later(src, dst) for src, dst in pairs]
+
+    tracks, leaving = {}, {}
     for n, rows, halves, parts in (
         ("down", D, 2, side),
         ("up", D, 2, side),
@@ -943,7 +953,10 @@
         ("c1", r.g_c1.shape[0], 1, 1),
     ):
         for part in range(parts):
-            tracks["%s%d" % (n, part)] = summed(n, part, rows, halves)
+            name = "%s%d" % (n, part)
+            tracks[name] = summed(n, part, rows, halves)
+            leaving[name] = leave(n, part)
+            tracks[name].then(functools.partial(start_all, leaving[name]))
     tracks["vec"] = small_sum(net, r.small, r.got_small, orders("vec", bits)[0])
 
     def acts_at(name):
@@ -962,6 +975,11 @@
     ready("down%d" % (side - 1), "up%d" % (side - 1))
     point("ffo")
     stage_mid_pull(r)
+    enc = [
+        net.copy(r.enc, r.enc_got, "y"),
+        pltpu.make_async_copy(r.enc, r.enc_o.at[rows_of_mine], r.own.at[39]),
+    ]
+    start_all(enc)
     stage_do(r, c, False)
     do_c = net.send(r.dot_out, r.dot.at[half:D], "c")
     point("mid")
@@ -972,11 +990,6 @@
     stage_diag(r, 0)
     do_c.wait()
     stage_diag(r, 1)
-    enc = [
-        net.copy(r.enc, r.enc_got, "y"),
-        pltpu.make_async_copy(r.enc, r.enc_o.at[rows_of_mine], r.own.at[39]),
-    ]
-
     both = half * 2
     home_y = net.copy(r.dkv.at[0:both], r.from_y, "y")
     home_d = net.copy(r.dkv.at[both : 2 * both], r.from_d, "c", "y")
@@ -988,7 +1001,6 @@
 
     at_step(4, home_y.start)
     at_step(8, home_d.start)
-    at_step(11, lambda: start_all(enc))
     at_step(12, home_c.start)
     for step in range(16):
         at_step(step, *acts_at("pull%d" % step))
@@ -1011,14 +1023,16 @@
         return carry
 
     lax.fori_loop(0, half // 32, total, 0)
-    dq_c.wait()
-    r.dsum[rows16((1 - c) * half, half), :] = r.from_c[0:half, :]
-
-    for part in (1, 2, 0):
+
+    def queries_came():
+        dq_c.wait()
+        r.dsum[rows16((1 - c) * half, half), :] = r.from_c[0:half, :]
+
+    for part in (1, 2):
         stage_qkv_weights(r, part)
         ready("qkv%d" % part)
         point("qkvw%d" % part)
-    stage_qkv_pull(r)
+    stage_qkv_pull(r, queries_came)
     point("norm")
     stage_norm_pull(r)
     rim = [net.send(r.sg.at[0:16], r.slots.at[0, i], dim) for i, dim in enumerate(("c", "y"))]
@@ -1027,8 +1041,15 @@
         stage_conv2_weights(r, part)
         ready("c2%d" % part)
         point("c2w%d" % part)
-    wait_all(rim)
-    stage_conv2_pull(r, pick_next(net, r.slots.at[0]))
+    stage_qkv_weights(r, 0)
+    ready("qkv0")
+    point("qkvw0")
+
+    def next_row():
+        wait_all(rim)
+        return pick_next(net, r.slots.at[0])
+
+    stage_conv2_pull(r, next_row)
     point("first")
     stage_first_pull(r)
     rim = [net.send(r.fe.at[0:16], r.slots.at[1, i], dim) for i, dim in enumerate(("c", "y"))]
@@ -1049,25 +1070,12 @@
     ]
     point("end")
     drain(*tracks.values())
-
-    ends.append(net.here(r.done_down, r.down_o))
-    for j in range(side):
-        ends.append(net.here(r.done_up.at[j * D : (j + 1) * D], r.up_o.at[:, j * D : (j + 1) * D]))
-    ends.append(net.here(r.done_out, r.out_o))
-    for part in range(3):
-        for j in range(2):
-            ends.append(
-                net.here(
-                    r.done_qkv.at[part * half : (part + 1) * half, j * half : (j + 1) * half],
-                    r.qkv_o.at[part, j * half : (j + 1) * half],
-                )
-            )
-    ends.append(net.here(r.done_c2, r.c2_o))
-    ends.append(net.here(r.done_c1, r.c1_o))
-    ends.append(net.here(r.small, r.small_o))
     mel_y.wait()
     ends.append(net.here(r.melg_got, r.mel_o.at[rows_of_yours]))
+    ends.append(net.here(r.small, r.small_o))
     wait_all(ends)
+    for copies in leaving.values():
+        wait_all(copies)
 
 
 def run_layer(bits, near, far, outs, T, D, F2, lanes):
@@ -1190,11 +1198,25 @@
     )
     outs.update({n: ((D,), F32) for n in ROW_BIASES})
 
+    big = ("mel", "c1", "c2", "qkv", "out", "up", "down")
+    names = ins + list(outs) + ["in_" + n for n in ins] + ["out_" + n for n in big] + ["came", "went"]
+
     def kernel(*refs):
         r = Box()
-        for n, ref in zip(ins + list(outs), refs):
+        for n, ref in zip(names, refs):
             setattr(r, n, ref)
         m = lax.axis_index("mp")
+        order = ["small_o", "enc_o", "down_o", "up_o", "qkv_o", "c2_o", "mel_o", "out_o", "c1_o"]
+        loads = {}
+        for k, n in enumerate(order):
+            loads[n] = pltpu.make_async_copy(getattr(r, n), getattr(r, "in_" + n), r.came.at[k])
+            loads[n].start()
+        went = []
+
+        def leave(n):
+            copy = pltpu.make_async_copy(getattr(r, "out_" + n), getattr(r, n), r.went.at[len(went)])
+            copy.start()
+            went.append(copy)
 
         def cast(src, dst):
             def one(rows):
@@ -1202,35 +1224,57 @@
 
             rows_loop(src.shape[0], 256, one)
 
-        cast(r.enc_o, r.enc.at[0])
-        cast(r.down_o, r.down)
-        cast(r.up_o, r.up)
-        cast(r.out_o, r.out)
+        loads["small_o"].wait()
+        for k, n in enumerate(ROW_BIASES):
+            getattr(r, n)[...] = r.in_small_o[k : k + 1, :].reshape(D)
+        r.qkvb[...] = r.in_small_o[QB : QB + 2, pl.ds(pl.multiple_of(m * half, 128), half)]
+        for k in range(side):
+            r.upb[k * D : (k + 1) * D] = r.in_small_o[pl.ds(UPB + m * side + k, 1), :].reshape(D)
+        loads["enc_o"].wait()
+        copy = pltpu.make_async_copy(r.in_enc_o, r.enc.at[0], r.went.at[len(big)])
+        copy.start()
+        for n in ("down", "up"):
+            loads[n + "_o"].wait()
+            cast(getattr(r, "in_" + n + "_o"), getattr(r, "out_" + n))
+            leave(n)
+        loads["qkv_o"].wait()
         for o in range(3):
-            cast(r.qkv_o.at[o], r.qkv.at[o])
-            cast(r.c2_o.at[o * D : (o + 1) * D], r.c2.at[o])
-            r.c1[o] = r.c1_o[o * mels : (o + 1) * mels, :].astype(F32)
+            cast(r.in_qkv_o.at[o], r.out_qkv.at[o])
+        leave("qkv")
+        loads["c2_o"].wait()
+        for o in range(3):
+            cast(r.in_c2_o.at[o * D : (o + 1) * D], r.out_c2.at[o])
+        leave("c2")
         row = lax.broadcasted_iota(jnp.int32, (128, 256), 0)
         lane = lax.broadcasted_iota(jnp.int32, (128, 256), 1)
         even = jnp.where(lane == 2 * row, 1.0, 0.0).astype(BF)
         odd = jnp.where(lane == 2 * row + 1, 1.0, 0.0).astype(BF)
+        loads["mel_o"].wait()
         for k in range(T2 // 128):
             rows = slice(k * 128, (k + 1) * 128)
-            value = tn(r.mel_o[rows, 0:128], even) + tn(r.mel_o[rows, 128:256], odd)
-            r.mel[0, :, k * 256 : (k + 1) * 256] = value[0:mels, :]
-        for k, n in enumerate(ROW_BIASES):
-            getattr(r, n)[...] = r.small_o[k : k + 1, :].reshape(D)
-        r.qkvb[...] = r.small_o[QB : QB + 2, pl.ds(pl.multiple_of(m * half, 128), half)]
-        for k in range(side):
-            r.upb[k * D : (k + 1) * D] = r.small_o[pl.ds(UPB + m * side + k, 1), :].reshape(D)
-
-    vmem = pl.BlockSpec(memory_space=pltpu.VMEM)
+            value = tn(r.in_mel_o[rows, 0:128], even) + tn(r.in_mel_o[rows, 128:256], odd)
+            r.out_mel[0, :, k * 256 : (k + 1) * 256] = value[0:mels, :]
+        leave("mel")
+        loads["out_o"].wait()
+        cast(r.in_out_o, r.out_out)
+        leave("out")
+        loads["c1_o"].wait()
+        for o in range(3):
+            r.out_c1[o] = r.in_c1_o[o * mels : (o + 1) * mels, :].astype(F32)
+        leave("c1")
+        copy.wait()
+        wait_all(went)
+
+    vmem, anywhere = pl.BlockSpec(memory_space=pltpu.VMEM), pl.BlockSpec(memory_space=pl.ANY)
     done = pl.pallas_call(
         kernel,
         name="finish",
         out_shape=[jax.ShapeDtypeStruct(*o) for o in outs.values()],
-        in_specs=[vmem] * len(ins),
-        out_specs=[vmem] * len(outs),
+        in_specs=[anywhere] * len(ins),
+        out_specs=[anywhere if n in big + ("enc",) else vmem for n in outs],
+        scratch_shapes=[pltpu.VMEM(got[n].shape, got[n].dtype) for n in ins]
+        + [pltpu.VMEM(*outs[n]) for n in big]
+        + [pltpu.SemaphoreType.DMA((len(ins),)), pltpu.SemaphoreType.DMA((len(big) + 1,))],
         compiler_params=pltpu.CompilerParams(vmem_limit_bytes=VMEM_LIMIT),
     )(*got.values())
     return dict(zip(outs, done))

time: 184 us -> 181 us (0.984)
  Pallas kernels: 183 us -> 180 us
where the time goes in v11:
time: 181 us
  Pallas kernels  180 us (99%)
    pallas_call x1, Pallas kernels, run_layer(): pl.pallas_call(kernel, name='layer', out_shape=[jax.ShapeDtypeStruct(*o)...  173 us
    pallas_call x1, Pallas kernels, run_finish(): pl.pallas_call(kernel, name='finish', out_shape=[jax.ShapeDtypeStruct(*o)...  6.69 us

profile of v11, /device:TPU:0, one launch (start us, length us, event | category | flops | bytes accessed | tf_op | source)
XLA Modules:
  0.0 180.9 jit_solution(14778544714341867813)
XLA Ops:
  0.7 173.4 %layer.1 = (bf16[1024,512]{1,0:T(8,128)(2,1)}, bf16[1024,256]{1,0:T(8,128)(2,1)}, bf16[1024,512]{1,0:T(8,128)(2,1)}, bf16[512,1024]{1,0:T(8,128)(2,1)}, bf16[256...) custom-call(bf16[3,80,512]{2,1,0:T(8,128)(2,1)} %refs_0_.1, ...), custom_call_target="tpu_custom_call" | custom-call | tf_op jit(solution)/shard_map/layer/pallas_call | solution.py:1168
  174.1 6.7 %finish.1 = (bf16[1,1024,512]{2,1,0:T(8,128)(2,1)}, f32[1,80,2048]{2,1,0:T(8,128)}, f32[3,80,512]{2,1,0:T(8,128)}, f32[3,512,512]{2,1,0:T(8,128)}, f32[3,512,256...) custom-call(bf16[1024,512]{1,0:T(8,128)(2,1)} %get-tuple-element.45., ...), custom_call_target="tpu_custom_call" | custom-call | tf_op jit(solution)/shard_map/finish/pallas_call | solution.py:1269

commit v12 on v11

--- a/solution.py
+++ b/solution.py
@@ -13,7 +13,7 @@
 BF = jnp.bfloat16
 F32 = jnp.float32
 MESH = pl.DeviceIdType.MESH
-VMEM_LIMIT = 61 * 1024 * 1024
+VMEM_LIMIT = 62 * 1024 * 1024
 C1B, C2B, N1G, N1B, OUB, N2G, N2B, DNB, QB, VB, UPB = range(11)
 
 
@@ -37,14 +37,18 @@
     return dot(a, b, 0, 0)
 
 
-def rows_loop(total, step, body, unroll=1):
+def flip(value):
+    return value.astype(F32).T.astype(BF)
+
+
+def rows_loop(total, step, body, unroll=2):
     step = min(step, total)
 
     def one(i, carry):
         body(pl.ds(pl.multiple_of(i * step, step), step))
         return carry
 
-    lax.fori_loop(0, total // step, one, 0, unroll=unroll)
+    lax.fori_loop(0, total // step, one, 0, unroll=min(unroll, total // step))
 
 
 def gelu_parts(v):
@@ -304,7 +308,7 @@
             r.ing[rows, :] = grad
             return acc + col(grad.astype(F32))
 
-        r.small[pl.ds(UPB + j, 1), :] = lax.fori_loop(0, T // 32, one, jnp.zeros((1, width), F32))
+        r.small[pl.ds(UPB + j, 1), :] = lax.fori_loop(0, T // 32, one, jnp.zeros((1, width), F32), unroll=2)
         act = r.act[...]
         ing = r.ing[...]
         out = nn(act, down)
@@ -314,8 +318,9 @@
         r.ntg[...] += back
         rows = pl.ds(pl.multiple_of(t * D, D), D)
         r.g_down[rows, :] = tn(act, r.bg[...]).astype(BF)
-        r.g_up[rows, :] = tn(r.ntwo[...], ing).astype(BF)
-
+        r.g_up[rows, :] = nn(r.ntwot[...], ing).astype(BF)
+
+    r.ntwot[...] = flip(r.ntwo[...])
     r.ffo[...] = jnp.zeros_like(r.ffo)
     r.ntg[...] = jnp.zeros_like(r.ntg)
     head_loop(parts, hooks, chunk)
@@ -338,7 +343,7 @@
         return accs[0] + col(grad * hat), accs[1] + col(grad), accs[2] + col(attg.astype(F32))
 
     zero = jnp.zeros((1, D), F32)
-    gain, bias, out_bias = lax.fori_loop(0, T // 32, one, (zero, zero, zero))
+    gain, bias, out_bias = lax.fori_loop(0, T // 32, one, (zero, zero, zero), unroll=2)
     add_small(r, N2G, gain)
     add_small(r, N2B, bias)
     add_small(r, OUB, out_bias)
@@ -451,7 +456,7 @@
         return accs[0] + col(grad * hat), accs[1] + col(grad), accs[2] + col(sg.astype(F32))
 
     zero = jnp.zeros((1, D), F32)
-    gain, bias, c2b = lax.fori_loop(0, T // 32, one, (zero, zero, zero))
+    gain, bias, c2b = lax.fori_loop(0, T // 32, one, (zero, zero, zero), unroll=2)
     add_small(r, N1G, gain)
     add_small(r, N1B, bias)
     add_small(r, C2B, c2b)
@@ -477,13 +482,12 @@
         r.fo[rows, :] = odd
         return acc + col(even.astype(F32)) + col(odd.astype(F32))
 
-    add_small(r, C1B, lax.fori_loop(0, T // 32, one, jnp.zeros((1, D), F32)))
+    add_small(r, C1B, lax.fori_loop(0, T // 32, one, jnp.zeros((1, D), F32), unroll=2))
 
 
 def stage_conv2_weights(r, i):
     D = r.stream.shape[1]
-    tap = (r.hp, r.he, r.ho)[i]
-    r.g_c2[i * D : (i + 1) * D, :] = tn(tap[...], r.sg[...]).astype(BF)
+    r.g_c2[i * D : (i + 1) * D, :] = nn(r.tapt[i][...], r.sg[...]).astype(BF)
 
 
 def stage_conv1_weights(r):
@@ -751,46 +755,48 @@
 
 
 ORDERS = dict(
-    down=("c-yx-zw", "c-xz-wy"),
-    up=("c-z-x-y-w", "c-xz-w-y"),
-    out=("c-zx-y-w",),
-    qkv=("c-z-x-y-w", "c-xy-w-z", "c-z-x-y-w"),
-    c2=("c-z-xy-w", "c-yx-w-z", "c-xy-w-z"),
+    down=("c-xy-z-w", "c-zx-yw"),
+    up=("c-xz-w-y", "c-zx-y-w"),
+    out=("c-yw-xz",),
+    qkv=("c-z-xy-w", "c-z-w-y-x", "x-c-z-y-w"),
+    c2=("c-z-xy-w", "c-xy-z-w", "c-yx-w-z"),
     c1=("cy-xz-w",),
-    vec=("z-w-c-x-y",),
+    vec=("c-w-xy-z",),
+)
+TRACKS = (
+    ("down", 0), ("down", 1), ("up", 0), ("up", 1), ("out", 0), ("qkv", 0), ("qkv", 1), ("qkv", 2),
+    ("c2", 0), ("c2", 1), ("c2", 2), ("c1", 0), ("vec", 0),
 )
 SCHEDULE = dict(
-    ff2=("down0", "up0"),
-    ffo=("down0", "down1", "up0", "up1"),
-    out=("down1", "up1", "out0"),
-    pull1=("out0",),
-    pull2=("down0", "up0"),
-    pull6=("out0",),
-    pull7=("down0", "down1", "up0", "up1"),
-    pull8=("out0",),
-    pull10=("up0",),
-    pull11=("out0",),
-    pull12=("down0", "down1", "up0", "up1"),
-    pull13=("out0",),
-    pull14=("down0", "down1", "up0", "up1"),
-    pull15=("out0",),
-    home=("down0",),
-    qkvw1=("down1", "up0", "up1", "out0", "qkv1"),
-    qkvw2=("qkv2",),
-    c2=("down1", "qkv1", "qkv2"),
-    c2w0=("c20",),
-    c2w1=("c21",),
-    c2w2=("up1", "c22"),
-    qkvw0=("qkv0",),
-    first=("up0", "c20", "c21"),
-    c1=("up1", "qkv0", "qkv1", "qkv2", "c22"),
-    c1w=("up0", "c10", "vec"),
-    mel=("qkv1", "qkv2", "c20", "c21"),
+    ff2=(0, 2),
+    ffo=(0, 1, 2, 3),
+    out=(1, 3, 4),
+    pull1=(4,),
+    pull3=(2,),
+    pull6=(0, 1),
+    pull7=(2, 3, 4),
+    pull8=(1,),
+    pull9=(0, 2, 4),
+    pull10=(1, 3),
+    pull11=(0, 2, 4),
+    pull12=(3,),
+    pull14=(0, 1),
+    pull15=(2, 3, 4),
+    home=(0, 1),
+    qkvw1=(2, 4, 6),
+    qkvw2=(3, 7),
+    c2=(0, 3, 6),
+    c2w0=(8,),
+    c2w1=(9,),
+    c2w2=(10,),
+    qkvw0=(5,),
+    first=(0, 7, 8, 9, 10),
+    c1=(5, 6, 7),
+    c1w=(11, 12),
+    mel=(8, 12),
     end=(
-        "vec", "qkv0", "c22", "qkv1", "c10", "c21", "qkv2", "c20", "vec", "qkv0", "qkv1", "c10",
-        "c22", "c21", "vec", "qkv2", "c20", "qkv0", "vec", "qkv1", "c10", "c22", "c21", "qkv2",
-        "c20", "qkv0", "vec", "c10", "c22", "c21", "qkv0", "qkv1", "qkv2", "c20", "c22", "qkv1",
-        "qkv0", "c10", "qkv2", "c21", "c20", "qkv0", "c22", "qkv2", "c21", "c20", "qkv0", "c22",
+        9, 10, 6, 7, 11, 5, 8, 12, 9, 11, 10, 6, 7, 5, 8, 9, 12, 6, 11, 10, 7, 5, 8, 9, 6, 12,
+        11, 10, 7, 5, 8, 9, 6, 5, 10, 7, 11, 7, 9, 6, 8, 5, 10, 9, 6, 5, 8, 7, 10,
     ),
 )
 
@@ -905,13 +911,19 @@
     far_own, near_own = project(m)
     stage_mask(r, sub)
     add_small(r, DNB, col(r.bg[...].astype(F32)))
-    r.normedt[...] = r.normed[...].astype(F32).T.astype(BF)
+    r.normedt[...] = flip(r.normed[...])
     qkv_c.wait()
     far_other, near_other = project(1 - m)
     wait_all(near_own)
     heads = half // HEAD
+
+    def flip_taps():
+        for tap, to in zip((r.hp, r.he, r.ho), r.tapt):
+            to[...] = flip(tap[...])
+
     hooks = {
         heads: [lambda: wait_all(near_other), lambda: wait_all(ff_z), lambda: start_all(ff_x)],
+        2 * heads - 1: [flip_taps],
         2 * heads: [lambda: wait_all(far_own)],
         3 * heads: [lambda: wait_all(far_other), lambda: wait_all(ff_x), lambda: start_all(ff_c)],
     }
@@ -957,10 +969,11 @@
             tracks[name] = summed(n, part, rows, halves)
             leaving[name] = leave(n, part)
             tracks[name].then(functools.partial(start_all, leaving[name]))
-    tracks["vec"] = small_sum(net, r.small, r.got_small, orders("vec", bits)[0])
+    tracks["vec0"] = small_sum(net, r.small, r.got_small, orders("vec", bits)[0])
 
     def acts_at(name):
-        return [act for n in SCHEDULE.get(name, ()) if n in tracks for act in tracks[n].take()]
+        names = ["%s%d" % TRACKS[k] for k in SCHEDULE.get(name, ())]
+        return [act for n in names if n in tracks for act in tracks[n].take()]
 
     def point(name):
         for act in acts_at(name):
@@ -1056,7 +1069,7 @@
     rim += [net.send(r.fo.at[T - 16 : T], r.slots.at[2, i], dim) for i, dim in enumerate(("c", "y"))]
     point("c1")
     stage_conv1_weights(r)
-    ready("c10", "vec")
+    ready("c10", "vec0")
     point("c1w")
     wait_all(rim)
     stage_mel(r, pick_next(net, r.slots.at[1]), pick_prev(net, r.slots.at[2]))
@@ -1110,6 +1123,7 @@
         mixt=(dt, F32),
         mixb=(dt, BF),
         normedt=(dt, BF),
+        ntwot=(dt, BF),
         mix_got=((half, T), BF),
         dot=(dt, BF),
         dot_out=((half, T), BF),
@@ -1152,6 +1166,7 @@
             scratch["got_%s%d" % (n, part)] = ((need, D), BF)
         scratch["done_" + n] = ((rows * parts, D), BF)
     if not alias:
+        scratch.update({"tapt%d" % i: (dt, BF) for i in range(3)})
         scratch.update(g_qkv=((6 * half, D), BF), g_c2=((6 * half, D), BF))
     names = list(near) + list(far) + list(outs) + list(scratch) + ["send", "recv", "own"]
 
@@ -1160,6 +1175,7 @@
         for n, ref in zip(names, refs):
             setattr(r, n, ref)
         r.odd, r.smg, r.sg, r.fe, r.fo, r.enc = r.shift, r.mid, r.ntwo, r.act, r.ing, r.bg
+        r.tapt = (r.hp, r.he, r.ho) if alias else (r.tapt0, r.tapt1, r.tapt2)
         if alias:
             r.g_qkv, r.g_c2 = r.kv.at[0 : 6 * half], r.kv.at[6 * half : 12 * half]
         layer(r, bits)

time: 181 us -> 183 us (1.011)
  Pallas kernels: 180 us -> 182 us
    pallas_call x1, Pallas kernels: 173 us -> 176 us  [run_layer(): pl.pallas_call(kernel, name='layer', out_shape=[jax.ShapeDtypeStruct(*o)...]
where the time goes in v12:
time: 183 us
  Pallas kernels  182 us (99%)
    pallas_call x1, Pallas kernels, run_layer(): pl.pallas_call(kernel, name='layer', out_shape=[jax.ShapeDtypeStruct(*o)...  176 us
    pallas_call x1, Pallas kernels, run_finish(): pl.pallas_call(kernel, name='finish', out_shape=[jax.ShapeDtypeStruct(*o)...  6.68 us

profile of v12, /device:TPU:0, one launch (start us, length us, event | category | flops | bytes accessed | tf_op | source)
XLA Modules:
  0.0 183.2 jit_solution(6474149348526306378)
XLA Ops:
  0.7 175.6 %layer.1 = (bf16[1024,512]{1,0:T(8,128)(2,1)}, bf16[1024,256]{1,0:T(8,128)(2,1)}, bf16[1024,512]{1,0:T(8,128)(2,1)}, bf16[512,1024]{1,0:T(8,128)(2,1)}, bf16[256...) custom-call(bf16[3,80,512]{2,1,0:T(8,128)(2,1)} %refs_0_.1, ...), custom_call_target="tpu_custom_call" | custom-call | tf_op jit(solution)/shard_map/layer/pallas_call | solution.py:1184
  176.3 6.7 %finish.1 = (bf16[1,1024,512]{2,1,0:T(8,128)(2,1)}, f32[1,80,2048]{2,1,0:T(8,128)}, f32[3,80,512]{2,1,0:T(8,128)}, f32[3,512,512]{2,1,0:T(8,128)}, f32[3,512,256...) custom-call(bf16[1024,512]{1,0:T(8,128)(2,1)} %get-tuple-element.45., ...), custom_call_target="tpu_custom_call" | custom-call | tf_op jit(solution)/shard_map/finish/pallas_call | solution.py:1285

commit v13 on v12

--- a/solution.py
+++ b/solution.py
@@ -41,7 +41,7 @@
     return value.astype(F32).T.astype(BF)
 
 
-def rows_loop(total, step, body, unroll=2):
+def rows_loop(total, step, body, unroll=1):
     step = min(step, total)
 
     def one(i, carry):
@@ -308,7 +308,7 @@
             r.ing[rows, :] = grad
             return acc + col(grad.astype(F32))
 
-        r.small[pl.ds(UPB + j, 1), :] = lax.fori_loop(0, T // 32, one, jnp.zeros((1, width), F32), unroll=2)
+        r.small[pl.ds(UPB + j, 1), :] = lax.fori_loop(0, T // 32, one, jnp.zeros((1, width), F32))
         act = r.act[...]
         ing = r.ing[...]
         out = nn(act, down)
@@ -343,7 +343,7 @@
         return accs[0] + col(grad * hat), accs[1] + col(grad), accs[2] + col(attg.astype(F32))
 
     zero = jnp.zeros((1, D), F32)
-    gain, bias, out_bias = lax.fori_loop(0, T // 32, one, (zero, zero, zero), unroll=2)
+    gain, bias, out_bias = lax.fori_loop(0, T // 32, one, (zero, zero, zero))
     add_small(r, N2G, gain)
     add_small(r, N2B, bias)
     add_small(r, OUB, out_bias)
@@ -400,9 +400,13 @@
                 p = jnp.exp(tn(k[:, rows], qs[i]) - top)
                 r.pb[rows, cols] = p.astype(BF)
                 r.ds[rows, cols] = (p * (tn(v[:, rows], dos[i]) - diag)).astype(BF)
-        both = [jnp.concatenate(one, axis=1) for one in (qs, dos)]
-        r.dkv[at_head(2 * g * S, h), :] = nt(both[0], r.ds[...]).astype(BF)
-        r.dkv[at_head((2 * g + 1) * S, h), :] = nt(both[1], r.pb[...]).astype(BF)
+        pair = [pl.ds(pl.multiple_of(i * S + h // 2 * 128, 128), 128) for i in range(2)]
+        for part, left, right in ((0, r.ds, r.qrow), (1, r.pb, r.dorow)):
+            r.turn[128 * part : 128 * (part + 1), :] = sum(
+                nn(left[:, i * T : (i + 1) * T], right[:, pair[i]]) for i in range(2)
+            ).T
+            value = r.turn[pl.ds(pl.multiple_of(128 * part + h % 2 * HEAD, HEAD), HEAD), :]
+            r.dkv[at_head((2 * g + part) * S, h), :] = value.astype(BF)
         dq = nn(k, r.ds[...])
         for i in range(2):
             r.dqt[at_head(i * S, h), :] += dq[:, i * T : (i + 1) * T]
@@ -456,7 +460,7 @@
         return accs[0] + col(grad * hat), accs[1] + col(grad), accs[2] + col(sg.astype(F32))
 
     zero = jnp.zeros((1, D), F32)
-    gain, bias, c2b = lax.fori_loop(0, T // 32, one, (zero, zero, zero), unroll=2)
+    gain, bias, c2b = lax.fori_loop(0, T // 32, one, (zero, zero, zero))
     add_small(r, N1G, gain)
     add_small(r, N1B, bias)
     add_small(r, C2B, c2b)
@@ -482,7 +486,7 @@
         r.fo[rows, :] = odd
         return acc + col(even.astype(F32)) + col(odd.astype(F32))
 
-    add_small(r, C1B, lax.fori_loop(0, T // 32, one, jnp.zeros((1, D), F32), unroll=2))
+    add_small(r, C1B, lax.fori_loop(0, T // 32, one, jnp.zeros((1, D), F32)))
 
 
 def stage_conv2_weights(r, i):
@@ -755,13 +759,13 @@
 
 
 ORDERS = dict(
-    down=("c-xy-z-w", "c-zx-yw"),
-    up=("c-xz-w-y", "c-zx-y-w"),
-    out=("c-yw-xz",),
-    qkv=("c-z-xy-w", "c-z-w-y-x", "x-c-z-y-w"),
-    c2=("c-z-xy-w", "c-xy-z-w", "c-yx-w-z"),
+    down=("c-y-z-xw", "c-x-z-y-w"),
+    up=("c-w-x-zy", "c-xz-w-y"),
+    out=("c-x-w-zy",),
+    qkv=("c-w-yx-z", "c-y-z-w-x", "x-c-z-y-w"),
+    c2=("c-z-yx-w", "c-xy-z-w", "c-xy-w-z"),
     c1=("cy-xz-w",),
-    vec=("c-w-xy-z",),
+    vec=("c-y-w-z-x",),
 )
 TRACKS = (
     ("down", 0), ("down", 1), ("up", 0), ("up", 1), ("out", 0), ("qkv", 0), ("qkv", 1), ("qkv", 2),
@@ -772,31 +776,30 @@
     ffo=(0, 1, 2, 3),
     out=(1, 3, 4),
     pull1=(4,),
-    pull3=(2,),
-    pull6=(0, 1),
-    pull7=(2, 3, 4),
-    pull8=(1,),
-    pull9=(0, 2, 4),
-    pull10=(1, 3),
-    pull11=(0, 2, 4),
-    pull12=(3,),
-    pull14=(0, 1),
-    pull15=(2, 3, 4),
-    home=(0, 1),
-    qkvw1=(2, 4, 6),
-    qkvw2=(3, 7),
-    c2=(0, 3, 6),
-    c2w0=(8,),
+    pull2=(0,),
+    pull5=(2, 3),
+    pull6=(0, 1, 4),
+    pull7=(2, 3),
+    pull10=(0, 3, 4),
+    pull11=(1, 2),
+    pull13=(0, 3, 4),
+    pull14=(1, 2),
+    pull15=(4,),
+    qkvw1=(1, 2, 3, 6),
+    qkvw2=(7,),
+    norm=(0, 4),
+    c2=(3, 6),
+    c2w0=(1, 8),
     c2w1=(9,),
-    c2w2=(10,),
+    c2w2=(0, 10),
     qkvw0=(5,),
-    first=(0, 7, 8, 9, 10),
-    c1=(5, 6, 7),
+    first=(8, 9),
+    c1=(1, 2, 4, 5, 6, 7, 10),
     c1w=(11, 12),
-    mel=(8, 12),
+    mel=(2, 4, 7, 8, 9, 12),
     end=(
-        9, 10, 6, 7, 11, 5, 8, 12, 9, 11, 10, 6, 7, 5, 8, 9, 12, 6, 11, 10, 7, 5, 8, 9, 6, 12,
-        11, 10, 7, 5, 8, 9, 6, 5, 10, 7, 11, 7, 9, 6, 8, 5, 10, 9, 6, 5, 8, 7, 10,
+        10, 1, 5, 6, 11, 7, 9, 8, 12, 1, 10, 11, 5, 7, 6, 9, 8, 10, 12, 11, 5, 6, 7, 9, 8, 10,
+        11, 6, 5, 12, 7, 8, 9, 10, 5, 6, 12, 7, 11, 7, 8, 9, 10, 5, 6, 8, 7, 9, 10, 5, 6,
     ),
 )
 
@@ -1001,7 +1004,11 @@
     point("out")
     stage_do(r, c, True)
     stage_diag(r, 0)
+    for i, home in enumerate((3 + c, 2)):
+        r.qrow[:, i * half : (i + 1) * half] = flip(r.kv[rows16(3 * home * half, half), :])
+    r.dorow[:, 0:half] = flip(r.dot[0:half, :])
     do_c.wait()
+    r.dorow[:, half:D] = flip(r.dot[half:D, :])
     stage_diag(r, 1)
     both = half * 2
     home_y = net.copy(r.dkv.at[0:both], r.from_y, "y")
@@ -1167,6 +1174,7 @@
         scratch["done_" + n] = ((rows * parts, D), BF)
     if not alias:
         scratch.update({"tapt%d" % i: (dt, BF) for i in range(3)})
+        scratch["turn"] = ((256, T), F32)
         scratch.update(g_qkv=((6 * half, D), BF), g_c2=((6 * half, D), BF))
     names = list(near) + list(far) + list(outs) + list(scratch) + ["send", "recv", "own"]
 
@@ -1175,6 +1183,9 @@
         for n, ref in zip(names, refs):
             setattr(r, n, ref)
         r.odd, r.smg, r.sg, r.fe, r.fo, r.enc = r.shift, r.mid, r.ntwo, r.act, r.ing, r.bg
+        r.qrow, r.dorow = r.act, r.ing
+        if alias:
+            r.turn = r.tmp.at[0:256]
         r.tapt = (r.hp, r.he, r.ho) if alias else (r.tapt0, r.tapt1, r.tapt2)
         if alias:
             r.g_qkv, r.g_c2 = r.kv.at[0 : 6 * half], r.kv.at[6 * half : 12 * half]

time: 183 us -> 180 us (0.984)
  Pallas kernels: 182 us -> 179 us
    pallas_call x1, Pallas kernels: 176 us -> 173 us  [run_layer(): pl.pallas_call(kernel, name='layer', out_shape=[jax.ShapeDtypeStruct(*o)...]
where the time goes in v13:
time: 180 us
  Pallas kernels  179 us (99%)
    pallas_call x1, Pallas kernels, run_layer(): pl.pallas_call(kernel, name='layer', out_shape=[jax.ShapeDtypeStruct(*o)...  173 us
    pallas_call x1, Pallas kernels, run_finish(): pl.pallas_call(kernel, name='finish', out_shape=[jax.ShapeDtypeStruct(*o)...  6.69 us

profile of v13, /device:TPU:0, one launch (start us, length us, event | category | flops | bytes accessed | tf_op | source)
XLA Modules:
  0.0 180.1 jit_solution(3736149852364718021)
XLA Ops:
  0.7 172.6 %layer.1 = (bf16[1024,512]{1,0:T(8,128)(2,1)}, bf16[1024,256]{1,0:T(8,128)(2,1)}, bf16[1024,512]{1,0:T(8,128)(2,1)}, bf16[512,1024]{1,0:T(8,128)(2,1)}, bf16[256...) custom-call(bf16[3,80,512]{2,1,0:T(8,128)(2,1)} %refs_0_.1, ...), custom_call_target="tpu_custom_call" | custom-call | tf_op jit(solution)/shard_map/layer/pallas_call | solution.py:1195
  173.3 6.7 %finish.1 = (bf16[1,1024,512]{2,1,0:T(8,128)(2,1)}, f32[1,80,2048]{2,1,0:T(8,128)}, f32[3,80,512]{2,1,0:T(8,128)}, f32[3,512,512]{2,1,0:T(8,128)}, f32[3,512,256...) custom-call(bf16[1024,512]{1,0:T(8,128)(2,1)} %get-tuple-element.45., ...), custom_call_target="tpu_custom_call" | custom-call | tf_op jit(solution)/shard_map/finish/pallas_call | solution.py:1296

commit v14 on v13

--- a/solution.py
+++ b/solution.py
@@ -239,17 +239,19 @@
         slot = own * (3 + c) + (1 - own) * ((g + 1) % 3)
         k = r.kv[at_head((3 * slot + 1) * S, h), :]
         v = r.kv[at_head((3 * slot + 2) * S, h), :]
+        turned = flip(k)
         for i, home in enumerate((3 + c, 2)):
-            q = r.kv[at_head(3 * home * S, h), :]
-            s = tn(k, q)
-            before = r.top[i * heads + h]
-            top = jnp.maximum(before, jnp.max(s, axis=0, keepdims=True))
-            p = jnp.exp(s - top)
-            keep = jnp.exp(before - top)
-            rows = at_head(i * S, h)
-            r.top[i * heads + h] = top
-            r.total[i * heads + h] = keep * r.total[i * heads + h] + jnp.sum(p, axis=0, keepdims=True)
-            r.mixt[rows, :] = keep * r.mixt[rows, :] + nn(v, p.astype(BF))
+            rows, at = at_head(i * S, h), i * heads + h
+            for start in range(0, T, 256):
+                cols = slice(start, start + 256)
+                s = nn(turned, r.kv[at_head(3 * home * S, h), cols])
+                before = r.top[at, :, cols]
+                top = jnp.maximum(before, jnp.max(s, axis=0, keepdims=True))
+                p = jnp.exp(s - top)
+                keep = jnp.exp(before - top)
+                r.top[at, :, cols] = top
+                r.total[at, :, cols] = keep * r.total[at, :, cols] + jnp.sum(p, axis=0, keepdims=True)
+                r.mixt[rows, cols] = keep * r.mixt[rows, cols] + nn(v, p.astype(BF))
 
     head_loop(4 * heads, hooks, body)
 
@@ -391,15 +393,15 @@
         slot = g + (g // 3) * c
         k = r.kv[at_head((3 * slot + 1) * S, h), :]
         v = r.kv[at_head((3 * slot + 2) * S, h), :]
-        qs = [r.kv[at_head(3 * home * S, h), :] for home in (3 + c, 2)]
-        dos = [r.dot[at_head(i * S, h), :] for i in range(2)]
-        for i in range(2):
-            top, diag = r.top[i * heads + h], r.diag[i * heads + h]
-            for at in range(0, T, 128):
-                rows, cols = slice(at, at + 128), slice(i * T, (i + 1) * T)
-                p = jnp.exp(tn(k[:, rows], qs[i]) - top)
-                r.pb[rows, cols] = p.astype(BF)
-                r.ds[rows, cols] = (p * (tn(v[:, rows], dos[i]) - diag)).astype(BF)
+        kt, vt = flip(k), flip(v)
+        for i, home in enumerate((3 + c, 2)):
+            at = i * heads + h
+            for start in range(0, T, 256):
+                cols, to = slice(start, start + 256), slice(i * T + start, i * T + start + 256)
+                p = jnp.exp(nn(kt, r.kv[at_head(3 * home * S, h), cols]) - r.top[at, :, cols])
+                r.pb[:, to] = p.astype(BF)
+                dp = nn(vt, r.dot[at_head(i * S, h), cols])
+                r.ds[:, to] = (p * (dp - r.diag[at, :, cols])).astype(BF)
         pair = [pl.ds(pl.multiple_of(i * S + h // 2 * 128, 128), 128) for i in range(2)]
         for part, left, right in ((0, r.ds, r.qrow), (1, r.pb, r.dorow)):
             r.turn[128 * part : 128 * (part + 1), :] = sum(

time: 180 us -> 186 us (1.033)
  Pallas kernels: 179 us -> 185 us
    pallas_call x1, Pallas kernels: 173 us -> 178 us  [run_layer(): pl.pallas_call(kernel, name='layer', out_shape=[jax.ShapeDtypeStruct(*o)...]
where the time goes in v14:
time: 186 us
  Pallas kernels  185 us (99%)
    pallas_call x1, Pallas kernels, run_layer(): pl.pallas_call(kernel, name='layer', out_shape=[jax.ShapeDtypeStruct(*o)...  178 us
    pallas_call x1, Pallas kernels, run_finish(): pl.pallas_call(kernel, name='finish', out_shape=[jax.ShapeDtypeStruct(*o)...  6.69 us

profile of v14, /device:TPU:0, one launch (start us, length us, event | category | flops | bytes accessed | tf_op | source)
XLA Modules:
  0.0 185.6 jit_solution(363718603725108698)
XLA Ops:
  0.7 178.1 %layer.1 = (bf16[1024,512]{1,0:T(8,128)(2,1)}, bf16[1024,256]{1,0:T(8,128)(2,1)}, bf16[1024,512]{1,0:T(8,128)(2,1)}, bf16[512,1024]{1,0:T(8,128)(2,1)}, bf16[256...) custom-call(bf16[3,80,512]{2,1,0:T(8,128)(2,1)} %refs_0_.1, ...), custom_call_target="tpu_custom_call" | custom-call | tf_op jit(solution)/shard_map/layer/pallas_call | solution.py:1197
  178.8 6.7 %finish.1 = (bf16[1,1024,512]{2,1,0:T(8,128)(2,1)}, f32[1,80,2048]{2,1,0:T(8,128)}, f32[3,80,512]{2,1,0:T(8,128)}, f32[3,512,512]{2,1,0:T(8,128)}, f32[3,512,256...) custom-call(bf16[1024,512]{1,0:T(8,128)(2,1)} %get-tuple-element.45., ...), custom_call_target="tpu_custom_call" | custom-call | tf_op jit(solution)/shard_map/finish/pallas_call | solution.py:1298

commit v15 on v13

--- a/solution.py
+++ b/solution.py
@@ -759,11 +759,11 @@
 
 
 ORDERS = dict(
-    down=("c-y-z-xw", "c-x-z-y-w"),
-    up=("c-w-x-zy", "c-xz-w-y"),
-    out=("c-x-w-zy",),
-    qkv=("c-w-yx-z", "c-y-z-w-x", "x-c-z-y-w"),
-    c2=("c-z-yx-w", "c-xy-z-w", "c-xy-w-z"),
+    down=("c-z-wy-x", "c-y-zx-w"),
+    up=("c-xy-wz", "c-zx-wy"),
+    out=("c-y-wx-z",),
+    qkv=("c-w-yx-z", "c-zy-x-w", "x-c-z-y-w"),
+    c2=("c-z-xy-w", "c-xy-z-w", "c-xy-w-z"),
     c1=("cy-xz-w",),
     vec=("c-y-w-z-x",),
 )
@@ -775,31 +775,33 @@
     ff2=(0, 2),
     ffo=(0, 1, 2, 3),
     out=(1, 3, 4),
-    pull1=(4,),
-    pull2=(0,),
-    pull5=(2, 3),
-    pull6=(0, 1, 4),
-    pull7=(2, 3),
+    pull1=(0, 4),
+    pull2=(2,),
+    pull3=(3,),
+    pull6=(0, 2),
+    pull7=(3, 4),
+    pull8=(0, 1),
+    pull9=(2,),
     pull10=(0, 3, 4),
-    pull11=(1, 2),
-    pull13=(0, 3, 4),
-    pull14=(1, 2),
-    pull15=(4,),
-    qkvw1=(1, 2, 3, 6),
-    qkvw2=(7,),
-    norm=(0, 4),
-    c2=(3, 6),
-    c2w0=(1, 8),
+    pull11=(1,),
+    pull12=(2, 4),
+    pull14=(0, 1, 2, 3, 4),
+    home=(3,),
+    qkvw1=(6,),
+    qkvw2=(1, 4, 7),
+    norm=(0,),
+    c2=(4, 6),
+    c2w0=(8,),
     c2w1=(9,),
     c2w2=(0, 10),
     qkvw0=(5,),
-    first=(8, 9),
-    c1=(1, 2, 4, 5, 6, 7, 10),
-    c1w=(11, 12),
-    mel=(2, 4, 7, 8, 9, 12),
+    first=(1, 8, 9),
+    c1=(5, 6, 7, 10),
+    c1w=(1, 11, 12),
+    mel=(6, 7, 8, 9, 12),
     end=(
-        10, 1, 5, 6, 11, 7, 9, 8, 12, 1, 10, 11, 5, 7, 6, 9, 8, 10, 12, 11, 5, 6, 7, 9, 8, 10,
-        11, 6, 5, 12, 7, 8, 9, 10, 5, 6, 12, 7, 11, 7, 8, 9, 10, 5, 6, 8, 7, 9, 10, 5, 6,
+        5, 10, 11, 6, 7, 9, 8, 12, 5, 10, 11, 6, 9, 7, 8, 12, 6, 5, 10, 11, 9, 7, 8, 5, 12, 10,
+        11, 7, 8, 9, 6, 5, 12, 10, 6, 7, 11, 7, 8, 5, 9, 10, 8, 5, 9, 7, 10,
     ),
 )
 
@@ -901,22 +903,24 @@
     def block(slot, part, h):
         return r.kv.at[rows16((3 * slot + part) * half + h * (half // 2), half // 2)]
 
-    def project(h):
+    def project(h, at_once):
         far, near = [], []
         for part in (1, 2, 0):
             stage_qkv(r, part, h)
             if part:
-                far.append(net.send(block(3 + c, part, h), block(0, part, h), "y"))
-                far.append(net.send(block(4 - c, part, h), block(1, part, h), "c", "y"))
+                far.append(net.copy(block(3 + c, part, h), block(0, part, h), "y"))
+                far.append(net.copy(block(4 - c, part, h), block(1, part, h), "c", "y"))
+                if at_once:
+                    start_all(far[-2:])
             near.append(net.send(block(4 - c, part, h), block(2, part, h), "c"))
         return far, near
 
-    far_own, near_own = project(m)
+    far_own, near_own = project(m, True)
     stage_mask(r, sub)
     add_small(r, DNB, col(r.bg[...].astype(F32)))
     r.normedt[...] = flip(r.normed[...])
     qkv_c.wait()
-    far_other, near_other = project(1 - m)
+    far_other, near_other = project(1 - m, False)
     wait_all(near_own)
     heads = half // HEAD
 
@@ -925,7 +929,7 @@
             to[...] = flip(tap[...])
 
     hooks = {
-        heads: [lambda: wait_all(near_other), lambda: wait_all(ff_z), lambda: start_all(ff_x)],
+        heads: [lambda: start_all(far_other), lambda: wait_all(near_other), lambda: wait_all(ff_z), lambda: start_all(ff_x)],
         2 * heads - 1: [flip_taps],
         2 * heads: [lambda: wait_all(far_own)],
         3 * heads: [lambda: wait_all(far_other), lambda: wait_all(ff_x), lambda: start_all(ff_c)],

time: 180 us -> 188 us (1.044)
  Pallas kernels: 179 us -> 187 us
    pallas_call x1, Pallas kernels: 173 us -> 180 us  [run_layer(): pl.pallas_call(kernel, name='layer', out_shape=[jax.ShapeDtypeStruct(*o)...]
where the time goes in v15:
time: 188 us
  Pallas kernels  187 us (99%)
    pallas_call x1, Pallas kernels, run_layer(): pl.pallas_call(kernel, name='layer', out_shape=[jax.ShapeDtypeStruct(*o)...  180 us
    pallas_call x1, Pallas kernels, run_finish(): pl.pallas_call(kernel, name='finish', out_shape=[jax.ShapeDtypeStruct(*o)...  6.69 us

profile of v15, /device:TPU:0, one launch (start us, length us, event | category | flops | bytes accessed | tf_op | source)
XLA Modules:
  0.0 187.9 jit_solution(17209906182400071551)
XLA Ops:
  0.7 180.4 %layer.1 = (bf16[1024,512]{1,0:T(8,128)(2,1)}, bf16[1024,256]{1,0:T(8,128)(2,1)}, bf16[1024,512]{1,0:T(8,128)(2,1)}, bf16[512,1024]{1,0:T(8,128)(2,1)}, bf16[256...) custom-call(bf16[3,80,512]{2,1,0:T(8,128)(2,1)} %refs_0_.1, ...), custom_call_target="tpu_custom_call" | custom-call | tf_op jit(solution)/shard_map/layer/pallas_call | solution.py:1199
  181.1 6.7 %finish.1 = (bf16[1,1024,512]{2,1,0:T(8,128)(2,1)}, f32[1,80,2048]{2,1,0:T(8,128)}, f32[3,80,512]{2,1,0:T(8,128)}, f32[3,512,512]{2,1,0:T(8,128)}, f32[3,512,256...) custom-call(bf16[1024,512]{1,0:T(8,128)(2,1)} %get-tuple-element.45., ...), custom_call_target="tpu_custom_call" | custom-call | tf_op jit(solution)/shard_map/finish/pallas_call | solution.py:1300
